TPU v7x, 32 devices: a whole 2x2x4 slice. The times are simulated.
32 devices in a mesh: shot: 2 (over y), gx: 4 (over z), gy: 4 (over x, core).
Axes of the slice: x: 2, y: 2, z: 4, core: 2. Of those that a mesh axis runs over, the one named last changes fastest.
Arguments:
- source_prev: float32 [64, 32, 320], P(('shot', 'gx'), 'gy'), parts along dimension 0, may hold values from -0.6 to 0.6
- source_now: float32 [64, 32, 320], P(('shot', 'gx'), 'gy'), parts along dimension 0, may hold values from -0.6 to 0.6
- receiver_prev: float32 [64, 32, 320], P(('shot', 'gx'), 'gy'), parts along dimension 0, may hold values from -6 to 6
- receiver_now: float32 [64, 32, 320], P(('shot', 'gx'), 'gy'), parts along dimension 0, may hold values from -6 to 6
- speed_squared: float32 [64, 32, 320], P(('shot', 'gx'), 'gy'), parts along dimension 0, may hold values from 0.05 to 0.18
- wavelet: float32 [20], P('shot'), parts along dimension 0, may hold values from -40 to 40
- source_cell: int32 [2], P('shot'), parts along dimension 0, may hold values from 0 to 327679
- traces: float32 [20, 1024], P('shot', ('gx', 'gy')), parts along dimension 0, may hold values from -18 to 18
- receiver_cells: int32 [2, 1024], P('shot', ('gx', 'gy')), parts along dimension 0, may hold values from 0 to 1023
- plan: int32 [8], P('shot'), parts along dimension 0, may hold values from 0 to 9, as said below
- stored_snapshots: bfloat16 [8, 32, 32, 320], P('shot', 'gx', 'gy'), parts along dimension 0, may hold values from -6 to 6
- image_before: float32 [64, 32, 320], P(('shot', 'gx'), 'gy'), parts along dimension 0, may hold values from -6 to 6
Outputs:
- new_source_prev: float32 [64, 32, 320], P(('shot', 'gx'), 'gy'), parts along dimension 0
- new_source_now: float32 [64, 32, 320], P(('shot', 'gx'), 'gy'), parts along dimension 0
- new_receiver_prev: float32 [64, 32, 320], P(('shot', 'gx'), 'gy'), parts along dimension 0
- new_receiver_now: float32 [64, 32, 320], P(('shot', 'gx'), 'gy'), parts along dimension 0
- snapshots: bfloat16 [8, 32, 32, 320], P('shot', 'gx', 'gy'), parts along dimension 0
- image: float32 [64, 32, 320], P(('shot', 'gx'), 'gy'), parts along dimension 0
There are 2 independent parts, one for each index of `shot`. A program takes and returns all parts, laid end to end along the dimension named above; each array names one. Nothing has to cross between parts.
Inputs may be any that keep to these rules, and one draw needn't show every extreme that they name: `plan`: 4 different steps in increasing order; the first is 0 and the last is 9.
All inputs are finite; a program needn't handle non-finite values.
Results may differ from a plain program's by a relative error of at most 0.001.
Values sent between devices are 32-bit elements; how exact they have to be, the bound alone decides.
No kernel may reach another device: no remote copies, remote signals or barrier semaphores. Data moves between devices by JAX's collectives and lax.ppermute only.
A program may use at most 64 MiB of HBM per device.

v0:
```python
import jax
import jax.numpy as jnp
from jax import lax
from jax.sharding import PartitionSpec as P

STENCIL_COEFFS = (-205.0 / 72.0, 8.0 / 5.0, -1.0 / 5.0, 8.0 / 315.0, -1.0 / 560.0)


def with_halo(block, sides, width):
    for axis, dim in sides:
        count = lax.axis_size(axis)
        forward = [(i, i + 1) for i in range(count - 1)]
        backward = [(target, source) for source, target in forward]
        low = lax.ppermute(
            lax.slice_in_dim(block, block.shape[dim] - width, None, axis=dim), axis, forward
        )
        high = lax.ppermute(lax.slice_in_dim(block, 0, width, axis=dim), axis, backward)
        block = jnp.concatenate([low, block, high], axis=dim)
    return block


def stencil(padded):
    span_x = padded.shape[0] - 8
    span_y = padded.shape[1] - 8
    depth_cells = padded.shape[2]
    deepened = jnp.pad(padded, ((0, 0), (0, 0), (4, 4)))

    def window(shift_x, shift_y, shift_z):
        return deepened[
            4 + shift_x : 4 + shift_x + span_x,
            4 + shift_y : 4 + shift_y + span_y,
            4 + shift_z : 4 + shift_z + depth_cells,
        ]

    summed = 3.0 * STENCIL_COEFFS[0] * window(0, 0, 0)
    for distance in range(1, 5):
        neighbours = window(distance, 0, 0) + window(-distance, 0, 0)
        neighbours = neighbours + window(0, distance, 0) + window(0, -distance, 0)
        neighbours = neighbours + window(0, 0, distance) + window(0, 0, -distance)
        summed = summed + STENCIL_COEFFS[distance] * neighbours
    return summed


def body(
    source_prev,
    source_now,
    receiver_prev,
    receiver_now,
    speed_squared,
    wavelet,
    source_cell,
    traces,
    receiver_cells,
    plan,
    stored_snapshots,
    image_before,
):
    block_x, block_y, depth_cells = source_now.shape
    grid_y = block_y * lax.axis_size("gy")
    start_x = lax.axis_index("gx") * block_x
    start_y = lax.axis_index("gy") * block_y
    total_steps = wavelet.shape[0]
    slot_count = plan.shape[0]
    border = 0
    span_x = block_x + 2 * border
    span_y = block_y + 2 * border
    plane_cells = span_x * span_y
    values = lax.all_gather(traces, ("gx", "gy"), axis=1, tiled=True)
    cell_ids = lax.all_gather(receiver_cells, ("gx", "gy"), axis=1, tiled=True)
    cell_ids = cell_ids[0]
    local_x = cell_ids // grid_y - (start_x - border)
    local_y = cell_ids % grid_y - (start_y - border)
    in_block = (local_x >= 0) & (local_x < span_x) & (local_y >= 0) & (local_y < span_y)
    local_cell = jnp.where(in_block, local_x * span_y + local_y, plane_cells)
    injected = (
        jnp.zeros((total_steps, plane_cells), jnp.float32)
        .at[:, local_cell]
        .add(values, mode="drop")
    )
    injected = injected.reshape(total_steps, span_x, span_y)
    snapshots = jnp.zeros(stored_snapshots.shape, jnp.bfloat16)
    imaged = image_before
    along_x = start_x - 0 + lax.broadcasted_iota(jnp.int32, (block_x + 2 * 0, 1, 1), 0)
    along_y = start_y - 0 + lax.broadcasted_iota(jnp.int32, (1, block_y + 2 * 0, 1), 1)
    along_x, along_y = (along_x, along_y)
    along_z = lax.broadcasted_iota(jnp.int32, (1, 1, depth_cells), 2)
    cell_id = source_cell[0]
    matches = (along_x == cell_id // (grid_y * depth_cells)) & (
        along_y == cell_id // depth_cells % grid_y
    )
    matches = matches & (along_z == cell_id % depth_cells)
    source_core = matches.astype(jnp.float32)
    source_before, source_field = (source_prev, source_now)
    receiver_before, receiver_field = (receiver_prev, receiver_now)
    for step_index in range(total_steps):
        back_time = total_steps - 1 - step_index
        padded = with_halo(jnp.stack([source_field, receiver_field]), (("gx", 1), ("gy", 2)), 4)
        source_spread = stencil(padded[0]) + wavelet[step_index] * source_core
        receiver_spread = stencil(padded[1]).at[:, :, 0].add(injected[back_time])
        source_latest = 2.0 * source_field - source_before + speed_squared * source_spread
        receiver_latest = 2.0 * receiver_field - receiver_before + speed_squared * receiver_spread
        source_before, source_field = (source_field, source_latest)
        receiver_before, receiver_field = (receiver_field, receiver_latest)
        record_matches = plan == step_index
        snapshots = jnp.where(
            record_matches[:, None, None, None], source_field.astype(jnp.bfloat16)[None], snapshots
        )
        correlate_matches = plan == back_time
        slot_index = jnp.sum(
            jnp.where(correlate_matches, jnp.arange(slot_count, dtype=jnp.int32), 0)
        )
        present = jnp.any(correlate_matches)
        snapshot = lax.dynamic_index_in_dim(stored_snapshots, slot_index, 0, keepdims=False).astype(
            jnp.float32
        )
        imaged = imaged + jnp.where(present, snapshot * receiver_field, 0.0)
    source_last, source_final = (source_before, source_field)
    previous, current = (receiver_before, receiver_field)
    return (source_last, source_final, previous, current, snapshots, imaged)


def solution(mesh):
    placed = (
        P(("shot", "gx"), "gy", None),
        P(("shot", "gx"), "gy", None),
        P(("shot", "gx"), "gy", None),
        P(("shot", "gx"), "gy", None),
        P(("shot", "gx"), "gy", None),
        P("shot"),
        P("shot"),
        P("shot", ("gx", "gy")),
        P("shot", ("gx", "gy")),
        P("shot"),
        P("shot", "gx", "gy", None),
        P(("shot", "gx"), "gy", None),
    )
    return jax.shard_map(
        body,
        mesh=mesh,
        in_specs=placed,
        out_specs=(
            P(("shot", "gx"), "gy", None),
            P(("shot", "gx"), "gy", None),
            P(("shot", "gx"), "gy", None),
            P(("shot", "gx"), "gy", None),
            P("shot", "gx", "gy", None),
            P(("shot", "gx"), "gy", None),
        ),
        check_vma=False,
    )
```

profile of v0, /device:TPU:18, one launch (start us, length us, event | category | flops | bytes accessed | tf_op | source)
XLA Modules:
  0.0 254.4 jit_solution(9579591347282151355)
XLA Ops:
  1.6 2.5 collective-permute-start.1
  4.1 3.5 %collective-permute-start = (f32[2,4,8,320]{3,2,1,0:T(8,128)S(1)}, f32[2,4,8,320]{3,2,1,0:T(8,128)S(1)}, u32[]{:S(2)}, u32[]{:S(2)}) collective-permute-start(f32[2,4,8,320]{3,2,1,0:T(8,128)S(1)} %get-tuple-element.250), channel_id=1, source_target_pairs={{0,4},{4,8},{8,12},{1,5},{5,9},{9,13},{2,6},{6,10},{10,14},{3,7},{... | collective-permute-start | bytes 245768 | tf_op jit(solution)/shard_map/ppermute | solution.py:14
  9.7 9.4 %all-reduce.20 = s32[1024]{0:T(1024)S(1)} all-reduce(s32[1024]{0:T(1024)S(1)} %bitcast_dynamic-update-slice_fusion), channel_id=1, replica_groups=mesh['shot'=2,'gx'=4,'gy'=4] {'gx','gy'}, use_global_device_ids=true, to_apply=%add.20 | all-reduce | flops 1024 | bytes 8192
  23.8 15.2 %all-gather = f32[16,64,10]{1,2,0:T(8,128)S(1)} all-gather(f32[1,64,10]{1,2,0:T(8,128)S(1)} %bitcast.208), channel_id=1, replica_groups=mesh['shot'=2,'gx'=4,'gy'=4] {'gx','gy'}, dimensions={0}, use_global_device_ids=true | all-gather | bytes 43520 | tf_op jit(solution)/shard_map/all_gather | solution.py:68
  39.2 6.0 %scatter_custom_fusion = f32[10,64]{0,1:T(8,128)S(1)} fusion(s32[1024]{0:T(1024)S(1)} %bitcast.209, f32[1024,10]{1,0:T(8,128)S(1)} %bitcast.206, f32[]{:T(128)} %constant.323.clone.1), kind=kCustom, calls=%fused_computation.926 | custom fusion | flops 10240 | bytes 2564 | tf_op jit(solution)/shard_map/scatter-add | solution.py:78
  49.3 3.3 %collective-permute-start.5 = (f32[2,4,8,320]{3,2,1,0:T(8,128)S(1)}, f32[2,4,8,320]{3,2,1,0:T(8,128)S(1)}, u32[]{:S(2)}, u32[]{:S(2)}) collective-permute-start(f32[2,4,8,320]{3,2,1,0:T(8,128)S(1)} %get-tuple-element.249), channel_id=1, source_target_pairs={{4,0},{8,4},{12,8},{5,1},{9,5},{13,9},{6,2},{10,6},{14,10},{7,3},{... | collective-permute-start | bytes 245768 | tf_op jit(solution)/shard_map/ppermute | solution.py:17
  52.6 2.6 %collective-permute-start.4 = (f32[2,4,8,320]{3,2,1,0:T(8,128)S(1)}, f32[2,4,8,320]{3,2,1,0:T(8,128)S(1)}, u32[]{:S(2)}, u32[]{:S(2)}) collective-permute-start(f32[2,4,8,320]{3,2,1,0:T(8,128)S(1)} %get-tuple-element.248), channel_id=1, source_target_pairs={{0,4},{4,8},{8,12},{1,5},{5,9},{9,13},{2,6},{6,10},{10,14},{3,7},{... | collective-permute-start | bytes 245768 | tf_op jit(solution)/shard_map/ppermute | solution.py:14
  56.3 4.3 %collective-permute-done.4 = f32[2,4,8,320]{3,2,1,0:T(8,128)S(1)} collective-permute-done((f32[2,4,8,320]{3,2,1,0:T(8,128)S(1)}, f32[2,4,8,320]{3,2,1,0:T(8,128)S(1)}, u32[]{:S(2)}, u32[]{:S(2)}) %collective-permute-start.4) | collective-permute-done | bytes 81952 | tf_op jit(solution)/shard_map/ppermute | solution.py:14
  60.7 3.7 %collective-permute-start.7 = (f32[2,16,4,320]{3,1,2,0:T(8,128)S(1)}, f32[2,16,4,320]{3,1,2,0:T(8,128)S(1)}, u32[]{:S(2)}, u32[]{:S(2)}) collective-permute-start(f32[2,16,4,320]{3,1,2,0:T(8,128)S(1)} %copy.731), channel_id=1, source_target_pairs={{1,0},{2,1},{3,2},{5,4},{6,5},{7,6},{9,8},{10,9},{11,10},{13,12},{... | collective-permute-start | bytes 491528 | tf_op jit(solution)/shard_map/ppermute | solution.py:17
  67.7 3.8 %collective-permute-done.6 = f32[2,16,4,320]{3,1,2,0:T(8,128)S(1)} collective-permute-done((f32[2,16,4,320]{3,1,2,0:T(8,128)S(1)}, f32[2,16,4,320]{3,1,2,0:T(8,128)S(1)}, u32[]{:S(2)}, u32[]{:S(2)}) %collective-permute-start.6) | collective-permute-done | bytes 163872 | tf_op jit(solution)/shard_map/ppermute | solution.py:14
  73.1 3.3 %collective-permute-start.9 = (f32[2,4,8,320]{3,2,1,0:T(8,128)S(1)}, f32[2,4,8,320]{3,2,1,0:T(8,128)S(1)}, u32[]{:S(2)}, u32[]{:S(2)}) collective-permute-start(f32[2,4,8,320]{3,2,1,0:T(8,128)S(1)} %get-tuple-element.247), channel_id=1, source_target_pairs={{4,0},{8,4},{12,8},{5,1},{9,5},{13,9},{6,2},{10,6},{14,10},{7,3},{... | collective-permute-start | bytes 245768 | tf_op jit(solution)/shard_map/ppermute | solution.py:17
  76.5 2.5 collective-permute-start.8
  79.6 3.3 %collective-permute-done.8 = f32[2,4,8,320]{3,2,1,0:T(8,128)S(1)} collective-permute-done((f32[2,4,8,320]{3,2,1,0:T(8,128)S(1)}, f32[2,4,8,320]{3,2,1,0:T(8,128)S(1)}, u32[]{:S(2)}, u32[]{:S(2)}) %collective-permute-start.8) | collective-permute-done | bytes 81952 | tf_op jit(solution)/shard_map/ppermute | solution.py:14
  88.3 3.8 %collective-permute-done.10 = f32[2,16,4,320]{3,1,2,0:T(8,128)S(1)} collective-permute-done((f32[2,16,4,320]{3,1,2,0:T(8,128)S(1)}, f32[2,16,4,320]{3,1,2,0:T(8,128)S(1)}, u32[]{:S(2)}, u32[]{:S(2)}) %collective-permute-start.10) | collective-permute-done | bytes 163872 | tf_op jit(solution)/shard_map/ppermute | solution.py:14
  95.7 3.9 %collective-permute-start.12 = (f32[2,4,8,320]{3,2,1,0:T(8,128)S(1)}, f32[2,4,8,320]{3,2,1,0:T(8,128)S(1)}, u32[]{:S(2)}, u32[]{:S(2)}) collective-permute-start(f32[2,4,8,320]{3,2,1,0:T(8,128)S(1)} %get-tuple-element.244), channel_id=1, source_target_pairs={{0,4},{4,8},{8,12},{1,5},{5,9},{9,13},{2,6},{6,10},{10,14},{3,7},{... | collective-permute-start | bytes 245768 | tf_op jit(solution)/shard_map/ppermute | solution.py:14
  107.5 3.8 %collective-permute-done.14 = f32[2,16,4,320]{3,1,2,0:T(8,128)S(1)} collective-permute-done((f32[2,16,4,320]{3,1,2,0:T(8,128)S(1)}, f32[2,16,4,320]{3,1,2,0:T(8,128)S(1)}, u32[]{:S(2)}, u32[]{:S(2)}) %collective-permute-start.14) | collective-permute-done | bytes 163872 | tf_op jit(solution)/shard_map/ppermute | solution.py:14
  114.9 3.9 %collective-permute-start.16 = (f32[2,4,8,320]{3,2,1,0:T(8,128)S(1)}, f32[2,4,8,320]{3,2,1,0:T(8,128)S(1)}, u32[]{:S(2)}, u32[]{:S(2)}) collective-permute-start(f32[2,4,8,320]{3,2,1,0:T(8,128)S(1)} %get-tuple-element.242), channel_id=1, source_target_pairs={{0,4},{4,8},{8,12},{1,5},{5,9},{9,13},{2,6},{6,10},{10,14},{3,7},{... | collective-permute-start | bytes 245768 | tf_op jit(solution)/shard_map/ppermute | solution.py:14
  126.7 3.8 %collective-permute-done.18 = f32[2,16,4,320]{3,1,2,0:T(8,128)S(1)} collective-permute-done((f32[2,16,4,320]{3,1,2,0:T(8,128)S(1)}, f32[2,16,4,320]{3,1,2,0:T(8,128)S(1)}, u32[]{:S(2)}, u32[]{:S(2)}) %collective-permute-start.18) | collective-permute-done | bytes 163872 | tf_op jit(solution)/shard_map/ppermute | solution.py:14
  134.2 3.9 %collective-permute-start.20 = (f32[2,4,8,320]{3,2,1,0:T(8,128)S(1)}, f32[2,4,8,320]{3,2,1,0:T(8,128)S(1)}, u32[]{:S(2)}, u32[]{:S(2)}) collective-permute-start(f32[2,4,8,320]{3,2,1,0:T(8,128)S(1)} %get-tuple-element.240), channel_id=1, source_target_pairs={{0,4},{4,8},{8,12},{1,5},{5,9},{9,13},{2,6},{6,10},{10,14},{3,7},{... | collective-permute-start | bytes 245768 | tf_op jit(solution)/shard_map/ppermute | solution.py:14
  142.8 2.6 %collective-permute-start.22 = (f32[2,16,4,320]{3,1,2,0:T(8,128)S(1)}, f32[2,16,4,320]{3,1,2,0:T(8,128)S(1)}, u32[]{:S(2)}, u32[]{:S(2)}) collective-permute-start(f32[2,16,4,320]{3,1,2,0:T(8,128)S(1)} %copy.738), channel_id=1, source_target_pairs={{0,1},{1,2},{2,3},{4,5},{5,6},{6,7},{8,9},{9,10},{10,11},{12,13},{... | collective-permute-start | bytes 491528 | tf_op jit(solution)/shard_map/ppermute | solution.py:14
  146.0 3.8 %collective-permute-done.22 = f32[2,16,4,320]{3,1,2,0:T(8,128)S(1)} collective-permute-done((f32[2,16,4,320]{3,1,2,0:T(8,128)S(1)}, f32[2,16,4,320]{3,1,2,0:T(8,128)S(1)}, u32[]{:S(2)}, u32[]{:S(2)}) %collective-permute-start.22) | collective-permute-done | bytes 163872 | tf_op jit(solution)/shard_map/ppermute | solution.py:14
  153.5 3.9 %collective-permute-start.24 = (f32[2,4,8,320]{3,2,1,0:T(8,128)S(1)}, f32[2,4,8,320]{3,2,1,0:T(8,128)S(1)}, u32[]{:S(2)}, u32[]{:S(2)}) collective-permute-start(f32[2,4,8,320]{3,2,1,0:T(8,128)S(1)} %get-tuple-element.238), channel_id=1, source_target_pairs={{0,4},{4,8},{8,12},{1,5},{5,9},{9,13},{2,6},{6,10},{10,14},{3,7},{... | collective-permute-start | bytes 245768 | tf_op jit(solution)/shard_map/ppermute | solution.py:14
  162.0 2.4 collective-permute-start.26
  165.3 3.8 %collective-permute-done.26 = f32[2,16,4,320]{3,1,2,0:T(8,128)S(1)} collective-permute-done((f32[2,16,4,320]{3,1,2,0:T(8,128)S(1)}, f32[2,16,4,320]{3,1,2,0:T(8,128)S(1)}, u32[]{:S(2)}, u32[]{:S(2)}) %collective-permute-start.26) | collective-permute-done | bytes 163872 | tf_op jit(solution)/shard_map/ppermute | solution.py:14
  172.7 3.9 %collective-permute-start.28 = (f32[2,4,8,320]{3,2,1,0:T(8,128)S(1)}, f32[2,4,8,320]{3,2,1,0:T(8,128)S(1)}, u32[]{:S(2)}, u32[]{:S(2)}) collective-permute-start(f32[2,4,8,320]{3,2,1,0:T(8,128)S(1)} %get-tuple-element.236), channel_id=1, source_target_pairs={{0,4},{4,8},{8,12},{1,5},{5,9},{9,13},{2,6},{6,10},{10,14},{3,7},{... | collective-permute-start | bytes 245768 | tf_op jit(solution)/shard_map/ppermute | solution.py:14
  184.5 3.8 %collective-permute-done.30 = f32[2,16,4,320]{3,1,2,0:T(8,128)S(1)} collective-permute-done((f32[2,16,4,320]{3,1,2,0:T(8,128)S(1)}, f32[2,16,4,320]{3,1,2,0:T(8,128)S(1)}, u32[]{:S(2)}, u32[]{:S(2)}) %collective-permute-start.30) | collective-permute-done | bytes 163872 | tf_op jit(solution)/shard_map/ppermute | solution.py:14
  192.0 3.9 %collective-permute-start.32 = (f32[2,4,8,320]{3,2,1,0:T(8,128)S(1)}, f32[2,4,8,320]{3,2,1,0:T(8,128)S(1)}, u32[]{:S(2)}, u32[]{:S(2)}) collective-permute-start(f32[2,4,8,320]{3,2,1,0:T(8,128)S(1)} %get-tuple-element.234), channel_id=1, source_target_pairs={{0,4},{4,8},{8,12},{1,5},{5,9},{9,13},{2,6},{6,10},{10,14},{3,7},{... | collective-permute-start | bytes 245768 | tf_op jit(solution)/shard_map/ppermute | solution.py:14
  200.5 2.4 collective-permute-start.34
  203.8 3.8 %collective-permute-done.34 = f32[2,16,4,320]{3,1,2,0:T(8,128)S(1)} collective-permute-done((f32[2,16,4,320]{3,1,2,0:T(8,128)S(1)}, f32[2,16,4,320]{3,1,2,0:T(8,128)S(1)}, u32[]{:S(2)}, u32[]{:S(2)}) %collective-permute-start.34) | collective-permute-done | bytes 163872 | tf_op jit(solution)/shard_map/ppermute | solution.py:14
  211.4 3.9 %collective-permute-start.36 = (f32[2,4,8,320]{3,2,1,0:T(8,128)S(1)}, f32[2,4,8,320]{3,2,1,0:T(8,128)S(1)}, u32[]{:S(2)}, u32[]{:S(2)}) collective-permute-start(f32[2,4,8,320]{3,2,1,0:T(8,128)S(1)} %get-tuple-element.232), channel_id=1, source_target_pairs={{0,4},{4,8},{8,12},{1,5},{5,9},{9,13},{2,6},{6,10},{10,14},{3,7},{... | collective-permute-start | bytes 245768 | tf_op jit(solution)/shard_map/ppermute | solution.py:14
  240.4 3.7 %collective-permute-done.38 = f32[2,16,4,320]{3,1,2,0:T(8,128)S(1)} collective-permute-done((f32[2,16,4,320]{3,1,2,0:T(8,128)S(1)}, f32[2,16,4,320]{3,1,2,0:T(8,128)S(1)}, u32[]{:S(2)}, u32[]{:S(2)}) %collective-permute-start.38) | collective-permute-done | bytes 163872 | tf_op jit(solution)/shard_map/ppermute | solution.py:14
  247.4 7.1 %fusion.361 = (f32[8,8,320]{2,1,0:T(8,128)}, f32[8,8,320]{2,1,0:T(8,128)}) fusion(f32[8,8,320]{2,1,0:T(8,128)S(1)} %multiply_add_fusion.1, f32[8,8,320]{2,1,0:T(8,128)S(1)} %multiply_add_fusion.3, f32[8,8,320]{2,1,0:T(8,128)S(1)} %multiply_add_fusion.4, f32[8,8,320]{2,1,0:T(8,128)S(1)} %multiply_add_fusion.8, f32[8,8,320]{2,1,0:T(8,128)S(1)} %copy-done.7, ...), kind=kLoop, calls=%fused_computation.864 | loop fusion | flops 1228800 | bytes 1556530 | tf_op jit(solution)/shard_map/add | solution.py:116
  (231 shorter events, 96.8 us)
Async XLA Ops:
  1.6 17.6 %collective-permute-start.1 = (f32[2,4,8,320]{3,2,1,0:T(8,128)S(1)}, f32[2,4,8,320]{3,2,1,0:T(8,128)S(1)}, u32[]{:S(2)}, u32[]{:S(2)}) collective-permute-start(f32[2,4,8,320]{3,2,1,0:T(8,128)S(1)} %get-tuple-element.251), channel_id=1, source_target_pairs={{4,0},{8,4},{12,8},{5,1},{9,5},{13,9},{6,2},{10,6},{14,10},{7,3},{... | collective-permute-start | bytes 245768 | tf_op jit(solution)/shard_map/ppermute | solution.py:17
  4.1 15.1 %collective-permute-start = (f32[2,4,8,320]{3,2,1,0:T(8,128)S(1)}, f32[2,4,8,320]{3,2,1,0:T(8,128)S(1)}, u32[]{:S(2)}, u32[]{:S(2)}) collective-permute-start(f32[2,4,8,320]{3,2,1,0:T(8,128)S(1)} %get-tuple-element.250), channel_id=1, source_target_pairs={{0,4},{4,8},{8,12},{1,5},{5,9},{9,13},{2,6},{6,10},{10,14},{3,7},{... | collective-permute-start | bytes 245768 | tf_op jit(solution)/shard_map/ppermute | solution.py:14
  19.3 26.6 %collective-permute-start.3 = (f32[2,16,4,320]{3,1,2,0:T(8,128)S(1)}, f32[2,16,4,320]{3,1,2,0:T(8,128)S(1)}, u32[]{:S(2)}, u32[]{:S(2)}) collective-permute-start(f32[2,16,4,320]{3,1,2,0:T(8,128)S(1)} %copy.729), channel_id=1, source_target_pairs={{1,0},{2,1},{3,2},{5,4},{6,5},{7,6},{9,8},{10,9},{11,10},{13,12},{... | collective-permute-start | bytes 491528 | tf_op jit(solution)/shard_map/ppermute | solution.py:17
  21.3 24.7 %collective-permute-start.2 = (f32[2,16,4,320]{3,1,2,0:T(8,128)S(1)}, f32[2,16,4,320]{3,1,2,0:T(8,128)S(1)}, u32[]{:S(2)}, u32[]{:S(2)}) collective-permute-start(f32[2,16,4,320]{3,1,2,0:T(8,128)S(1)} %copy.728), channel_id=1, source_target_pairs={{0,1},{1,2},{2,3},{4,5},{5,6},{6,7},{8,9},{9,10},{10,11},{12,13},{... | collective-permute-start | bytes 491528 | tf_op jit(solution)/shard_map/ppermute | solution.py:14
  49.3 6.9 %collective-permute-start.5 = (f32[2,4,8,320]{3,2,1,0:T(8,128)S(1)}, f32[2,4,8,320]{3,2,1,0:T(8,128)S(1)}, u32[]{:S(2)}, u32[]{:S(2)}) collective-permute-start(f32[2,4,8,320]{3,2,1,0:T(8,128)S(1)} %get-tuple-element.249), channel_id=1, source_target_pairs={{4,0},{8,4},{12,8},{5,1},{9,5},{13,9},{6,2},{10,6},{14,10},{7,3},{... | collective-permute-start | bytes 245768 | tf_op jit(solution)/shard_map/ppermute | solution.py:17
  52.6 8.0 %collective-permute-start.4 = (f32[2,4,8,320]{3,2,1,0:T(8,128)S(1)}, f32[2,4,8,320]{3,2,1,0:T(8,128)S(1)}, u32[]{:S(2)}, u32[]{:S(2)}) collective-permute-start(f32[2,4,8,320]{3,2,1,0:T(8,128)S(1)} %get-tuple-element.248), channel_id=1, source_target_pairs={{0,4},{4,8},{8,12},{1,5},{5,9},{9,13},{2,6},{6,10},{10,14},{3,7},{... | collective-permute-start | bytes 245768 | tf_op jit(solution)/shard_map/ppermute | solution.py:14
  60.7 6.9 %collective-permute-start.7 = (f32[2,16,4,320]{3,1,2,0:T(8,128)S(1)}, f32[2,16,4,320]{3,1,2,0:T(8,128)S(1)}, u32[]{:S(2)}, u32[]{:S(2)}) collective-permute-start(f32[2,16,4,320]{3,1,2,0:T(8,128)S(1)} %copy.731), channel_id=1, source_target_pairs={{1,0},{2,1},{3,2},{5,4},{6,5},{7,6},{9,8},{10,9},{11,10},{13,12},{... | collective-permute-start | bytes 491528 | tf_op jit(solution)/shard_map/ppermute | solution.py:17
  64.4 7.0 %collective-permute-start.6 = (f32[2,16,4,320]{3,1,2,0:T(8,128)S(1)}, f32[2,16,4,320]{3,1,2,0:T(8,128)S(1)}, u32[]{:S(2)}, u32[]{:S(2)}) collective-permute-start(f32[2,16,4,320]{3,1,2,0:T(8,128)S(1)} %copy.730), channel_id=1, source_target_pairs={{0,1},{1,2},{2,3},{4,5},{5,6},{6,7},{8,9},{9,10},{10,11},{12,13},{... | collective-permute-start | bytes 491528 | tf_op jit(solution)/shard_map/ppermute | solution.py:14
  73.1 6.5 %collective-permute-start.9 = (f32[2,4,8,320]{3,2,1,0:T(8,128)S(1)}, f32[2,4,8,320]{3,2,1,0:T(8,128)S(1)}, u32[]{:S(2)}, u32[]{:S(2)}) collective-permute-start(f32[2,4,8,320]{3,2,1,0:T(8,128)S(1)} %get-tuple-element.247), channel_id=1, source_target_pairs={{4,0},{8,4},{12,8},{5,1},{9,5},{13,9},{6,2},{10,6},{14,10},{7,3},{... | collective-permute-start | bytes 245768 | tf_op jit(solution)/shard_map/ppermute | solution.py:17
  76.5 6.5 %collective-permute-start.8 = (f32[2,4,8,320]{3,2,1,0:T(8,128)S(1)}, f32[2,4,8,320]{3,2,1,0:T(8,128)S(1)}, u32[]{:S(2)}, u32[]{:S(2)}) collective-permute-start(f32[2,4,8,320]{3,2,1,0:T(8,128)S(1)} %get-tuple-element.246), channel_id=1, source_target_pairs={{0,4},{4,8},{8,12},{1,5},{5,9},{9,13},{2,6},{6,10},{10,14},{3,7},{... | collective-permute-start | bytes 245768 | tf_op jit(solution)/shard_map/ppermute | solution.py:14
  85.0 7.0 %collective-permute-start.10 = (f32[2,16,4,320]{3,1,2,0:T(8,128)S(1)}, f32[2,16,4,320]{3,1,2,0:T(8,128)S(1)}, u32[]{:S(2)}, u32[]{:S(2)}) collective-permute-start(f32[2,16,4,320]{3,1,2,0:T(8,128)S(1)} %copy.732), channel_id=1, source_target_pairs={{0,1},{1,2},{2,3},{4,5},{5,6},{6,7},{8,9},{9,10},{10,11},{12,13},{... | collective-permute-start | bytes 491528 | tf_op jit(solution)/shard_map/ppermute | solution.py:14
  93.7 6.5 %collective-permute-start.13 = (f32[2,4,8,320]{3,2,1,0:T(8,128)S(1)}, f32[2,4,8,320]{3,2,1,0:T(8,128)S(1)}, u32[]{:S(2)}, u32[]{:S(2)}) collective-permute-start(f32[2,4,8,320]{3,2,1,0:T(8,128)S(1)} %get-tuple-element.245), channel_id=1, source_target_pairs={{4,0},{8,4},{12,8},{5,1},{9,5},{13,9},{6,2},{10,6},{14,10},{7,3},{... | collective-permute-start | bytes 245768 | tf_op jit(solution)/shard_map/ppermute | solution.py:17
  95.7 6.5 %collective-permute-start.12 = (f32[2,4,8,320]{3,2,1,0:T(8,128)S(1)}, f32[2,4,8,320]{3,2,1,0:T(8,128)S(1)}, u32[]{:S(2)}, u32[]{:S(2)}) collective-permute-start(f32[2,4,8,320]{3,2,1,0:T(8,128)S(1)} %get-tuple-element.244), channel_id=1, source_target_pairs={{0,4},{4,8},{8,12},{1,5},{5,9},{9,13},{2,6},{6,10},{10,14},{3,7},{... | collective-permute-start | bytes 245768 | tf_op jit(solution)/shard_map/ppermute | solution.py:14
  104.3 7.0 %collective-permute-start.14 = (f32[2,16,4,320]{3,1,2,0:T(8,128)S(1)}, f32[2,16,4,320]{3,1,2,0:T(8,128)S(1)}, u32[]{:S(2)}, u32[]{:S(2)}) collective-permute-start(f32[2,16,4,320]{3,1,2,0:T(8,128)S(1)} %copy.734), channel_id=1, source_target_pairs={{0,1},{1,2},{2,3},{4,5},{5,6},{6,7},{8,9},{9,10},{10,11},{12,13},{... | collective-permute-start | bytes 491528 | tf_op jit(solution)/shard_map/ppermute | solution.py:14
  113.0 6.5 %collective-permute-start.17 = (f32[2,4,8,320]{3,2,1,0:T(8,128)S(1)}, f32[2,4,8,320]{3,2,1,0:T(8,128)S(1)}, u32[]{:S(2)}, u32[]{:S(2)}) collective-permute-start(f32[2,4,8,320]{3,2,1,0:T(8,128)S(1)} %get-tuple-element.243), channel_id=1, source_target_pairs={{4,0},{8,4},{12,8},{5,1},{9,5},{13,9},{6,2},{10,6},{14,10},{7,3},{... | collective-permute-start | bytes 245768 | tf_op jit(solution)/shard_map/ppermute | solution.py:17
  114.9 6.5 %collective-permute-start.16 = (f32[2,4,8,320]{3,2,1,0:T(8,128)S(1)}, f32[2,4,8,320]{3,2,1,0:T(8,128)S(1)}, u32[]{:S(2)}, u32[]{:S(2)}) collective-permute-start(f32[2,4,8,320]{3,2,1,0:T(8,128)S(1)} %get-tuple-element.242), channel_id=1, source_target_pairs={{0,4},{4,8},{8,12},{1,5},{5,9},{9,13},{2,6},{6,10},{10,14},{3,7},{... | collective-permute-start | bytes 245768 | tf_op jit(solution)/shard_map/ppermute | solution.py:14
  123.5 7.0 %collective-permute-start.18 = (f32[2,16,4,320]{3,1,2,0:T(8,128)S(1)}, f32[2,16,4,320]{3,1,2,0:T(8,128)S(1)}, u32[]{:S(2)}, u32[]{:S(2)}) collective-permute-start(f32[2,16,4,320]{3,1,2,0:T(8,128)S(1)} %copy.736), channel_id=1, source_target_pairs={{0,1},{1,2},{2,3},{4,5},{5,6},{6,7},{8,9},{9,10},{10,11},{12,13},{... | collective-permute-start | bytes 491528 | tf_op jit(solution)/shard_map/ppermute | solution.py:14
  132.2 6.5 %collective-permute-start.21 = (f32[2,4,8,320]{3,2,1,0:T(8,128)S(1)}, f32[2,4,8,320]{3,2,1,0:T(8,128)S(1)}, u32[]{:S(2)}, u32[]{:S(2)}) collective-permute-start(f32[2,4,8,320]{3,2,1,0:T(8,128)S(1)} %get-tuple-element.241), channel_id=1, source_target_pairs={{4,0},{8,4},{12,8},{5,1},{9,5},{13,9},{6,2},{10,6},{14,10},{7,3},{... | collective-permute-start | bytes 245768 | tf_op jit(solution)/shard_map/ppermute | solution.py:17
  134.2 6.5 %collective-permute-start.20 = (f32[2,4,8,320]{3,2,1,0:T(8,128)S(1)}, f32[2,4,8,320]{3,2,1,0:T(8,128)S(1)}, u32[]{:S(2)}, u32[]{:S(2)}) collective-permute-start(f32[2,4,8,320]{3,2,1,0:T(8,128)S(1)} %get-tuple-element.240), channel_id=1, source_target_pairs={{0,4},{4,8},{8,12},{1,5},{5,9},{9,13},{2,6},{6,10},{10,14},{3,7},{... | collective-permute-start | bytes 245768 | tf_op jit(solution)/shard_map/ppermute | solution.py:14
  142.8 7.0 %collective-permute-start.22 = (f32[2,16,4,320]{3,1,2,0:T(8,128)S(1)}, f32[2,16,4,320]{3,1,2,0:T(8,128)S(1)}, u32[]{:S(2)}, u32[]{:S(2)}) collective-permute-start(f32[2,16,4,320]{3,1,2,0:T(8,128)S(1)} %copy.738), channel_id=1, source_target_pairs={{0,1},{1,2},{2,3},{4,5},{5,6},{6,7},{8,9},{9,10},{10,11},{12,13},{... | collective-permute-start | bytes 491528 | tf_op jit(solution)/shard_map/ppermute | solution.py:14
  151.5 6.5 %collective-permute-start.25 = (f32[2,4,8,320]{3,2,1,0:T(8,128)S(1)}, f32[2,4,8,320]{3,2,1,0:T(8,128)S(1)}, u32[]{:S(2)}, u32[]{:S(2)}) collective-permute-start(f32[2,4,8,320]{3,2,1,0:T(8,128)S(1)} %get-tuple-element.239), channel_id=1, source_target_pairs={{4,0},{8,4},{12,8},{5,1},{9,5},{13,9},{6,2},{10,6},{14,10},{7,3},{... | collective-permute-start | bytes 245768 | tf_op jit(solution)/shard_map/ppermute | solution.py:17
  153.5 6.5 %collective-permute-start.24 = (f32[2,4,8,320]{3,2,1,0:T(8,128)S(1)}, f32[2,4,8,320]{3,2,1,0:T(8,128)S(1)}, u32[]{:S(2)}, u32[]{:S(2)}) collective-permute-start(f32[2,4,8,320]{3,2,1,0:T(8,128)S(1)} %get-tuple-element.238), channel_id=1, source_target_pairs={{0,4},{4,8},{8,12},{1,5},{5,9},{9,13},{2,6},{6,10},{10,14},{3,7},{... | collective-permute-start | bytes 245768 | tf_op jit(solution)/shard_map/ppermute | solution.py:14
  162.0 7.0 %collective-permute-start.26 = (f32[2,16,4,320]{3,1,2,0:T(8,128)S(1)}, f32[2,16,4,320]{3,1,2,0:T(8,128)S(1)}, u32[]{:S(2)}, u32[]{:S(2)}) collective-permute-start(f32[2,16,4,320]{3,1,2,0:T(8,128)S(1)} %copy.740), channel_id=1, source_target_pairs={{0,1},{1,2},{2,3},{4,5},{5,6},{6,7},{8,9},{9,10},{10,11},{12,13},{... | collective-permute-start | bytes 491528 | tf_op jit(solution)/shard_map/ppermute | solution.py:14
  170.8 6.5 %collective-permute-start.29 = (f32[2,4,8,320]{3,2,1,0:T(8,128)S(1)}, f32[2,4,8,320]{3,2,1,0:T(8,128)S(1)}, u32[]{:S(2)}, u32[]{:S(2)}) collective-permute-start(f32[2,4,8,320]{3,2,1,0:T(8,128)S(1)} %get-tuple-element.237), channel_id=1, source_target_pairs={{4,0},{8,4},{12,8},{5,1},{9,5},{13,9},{6,2},{10,6},{14,10},{7,3},{... | collective-permute-start | bytes 245768 | tf_op jit(solution)/shard_map/ppermute | solution.py:17
  172.7 6.5 %collective-permute-start.28 = (f32[2,4,8,320]{3,2,1,0:T(8,128)S(1)}, f32[2,4,8,320]{3,2,1,0:T(8,128)S(1)}, u32[]{:S(2)}, u32[]{:S(2)}) collective-permute-start(f32[2,4,8,320]{3,2,1,0:T(8,128)S(1)} %get-tuple-element.236), channel_id=1, source_target_pairs={{0,4},{4,8},{8,12},{1,5},{5,9},{9,13},{2,6},{6,10},{10,14},{3,7},{... | collective-permute-start | bytes 245768 | tf_op jit(solution)/shard_map/ppermute | solution.py:14
  181.3 7.0 %collective-permute-start.30 = (f32[2,16,4,320]{3,1,2,0:T(8,128)S(1)}, f32[2,16,4,320]{3,1,2,0:T(8,128)S(1)}, u32[]{:S(2)}, u32[]{:S(2)}) collective-permute-start(f32[2,16,4,320]{3,1,2,0:T(8,128)S(1)} %copy.742), channel_id=1, source_target_pairs={{0,1},{1,2},{2,3},{4,5},{5,6},{6,7},{8,9},{9,10},{10,11},{12,13},{... | collective-permute-start | bytes 491528 | tf_op jit(solution)/shard_map/ppermute | solution.py:14
  190.0 6.5 %collective-permute-start.33 = (f32[2,4,8,320]{3,2,1,0:T(8,128)S(1)}, f32[2,4,8,320]{3,2,1,0:T(8,128)S(1)}, u32[]{:S(2)}, u32[]{:S(2)}) collective-permute-start(f32[2,4,8,320]{3,2,1,0:T(8,128)S(1)} %get-tuple-element.235), channel_id=1, source_target_pairs={{4,0},{8,4},{12,8},{5,1},{9,5},{13,9},{6,2},{10,6},{14,10},{7,3},{... | collective-permute-start | bytes 245768 | tf_op jit(solution)/shard_map/ppermute | solution.py:17
  192.0 6.5 %collective-permute-start.32 = (f32[2,4,8,320]{3,2,1,0:T(8,128)S(1)}, f32[2,4,8,320]{3,2,1,0:T(8,128)S(1)}, u32[]{:S(2)}, u32[]{:S(2)}) collective-permute-start(f32[2,4,8,320]{3,2,1,0:T(8,128)S(1)} %get-tuple-element.234), channel_id=1, source_target_pairs={{0,4},{4,8},{8,12},{1,5},{5,9},{9,13},{2,6},{6,10},{10,14},{3,7},{... | collective-permute-start | bytes 245768 | tf_op jit(solution)/shard_map/ppermute | solution.py:14
  200.5 7.0 %collective-permute-start.34 = (f32[2,16,4,320]{3,1,2,0:T(8,128)S(1)}, f32[2,16,4,320]{3,1,2,0:T(8,128)S(1)}, u32[]{:S(2)}, u32[]{:S(2)}) collective-permute-start(f32[2,16,4,320]{3,1,2,0:T(8,128)S(1)} %copy.744), channel_id=1, source_target_pairs={{0,1},{1,2},{2,3},{4,5},{5,6},{6,7},{8,9},{9,10},{10,11},{12,13},{... | collective-permute-start | bytes 491528 | tf_op jit(solution)/shard_map/ppermute | solution.py:14
  209.3 25.6 %collective-permute-start.37 = (f32[2,4,8,320]{3,2,1,0:T(8,128)S(1)}, f32[2,4,8,320]{3,2,1,0:T(8,128)S(1)}, u32[]{:S(2)}, u32[]{:S(2)}) collective-permute-start(f32[2,4,8,320]{3,2,1,0:T(8,128)S(1)} %get-tuple-element.233), channel_id=1, source_target_pairs={{4,0},{8,4},{12,8},{5,1},{9,5},{13,9},{6,2},{10,6},{14,10},{7,3},{... | collective-permute-start | bytes 245768 | tf_op jit(solution)/shard_map/ppermute | solution.py:17
  211.4 23.6 %collective-permute-start.36 = (f32[2,4,8,320]{3,2,1,0:T(8,128)S(1)}, f32[2,4,8,320]{3,2,1,0:T(8,128)S(1)}, u32[]{:S(2)}, u32[]{:S(2)}) collective-permute-start(f32[2,4,8,320]{3,2,1,0:T(8,128)S(1)} %get-tuple-element.232), channel_id=1, source_target_pairs={{0,4},{4,8},{8,12},{1,5},{5,9},{9,13},{2,6},{6,10},{10,14},{3,7},{... | collective-permute-start | bytes 245768 | tf_op jit(solution)/shard_map/ppermute | solution.py:14
  237.1 7.0 %collective-permute-start.38 = (f32[2,16,4,320]{3,1,2,0:T(8,128)S(1)}, f32[2,16,4,320]{3,1,2,0:T(8,128)S(1)}, u32[]{:S(2)}, u32[]{:S(2)}) collective-permute-start(f32[2,16,4,320]{3,1,2,0:T(8,128)S(1)} %copy.746), channel_id=1, source_target_pairs={{0,1},{1,2},{2,3},{4,5},{5,6},{6,7},{8,9},{9,10},{10,11},{12,13},{... | collective-permute-start | bytes 491528 | tf_op jit(solution)/shard_map/ppermute | solution.py:14
  (22 other events, 187.4 us)
where the time goes:
time: 256 us; the launch traced here: 254 us
  starting transfers between devices  104 us (41%)
  waiting for transfers between devices  64.7 us (25%)
  other arithmetic  32.2 us (13%)
  blocking collectives  24.6 us (10%)
  between operations  22.2 us (9%)
  local copies, waits for them, and re-layouts  7.13 us (3%)
    ppermute x20, starting transfers between devices, with_halo(): lax.ppermute(lax.slice_in_dim(block, block.shape[dim] - width, None, axis...  59.9 us
    ppermute x20, waiting for transfers between devices, with_halo(): lax.ppermute(lax.slice_in_dim(block, block.shape[dim] - width, None, axis...  53 us
    ppermute x20, starting transfers between devices, with_halo(): lax.ppermute(lax.slice_in_dim(block, 0, width, axis=dim), axis, backward)  43.7 us
    all_gather x1, blocking collectives, body(): values = lax.all_gather(traces, ('gx', 'gy'), axis=1, tiled=True)  15.2 us
    ppermute x20, waiting for transfers between devices, with_halo(): lax.ppermute(lax.slice_in_dim(block, 0, width, axis=dim), axis, backward)  11.7 us
    convert_element_type x10, other arithmetic, body(): source_field.astype(jnp.bfloat16)[None]  9.89 us
    unnamed x1, blocking collectives  9.37 us
    add x1, other arithmetic, body(): imaged = imaged + jnp.where(present, snapshot * receiver_field, 0.0)  7.05 us
  transfers between devices with their start and end apart: 40, of which 33 were waited for; matrix products, arithmetic and copies ran while one was open for 4% of the time, Pallas kernels for 0%

commit v1 on v0

v1 whole, which is shorter than its diff:
```python
import functools

import jax
import jax.numpy as jnp
from jax import lax
from jax.experimental import pallas as pl
from jax.experimental.pallas import tpu as pltpu
from jax.sharding import PartitionSpec as P

STENCIL_COEFFS = (-205.0 / 72.0, 8.0 / 5.0, -1.0 / 5.0, 8.0 / 315.0, -1.0 / 560.0)
REACH = 4
HALO = 2 * REACH
LANES = 128
ROWS = 8
AXES = ("gx", "gy")


class Layout:
    def __init__(self, mesh, block_x, block_y, depth, steps, slots):
        self.nx, self.ny = mesh.shape["gx"], mesh.shape["gy"]
        self.columns = self.ny // 2
        self.bx, self.by, self.depth = block_x, block_y, depth
        self.steps, self.slots = steps, slots
        self.cy = 2 * block_y
        self.zt = pl.cdiv(depth + REACH, LANES)
        self.rest = depth - (self.zt - 1) * LANES
        self.packed = 0 < self.rest <= LANES // 2
        self.ex, self.ey = block_x + 2 * REACH, self.cy + 2 * REACH
        self.zrows = self.cy * (self.zt - 1) + self.cy // 2 if self.packed else self.cy * self.zt
        self.z_parities = [p for p in (0, 1) if p + 1 < self.nx]
        self.y_parities = [p for p in (0, 1) if p + 1 < self.columns]
        assert self.ny % 2 == 0 and block_x >= HALO and block_y % ROWS == 0 and steps % 2 == 0

    def device(self, x, column, core):
        return x * self.ny + 2 * column + core

    def permutation(self, move):
        pairs = []
        for x in range(self.nx):
            for column in range(self.columns):
                other = move(x, column)
                there = 0 <= other[0] < self.nx and 0 <= other[1] < self.columns
                for core in (0, 1):
                    target = self.device(*other, core) if there else self.device(x, column, 1 - core)
                    pairs.append((self.device(x, column, core), target))
        return pairs

    def z_permutation(self, pz):
        return self.permutation(lambda x, c: (x + (1 if x % 2 == pz else -1), c))

    def y_permutation(self, py):
        return self.permutation(lambda x, c: (x, c + (1 if c % 2 == py else -1)))

    def d_permutation(self, pz, py):
        return self.permutation(
            lambda x, c: (x + (1 if x % 2 == pz else -1), c + (1 if c % 2 == py else -1))
        )

    def core_permutation(self):
        return self.permutation(lambda x, c: (-1, -1))

    def place(self):
        gx, gy = lax.axis_index("gx"), lax.axis_index("gy")
        return gx, gy // 2, gy % 2

    def z_side(self, pz):
        gx, _, _ = self.place()
        right = gx % 2 == pz
        return right, jnp.where(right, gx + 1 < self.nx, gx > 0)

    def y_side(self, py):
        _, column, _ = self.place()
        high = column % 2 == py
        return high, jnp.where(high, column + 1 < self.columns, column > 0)


def lane_ids(rows):
    return lax.broadcasted_iota(jnp.int32, (rows, LANES), 1)


def pack(tiles, lay, rows):
    if not lay.packed:
        return list(tiles)
    last = tiles[-1]
    return list(tiles[:-1]) + [last[: rows // 2] + pltpu.roll(last[rows // 2 :], LANES // 2, 1)]


def unpack(block, lay, rows):
    tiles = [block[t * rows : (t + 1) * rows] for t in range(lay.zt - 1)]
    start = (lay.zt - 1) * rows
    if not lay.packed:
        return tiles + [block[start : start + rows]]
    both = block[start : start + rows // 2]
    low = lane_ids(rows // 2) < LANES // 2
    first = jnp.where(low, both, 0.0)
    second = pltpu.roll(jnp.where(low, 0.0, both), LANES // 2, 1)
    return tiles + [jnp.concatenate([first, second], 0)]


def store_packed(ref, index, tiles, lay, rows):
    row = 0
    for piece in pack(tiles, lay, rows):
        ref[index, row : row + piece.shape[0], :] = piece
        row += piece.shape[0]


def write_y_message(ref, lead, source, lay, high):
    for x in range(lay.bx):
        for t in range(lay.zt):
            rows = jnp.where(
                high, source[x, t, lay.cy - ROWS : lay.cy, :], source[x, t, 0:ROWS, :]
            )
            ref[lead * lay.bx + x, t * ROWS : (t + 1) * ROWS, :] = rows


def write_d_message(ref, source, lay, right, high):
    start = jnp.where(right, lay.bx - REACH, 0)
    for x in range(REACH):
        for t in range(lay.zt):
            rows = jnp.where(
                high,
                source[start + x, t, lay.cy - ROWS : lay.cy, :],
                source[start + x, t, 0:ROWS, :],
            )
            ref[x, t * ROWS : (t + 1) * ROWS, :] = rows


def prepare_kernel(lay, *refs):
    (src_now, src_prev, rec_now, rec_prev, speed, other), refs = refs[:6], refs[6:]
    (p, q, s), refs = refs[:3], refs[3:]
    nz, ny = len(lay.z_parities), len(lay.y_parities)
    z_messages, refs = refs[:nz], refs[nz:]
    y_messages, d_messages = refs[:ny], refs[ny:]
    _, _, core = lay.place()
    first = core == 0
    edge = (lay.zt - 1) * LANES
    for ref in (p, q, s):
        ref[:, lay.zt - 1, :, :] = jnp.zeros((lay.bx, lay.cy, LANES), jnp.float32)
    for index, (ref, a, b) in enumerate(((p, src_now, rec_now), (q, src_prev, rec_prev), (s, speed, speed))):
        for x in range(lay.bx):
            for t in range(lay.zt):
                width = LANES if t + 1 < lay.zt else lay.rest
                lanes = slice(t * LANES, t * LANES + width)
                mine = a[x, :, lanes] if a is b else jnp.where(first, a[x, :, lanes], b[x, :, lanes])
                theirs = other[index, x, :, lanes]
                ref[x, t, 0 : lay.by, 0:width] = jnp.where(first, mine, theirs)
                ref[x, t, lay.by : lay.cy, 0:width] = jnp.where(first, theirs, mine)
    sides = [lay.z_side(pz)[0] for pz in lay.z_parities]
    for x in range(lay.bx):
        tiles = [p[x, t] for t in range(lay.zt)]
        for message in z_messages:
            store_packed(message, x, tiles, lay, lay.cy)
    for message, right in zip(z_messages, sides):
        start = jnp.where(right, lay.bx - REACH, 0)
        for lead, ref in ((0, q), (1, s)):
            for x in range(REACH):
                tiles = [ref[start + x, t] for t in range(lay.zt)]
                store_packed(message, lay.bx + lead * REACH + x, tiles, lay, lay.cy)
    highs = [lay.y_side(py)[0] for py in lay.y_parities]
    for message, high in zip(y_messages, highs):
        for lead, ref in enumerate((p, q, s)):
            write_y_message(message, lead, ref, lay, high)
    corners = [(right, high) for right in sides for high in highs]
    for message, (right, high) in zip(d_messages, corners):
        write_d_message(message, p, lay, right, high)


def planes_kernel(lay, gathered, planes, total):
    gx, column, core = lay.place()
    start_x, start_y = gx * lay.bx - REACH, column * lay.cy - REACH
    cells = lay.ex * lay.ey
    padded = gathered.shape[1]
    total[...] = jnp.zeros_like(total)

    def add(index, carry):
        values = gathered[index]
        x = values[lay.steps : lay.steps + 1, :].astype(jnp.int32) - start_x
        y = values[lay.steps + 1 : lay.steps + 2, :].astype(jnp.int32) - start_y
        inside = (x >= 0) & (x < lay.ex) & (y >= 0) & (y < lay.ey)
        cell = jnp.where(inside, x * lay.ey + y, -1)
        ids = lax.broadcasted_iota(jnp.int32, (cells, LANES), 0)
        chosen = jnp.where(ids == cell, 1.0, 0.0).astype(jnp.bfloat16)
        high = values.astype(jnp.bfloat16)
        rest = values - high.astype(jnp.float32)
        middle = rest.astype(jnp.bfloat16)
        low = (rest - middle.astype(jnp.float32)).astype(jnp.bfloat16)
        fill = jnp.zeros((LANES - 3 * padded, LANES), jnp.bfloat16)
        parts = jnp.concatenate([high, middle, low, fill], 0)
        total[...] += lax.dot_general(
            chosen, parts, (((1,), (1,)), ((), ())), preferred_element_type=jnp.float32
        )
        return carry

    lax.fori_loop(0, gathered.shape[0], add, 0)
    summed = total[...]
    summed = (
        summed + pltpu.roll(summed, LANES - padded, 1) + pltpu.roll(summed, LANES - 2 * padded, 1)
    )
    summed = jnp.where(core == 1, summed, 0.0)
    planes[...] = summed.reshape(lay.ex, lay.ey, LANES)


def advance(lay, field, x, y, rows, before, speed, injected):
    lane = lane_ids(rows)
    centre = [field[x, t, y : y + rows, :] for t in range(lay.zt)]
    sums = []
    for k in range(1, REACH + 1):
        left = [pltpu.roll(c, k, 1) for c in centre]
        right = [pltpu.roll(c, LANES - k, 1) for c in centre]
        per_tile = []
        for t in range(lay.zt):
            lower = jnp.where(lane < k, left[t - 1], left[t])
            upper = jnp.where(lane < LANES - k, right[t], right[(t + 1) % lay.zt])
            around = field[x - k, t, y : y + rows, :] + field[x + k, t, y : y + rows, :]
            around += field[x, t, y - k : y - k + rows, :] + field[x, t, y + k : y + k + rows, :]
            per_tile.append(around + (lower + upper))
        sums.append(per_tile)
    out = []
    for t in range(lay.zt):
        drive = 3.0 * STENCIL_COEFFS[0] * centre[t]
        for k in range(REACH):
            drive += STENCIL_COEFFS[k + 1] * sums[k][t]
        if t == 0:
            drive += injected
        out.append(2.0 * centre[t] - before[t] + speed[t] * drive)
    return out


def round_kernel(lay, time, first, last, *refs):
    nz, ny = len(lay.z_parities), len(lay.y_parities)
    (wavelet, where, p, q, s, planes), refs = refs[:6], refs[6:]
    z_in, refs = refs[:nz], refs[nz:]
    y_in, refs = refs[:ny], refs[ny:]
    d_in, refs = refs[: nz * ny], refs[nz * ny :]
    (middle, latest), refs = refs[:2], refs[2:]
    if last:
        q_out, buffer = refs[:2]
    else:
        (q_out, z_out), refs = refs[:2], refs[2:]
        y_out, refs = refs[:ny], refs[ny:]
        d_out, refs = refs[: nz * ny], refs[nz * ny :]
        if first:
            s_out, q_ext, buffer = refs
        else:
            (buffer,) = refs
    z_sides = [lay.z_side(pz) for pz in lay.z_parities]
    y_sides = [lay.y_side(py) for py in lay.y_parities]
    bx, cy, zt = lay.bx, lay.cy, lay.zt
    own_x, own_y = HALO, HALO

    buffer[own_x : own_x + bx, :, own_y : own_y + cy, :] = p[...]
    for is_right, start in ((False, 0), (True, own_x + bx)):
        wants = [v & (r if is_right else ~r) for r, v in z_sides]
        for x in range(HALO):
            row = x if is_right else bx - HALO + x
            block = sum((jnp.where(w, m[row], 0.0) for w, m in zip(wants, z_in)), jnp.zeros((lay.zrows, LANES), jnp.float32))
            for t, tile in enumerate(unpack(block, lay, cy)):
                buffer[start + x, t, own_y : own_y + cy, :] = tile
    for is_high, start in ((False, 0), (True, own_y + cy)):
        wants = [v & (h if is_high else ~h) for h, v in y_sides]
        for x in range(bx):
            for t in range(zt):
                rows = slice(t * ROWS, (t + 1) * ROWS)
                buffer[own_x + x, t, start : start + ROWS, :] = sum(
                    (jnp.where(w, m[x, rows, :], 0.0) for w, m in zip(wants, y_in)),
                    jnp.zeros((ROWS, LANES), jnp.float32),
                )
        for is_right, x_start in ((False, own_x - REACH), (True, own_x + bx)):
            corner = [
                v & u & (r if is_right else ~r) & (h if is_high else ~h)
                for r, v in z_sides
                for h, u in y_sides
            ]
            for x in range(REACH):
                for t in range(zt):
                    rows = slice(t * ROWS, (t + 1) * ROWS)
                    buffer[x_start + x, t, start : start + ROWS, :] = sum(
                        (jnp.where(w, m[x, rows, :], 0.0) for w, m in zip(corner, d_in)),
                        jnp.zeros((ROWS, LANES), jnp.float32),
                    )

    if first:
        for lead, own, ext in ((0, q, q_ext), (1, s, s_out)):
            ext[...] = jnp.zeros_like(ext)
            for x in range(bx):
                for t in range(zt):
                    ext[REACH + x, t, REACH : REACH + cy, :] = own[x, t]
            for is_right, start in ((False, 0), (True, REACH + bx)):
                wants = [v & (r if is_right else ~r) for r, v in z_sides]
                for x in range(REACH):
                    row = bx + lead * REACH + x
                    block = sum((jnp.where(w, m[row], 0.0) for w, m in zip(wants, z_in)), jnp.zeros((lay.zrows, LANES), jnp.float32))
                    for t, tile in enumerate(unpack(block, lay, cy)):
                        ext[start + x, t, REACH : REACH + cy, :] = tile
            for is_high, start, cut in ((False, 0, ROWS - REACH), (True, REACH + cy, 0)):
                wants = [v & (h if is_high else ~h) for h, v in y_sides]
                for x in range(bx):
                    for t in range(zt):
                        rows = slice(t * ROWS + cut, t * ROWS + cut + REACH)
                        ext[REACH + x, t, start : start + REACH, :] = sum(
                            (jnp.where(w, m[(lead + 1) * bx + x, rows, :], 0.0) for w, m in zip(wants, y_in)),
                            jnp.zeros((REACH, LANES), jnp.float32),
                        )
        q, s = q_ext, s_out

    def injected(x, rows, y, back):
        values = pltpu.roll(planes[x], LANES - back, 1) if back else planes[x]
        return jnp.where(lane_ids(lay.ey) == 0, values, 0.0)[y : y + rows]

    def add_source(target, speed_rows, x, y, count_x, count_y, amount):
        @pl.when((x >= 0) & (x < count_x) & (y >= 0) & (y < count_y))
        def _():
            depth = where[2]
            tile, lane = depth // LANES, depth % LANES
            shape = (count_y, LANES)
            here = (lax.broadcasted_iota(jnp.int32, shape, 0) == y) & (
                lax.broadcasted_iota(jnp.int32, shape, 1) == lane
            )
            target[x, tile] += jnp.where(here, speed_rows(x, tile) * amount, 0.0)

    def step_one(x, carry):
        out = advance(
            lay, buffer, x + REACH, REACH, lay.ey,
            [q[x, t] for t in range(zt)], [s[x, t] for t in range(zt)],
            injected(x, lay.ey, 0, lay.steps - 1 - time),
        )
        for t in range(zt):
            q_out[x, t] = out[t]
        return carry

    lax.fori_loop(0, lay.ex, step_one, 0)
    add_source(q_out, lambda x, t: s[x, t], where[0] + REACH, where[1] + REACH, lay.ex, lay.ey, wavelet[time])

    def step_two(x, carry):
        out = advance(
            lay, q_out, x + REACH, REACH, cy,
            [p[x, t] for t in range(zt)],
            [s[x + REACH, t, REACH : REACH + cy, :] for t in range(zt)],
            injected(x + REACH, cy, REACH, lay.steps - 2 - time),
        )
        for t in range(zt):
            latest[x, t] = out[t]
            middle[x, t] = q_out[x + REACH, t, REACH : REACH + cy, :]
        return carry

    lax.fori_loop(0, bx, step_two, 0)
    add_source(
        latest, lambda x, t: s[x + REACH, t, REACH : REACH + cy, :], where[0], where[1], bx, cy, wavelet[time + 1]
    )

    if not last:
        for x in range(bx):
            store_packed(z_out, x, [latest[x, t] for t in range(zt)], lay, cy)
        for message, (high, _) in zip(y_out, y_sides):
            write_y_message(message, 0, latest, lay, high)
        corners = [(right, high) for right, _ in z_sides for high, _ in y_sides]
        for message, (right, high) in zip(d_out, corners):
            write_d_message(message, latest, lay, right, high)


def collect_kernel(lay, times, *refs):
    fields, own, theirs = refs[: lay.steps], refs[lay.steps], refs[lay.steps + 1]
    _, _, core = lay.place()

    def put(index, field):
        for x in range(lay.bx):
            for t in range(lay.zt):
                low, high = field[x, t, 0 : lay.by, :], field[x, t, lay.by : lay.cy, :]
                own[index, x, t] = jnp.where(core == 0, low, high)
                theirs[index, x, t] = jnp.where(core == 0, high, low)

    put(0, fields[lay.steps - 2])
    put(1, fields[lay.steps - 1])
    for slot in range(lay.slots - 1):
        for time in range(lay.steps):
            pl.when(times[slot] == time)(functools.partial(put, 2 + slot, fields[time]))


def finish_kernel(lay, own, theirs, stored, image_before, *outs):
    src_prev, src_now, rec_prev, rec_now, snapshots, image = outs
    _, _, core = lay.place()
    first = core == 0
    for x in range(lay.bx):
        for t in range(lay.zt):
            width = LANES if t + 1 < lay.zt else lay.rest
            lanes = slice(t * LANES, t * LANES + width)
            source = [jnp.where(first, own[i, x, t], theirs[i, x, t])[:, :width] for i in range(lay.slots + 1)]
            receiver = [jnp.where(first, theirs[i, x, t], own[i, x, t])[:, :width] for i in range(lay.slots + 1)]
            src_prev[x, :, lanes], src_now[x, :, lanes] = source[0], source[1]
            rec_prev[x, :, lanes], rec_now[x, :, lanes] = receiver[0], receiver[1]
            total = image_before[x, :, lanes]
            for slot in range(lay.slots):
                kept = source[1] if slot == lay.slots - 1 else source[2 + slot]
                snapshots[slot, x, :, lanes] = kept.astype(jnp.bfloat16)
                crossed = receiver[1] if slot == 0 else receiver[1 + lay.slots - slot]
                total += stored[slot, x, :, lanes].astype(jnp.float32) * crossed
            image[x, :, lanes] = total


def call(kernel, outs, operands, scratch=(), scalars=0):
    in_specs = [pl.BlockSpec(memory_space=pltpu.SMEM)] * scalars
    in_specs += [pl.BlockSpec(memory_space=pltpu.VMEM)] * (len(operands) - scalars)
    return pl.pallas_call(
        kernel,
        out_shape=[jax.ShapeDtypeStruct(shape, dtype) for shape, dtype in outs],
        in_specs=in_specs,
        out_specs=[pl.BlockSpec(memory_space=pltpu.VMEM)] * len(outs),
        scratch_shapes=list(scratch),
        compiler_params=pltpu.CompilerParams(vmem_limit_bytes=16 * 1024 * 1024),
    )(*operands)


def gather_traces(lay, traces, receiver_cells):
    grid_y = lay.by * lay.ny
    cells = receiver_cells
    rows = [traces, (cells // grid_y).astype(jnp.float32), (cells % grid_y).astype(jnp.float32)]
    padded = pl.cdiv(lay.steps + 2, 2 * ROWS) * 2 * ROWS
    rows.append(jnp.zeros((padded - lay.steps - 2, traces.shape[1]), jnp.float32))
    message = jnp.concatenate(rows, 0)
    other = lax.ppermute(message, AXES, lay.core_permutation())
    message = jnp.concatenate([message, other], 1)[None]
    if message.shape[2] != LANES:
        spare = -message.shape[2] % LANES
        fill = jnp.full((1, padded, spare), -1e6, jnp.float32)
        message = jnp.concatenate([message, fill], 2)
        message = message.reshape(padded, -1, LANES).transpose(1, 0, 2)
    for count, move in (
        (lay.columns, lambda x, c, bit: (x, c ^ bit)),
        (lay.nx, lambda x, c, bit: (x ^ bit, c)),
    ):
        assert count & (count - 1) == 0
        bit = 1
        while bit < count:
            pairs = lay.permutation(functools.partial(move, bit=bit))
            message = jnp.concatenate([message, lax.ppermute(message, AXES, pairs)], 0)
            bit *= 2
    return message


def body(
    mesh,
    source_prev,
    source_now,
    receiver_prev,
    receiver_now,
    speed_squared,
    wavelet,
    source_cell,
    traces,
    receiver_cells,
    plan,
    stored_snapshots,
    image_before,
):
    steps, slots = wavelet.shape[0], plan.shape[0]
    lay = Layout(mesh, *source_now.shape, steps, slots)
    f32 = jnp.float32
    gx, gy = lax.axis_index("gx"), lax.axis_index("gy")
    column, core = gy // 2, gy % 2
    first = core == 0
    nz, ny = len(lay.z_parities), len(lay.y_parities)

    swapped = jnp.stack(
        [
            jnp.where(first, receiver_now, source_now),
            jnp.where(first, receiver_prev, source_prev),
            speed_squared,
        ]
    )
    swapped = lax.ppermute(swapped, AXES, lay.core_permutation())
    gathered = gather_traces(lay, traces, receiver_cells)

    grid_y = lay.by * lay.ny
    cell = source_cell[0]
    where = jnp.stack(
        [
            cell // (grid_y * lay.depth) - gx * lay.bx,
            cell // lay.depth % grid_y - column * lay.cy,
            cell % lay.depth,
        ]
    ).astype(jnp.int32)
    amounts = jnp.where(first, wavelet, 0.0)
    times = jnp.where(first, plan[:-1], (steps - 1 - plan[1:])[::-1])

    block = (lay.bx, lay.zt, lay.cy, LANES)
    ext = (lay.ex, lay.zt, lay.ey, LANES)
    field = (lay.bx + 2 * HALO, lay.zt, lay.cy + 2 * HALO, LANES)
    y_rows = lay.zt * ROWS
    z_shape = (lay.bx, lay.zrows, LANES)
    y_shape = (lay.bx, y_rows, LANES)
    d_shape = (REACH, y_rows, LANES)

    outs = [(block, f32)] * 3 + [((lay.bx + 2 * REACH, lay.zrows, LANES), f32)] * nz
    outs += [((3 * lay.bx, y_rows, LANES), f32)] * ny + [(d_shape, f32)] * (nz * ny)
    made = call(
        functools.partial(prepare_kernel, lay),
        outs,
        [source_now, source_prev, receiver_now, receiver_prev, speed_squared, swapped],
    )
    (p, q, s), made = made[:3], made[3:]
    z_out, y_out, d_out = made[:nz], made[nz : nz + ny], made[nz + ny :]
    (planes,) = call(
        functools.partial(planes_kernel, lay),
        [((lay.ex, lay.ey, LANES), f32)],
        [gathered],
        [pltpu.VMEM((lay.ex * lay.ey, LANES), f32)],
    )

    fields = []
    for time in range(0, steps, 2):
        begin, end = time == 0, time + 2 == steps
        z_in = [lax.ppermute(m, AXES, lay.z_permutation(pz)) for m, pz in zip(z_out, lay.z_parities)]
        y_in = [lax.ppermute(m, AXES, lay.y_permutation(py)) for m, py in zip(y_out, lay.y_parities)]
        diagonals = [lay.d_permutation(pz, py) for pz in lay.z_parities for py in lay.y_parities]
        d_in = [lax.ppermute(m, AXES, pairs) for m, pairs in zip(d_out, diagonals)]
        outs, scratch = [(block, f32)] * 2, []
        if end:
            scratch.append(pltpu.VMEM(ext, f32))
        else:
            outs += [(ext, f32), (z_shape, f32)] + [(y_shape, f32)] * ny + [(d_shape, f32)] * (nz * ny)
            if begin:
                outs.append((ext, f32))
                scratch.append(pltpu.VMEM(ext, f32))
        scratch.append(pltpu.VMEM(field, f32))
        made = call(
            functools.partial(round_kernel, lay, time, begin, end),
            outs,
            [amounts, where, p, q, s, planes, *z_in, *y_in, *d_in],
            scratch,
            scalars=2,
        )
        fields += made[:2]
        if not end:
            p, q, z_out = made[1], made[2], [made[3]] * nz
            y_out, d_out = made[4 : 4 + ny], made[4 + ny : 4 + ny + nz * ny]
            if begin:
                s = made[-1]

    kept = (slots + 1, lay.bx, lay.zt, lay.by, LANES)
    own, theirs = call(
        functools.partial(collect_kernel, lay), [(kept, f32)] * 2, [times, *fields], scalars=1
    )
    theirs = lax.ppermute(theirs, AXES, lay.core_permutation())
    shape = source_now.shape
    return tuple(
        call(
            functools.partial(finish_kernel, lay),
            [(shape, f32)] * 4 + [(stored_snapshots.shape, jnp.bfloat16), (shape, f32)],
            [own, theirs, stored_snapshots, image_before],
        )
    )


def solution(mesh):
    block = P(("shot", "gx"), "gy", None)
    line = P("shot", ("gx", "gy"))
    volume = P("shot", "gx", "gy", None)
    return jax.shard_map(
        functools.partial(body, mesh),
        mesh=mesh,
        in_specs=(block,) * 5 + (P("shot"), P("shot"), line, line, P("shot"), volume, block),
        out_specs=(block,) * 4 + (volume, block),
        check_vma=False,
    )
```

time: 256 us -> 90.8 us (0.35)
  the two profiles are of different devices: /device:TPU:18 before, /device:TPU:0 now
where the time goes in v1:
time: 90.8 us; the launch traced here: 90.6 us
  starting transfers between devices  36.2 us (40%)
  Pallas kernels  25.6 us (28%)
  waiting for transfers between devices  24.9 us (27%)
  other arithmetic  1.88 us (2%)
  between operations  1.64 us (2%)
    pallas_call x9, Pallas kernels, call(): pl.pallas_call(kernel, out_shape=[jax.ShapeDtypeStruct(shape, dtype) for...  25.6 us
    ppermute x10, starting transfers between devices, body(): lax.ppermute(m, AXES, lay.z_permutation(pz))  18.7 us
    ppermute x10, waiting for transfers between devices, body(): d_in = [lax.ppermute(m, AXES, pairs) for m, pairs in zip(d_out, diagonals)]  15.5 us
    ppermute x3, starting transfers between devices, gather_traces(): message = jnp.concatenate([message, lax.ppermute(message, AXES, pairs)], 0)  7.81 us
    ppermute x3, waiting for transfers between devices, gather_traces(): message = jnp.concatenate([message, lax.ppermute(message, AXES, pairs)], 0)  6.91 us
    ppermute x10, starting transfers between devices, body(): d_in = [lax.ppermute(m, AXES, pairs) for m, pairs in zip(d_out, diagonals)]  4.53 us
    ppermute x5, starting transfers between devices, body(): lax.ppermute(m, AXES, lay.y_permutation(py))  4.48 us
    ppermute x1, waiting for transfers between devices, body(): theirs = lax.ppermute(theirs, AXES, lay.core_permutation())  1.85 us
  transfers between devices with their start and end apart: 31, of which 8 were waited for; matrix products, arithmetic and copies ran while one was open for 1% of the time, Pallas kernels for 2%

profile of v1, /device:TPU:0, one launch (start us, length us, event | category | flops | bytes accessed | tf_op | source)
XLA Modules:
  0.0 90.6 jit_solution(15506441928991902062)
XLA Ops:
  0.6 0.7 fusion.1
  1.9 1.0 %select_bitcast_fusion = (f32[1,8,8,320]{3,2,1,0:T(8,128)S(1)}, f32[1,8,8,320]{3,2,1,0:T(8,128)S(1)}) fusion(f32[8,8,320]{2,1,0:T(8,128)} %refs_3_.1, f32[8,8,320]{2,1,0:T(8,128)} %refs_1_.1, pred[]{:T(512)S(6)} %eq.9, f32[8,8,320]{2,1,0:T(8,128)} %refs_2_.1, f32[8,8,320]{2,1,0:T(8,128)} %refs_0_.1), kind=kLoop, calls=%fused_computation.1 | loop fusion | flops 40960 | bytes 491521 | tf_op jit(solution)/shard_map/stack | solution.py:463
  3.0 2.7 %collective-permute-start.2 = (f32[1,16,128]{2,1,0:T(8,128)S(1)}, f32[1,16,128]{2,1,0:T(8,128)S(1)}, u32[]{:S(2)}, u32[]{:S(2)}) collective-permute-start(f32[1,16,128]{2,1,0:T(8,128)S(1)} %maximum_bitcast_fusion), channel_id=1, source_target_pairs={{0,2},{1,3},{2,0},{3,1},{4,6},{5,7},{6,4},{7,5},{8,10},{9,11},{10,... | collective-permute-start | bytes 24584 | tf_op jit(solution)/shard_map/ppermute | solution.py:435
  5.8 1.4 %collective-permute-done.2 = f32[1,16,128]{2,1,0:T(8,128)S(1)} collective-permute-done((f32[1,16,128]{2,1,0:T(8,128)S(1)}, f32[1,16,128]{2,1,0:T(8,128)S(1)}, u32[]{:S(2)}, u32[]{:S(2)}) %collective-permute-start.2) | collective-permute-done | bytes 8224 | tf_op jit(solution)/shard_map/ppermute | solution.py:435
  7.2 2.1 %collective-permute-start.3 = (f32[2,16,128]{2,1,0:T(8,128)S(1)}, f32[2,16,128]{2,1,0:T(8,128)S(1)}, u32[]{:S(2)}, u32[]{:S(2)}) collective-permute-start(f32[2,16,128]{2,1,0:T(8,128)S(1)} %pad_maximum_fusion.3), channel_id=1, source_target_pairs={{0,4},{1,5},{2,6},{3,7},{4,0},{5,1},{6,2},{7,3},{8,12},{9,13},{10,... | collective-permute-start | bytes 49160 | tf_op jit(solution)/shard_map/ppermute | solution.py:435
  10.3 1.6 %collective-permute-start.7 = (f32[24,24,128]{2,1,0:T(8,128)S(1)}, f32[24,24,128]{2,1,0:T(8,128)S(1)}, u32[]{:S(2)}, u32[]{:S(2)}) collective-permute-start(f32[24,24,128]{2,1,0:T(8,128)S(1)} %get-tuple-element.52), channel_id=1, source_target_pairs={{0,2},{1,3},{2,0},{3,1},{4,6},{5,7},{6,4},{7,5},{8,10},{9,11},{10,... | collective-permute-start | bytes 884744 | tf_op jit(solution)/shard_map/ppermute | solution.py:513
  12.3 3.0 %collective-permute-start.4 = (f32[4,16,128]{2,1,0:T(8,128)S(1)}, f32[4,16,128]{2,1,0:T(8,128)S(1)}, u32[]{:S(2)}, u32[]{:S(2)}) collective-permute-start(f32[4,16,128]{2,1,0:T(8,128)S(1)} %pad_maximum_fusion.2), channel_id=1, source_target_pairs={{0,8},{1,9},{2,10},{3,11},{4,12},{5,13},{6,14},{7,15},{8,0},{9,1},... | collective-permute-start | bytes 98312 | tf_op jit(solution)/shard_map/ppermute | solution.py:435
  15.4 1.4 %collective-permute-start.8 = (f32[4,24,128]{2,1,0:T(8,128)S(1)}, f32[4,24,128]{2,1,0:T(8,128)S(1)}, u32[]{:S(2)}, u32[]{:S(2)}) collective-permute-start(f32[4,24,128]{2,1,0:T(8,128)S(1)} %get-tuple-element.53), channel_id=1, source_target_pairs={{0,6},{1,7},{2,4},{3,5},{4,2},{5,3},{6,0},{7,1},{8,14},{9,15},{10,... | collective-permute-start | bytes 147464 | tf_op jit(solution)/shard_map/ppermute | solution.py:515
  16.9 5.5 %collective-permute-done.4 = f32[4,16,128]{2,1,0:T(8,128)S(1)} collective-permute-done((f32[4,16,128]{2,1,0:T(8,128)S(1)}, f32[4,16,128]{2,1,0:T(8,128)S(1)}, u32[]{:S(2)}, u32[]{:S(2)}) %collective-permute-start.4) | collective-permute-done | bytes 32800 | tf_op jit(solution)/shard_map/ppermute | solution.py:435
  22.4 1.5 %shard_map.164.refs_5_ = f32[16,24,128]{2,1,0:T(8,128)S(1)} custom-call(f32[8,16,128]{2,1,0:T(8,128)S(1)} %pad_maximum_fusion.1.gathered), custom_call_target="tpu_custom_call" | custom-call | tf_op jit(solution)/shard_map/pallas_call | solution.py:403
  23.9 4.6 %shard_map.165 = (f32[8,3,16,128]{3,2,1,0:T(8,128)S(1)}, f32[8,3,16,128]{3,2,1,0:T(8,128)S(1)}, f32[16,3,24,128]{3,2,1,0:T(8,128)S(1)}, f32[8,40,128]{2,1,0:T(8,...) custom-call(f32[10]{0:T(128)S(1)} %broadcast_select_fusion.refs_0_, ...), custom_call_target="tpu_custom_call" | custom-call | tf_op jit(solution)/shard_map/pallas_call | solution.py:403
  28.5 0.6 collective-permute-start.11
  29.1 4.7 %collective-permute-start.10 = (f32[8,40,128]{2,1,0:T(8,128)S(1)}, f32[8,40,128]{2,1,0:T(8,128)S(1)}, u32[]{:S(2)}, u32[]{:S(2)}) collective-permute-start(f32[8,40,128]{2,1,0:T(8,128)S(1)} %get-tuple-element.59), channel_id=1, source_target_pairs={{0,4},{1,5},{2,6},{3,7},{4,0},{5,1},{6,2},{7,3},{8,12},{9,13},{10,... | collective-permute-start | bytes 491528 | tf_op jit(solution)/shard_map/ppermute | solution.py:512
  34.3 1.1 %collective-permute-start.13 = (f32[4,24,128]{2,1,0:T(8,128)S(1)}, f32[4,24,128]{2,1,0:T(8,128)S(1)}, u32[]{:S(2)}, u32[]{:S(2)}) collective-permute-start(f32[4,24,128]{2,1,0:T(8,128)S(1)} %get-tuple-element.61), channel_id=1, source_target_pairs={{0,6},{1,7},{2,4},{3,5},{4,2},{5,3},{6,0},{7,1},{8,14},{9,15},{10,... | collective-permute-start | bytes 147464 | tf_op jit(solution)/shard_map/ppermute | solution.py:515
  35.4 3.9 %collective-permute-done.13.refs_9_ = f32[4,24,128]{2,1,0:T(8,128)S(1)} collective-permute-done((f32[4,24,128]{2,1,0:T(8,128)S(1)}, f32[4,24,128]{2,1,0:T(8,128)S(1)}, u32[]{:S(2)}, u32[]{:S(2)}) %collective-permute-start.13) | collective-permute-done | bytes 49184 | tf_op jit(solution)/shard_map/ppermute | solution.py:515
  39.3 4.4 %shard_map.166 = (f32[8,3,16,128]{3,2,1,0:T(8,128)S(1)}, f32[8,3,16,128]{3,2,1,0:T(8,128)S(1)}, f32[16,3,24,128]{3,2,1,0:T(8,128)S(1)}, f32[8,40,128]{2,1,0:T(8,...) custom-call(f32[10]{0:T(128)S(1)} %broadcast_select_fusion.refs_0_, ...), custom_call_target="tpu_custom_call" | custom-call | tf_op jit(solution)/shard_map/pallas_call | solution.py:403
  43.8 4.9 %collective-permute-start.15 = (f32[8,40,128]{2,1,0:T(8,128)S(1)}, f32[8,40,128]{2,1,0:T(8,128)S(1)}, u32[]{:S(2)}, u32[]{:S(2)}) collective-permute-start(f32[8,40,128]{2,1,0:T(8,128)S(1)} %get-tuple-element.66), channel_id=1, source_target_pairs={{0,4},{1,5},{2,6},{3,7},{4,0},{5,1},{6,2},{7,3},{8,12},{9,13},{10,... | collective-permute-start | bytes 491528 | tf_op jit(solution)/shard_map/ppermute | solution.py:512
  49.2 1.0 %collective-permute-start.18 = (f32[4,24,128]{2,1,0:T(8,128)S(1)}, f32[4,24,128]{2,1,0:T(8,128)S(1)}, u32[]{:S(2)}, u32[]{:S(2)}) collective-permute-start(f32[4,24,128]{2,1,0:T(8,128)S(1)} %get-tuple-element.68), channel_id=1, source_target_pairs={{0,6},{1,7},{2,4},{3,5},{4,2},{5,3},{6,0},{7,1},{8,14},{9,15},{10,... | collective-permute-start | bytes 147464 | tf_op jit(solution)/shard_map/ppermute | solution.py:515
  50.2 4.0 %collective-permute-done.18.refs_9_ = f32[4,24,128]{2,1,0:T(8,128)S(1)} collective-permute-done((f32[4,24,128]{2,1,0:T(8,128)S(1)}, f32[4,24,128]{2,1,0:T(8,128)S(1)}, u32[]{:S(2)}, u32[]{:S(2)}) %collective-permute-start.18) | collective-permute-done | bytes 49184 | tf_op jit(solution)/shard_map/ppermute | solution.py:515
  54.2 4.4 %shard_map.167 = (f32[8,3,16,128]{3,2,1,0:T(8,128)S(1)}, f32[8,3,16,128]{3,2,1,0:T(8,128)S(1)}, f32[16,3,24,128]{3,2,1,0:T(8,128)S(1)}, f32[8,40,128]{2,1,0:T(8,...) custom-call(f32[10]{0:T(128)S(1)} %broadcast_select_fusion.refs_0_, ...), custom_call_target="tpu_custom_call" | custom-call | tf_op jit(solution)/shard_map/pallas_call | solution.py:403
  58.8 3.1 %collective-permute-start.20 = (f32[8,40,128]{2,1,0:T(8,128)S(1)}, f32[8,40,128]{2,1,0:T(8,128)S(1)}, u32[]{:S(2)}, u32[]{:S(2)}) collective-permute-start(f32[8,40,128]{2,1,0:T(8,128)S(1)} %get-tuple-element.73), channel_id=1, source_target_pairs={{0,4},{1,5},{2,6},{3,7},{4,0},{5,1},{6,2},{7,3},{8,12},{9,13},{10,... | collective-permute-start | bytes 491528 | tf_op jit(solution)/shard_map/ppermute | solution.py:512
  62.4 1.0 %collective-permute-start.23 = (f32[4,24,128]{2,1,0:T(8,128)S(1)}, f32[4,24,128]{2,1,0:T(8,128)S(1)}, u32[]{:S(2)}, u32[]{:S(2)}) collective-permute-start(f32[4,24,128]{2,1,0:T(8,128)S(1)} %get-tuple-element.75), channel_id=1, source_target_pairs={{0,6},{1,7},{2,4},{3,5},{4,2},{5,3},{6,0},{7,1},{8,14},{9,15},{10,... | collective-permute-start | bytes 147464 | tf_op jit(solution)/shard_map/ppermute | solution.py:515
  63.6 4.0 %collective-permute-done.23.refs_9_ = f32[4,24,128]{2,1,0:T(8,128)S(1)} collective-permute-done((f32[4,24,128]{2,1,0:T(8,128)S(1)}, f32[4,24,128]{2,1,0:T(8,128)S(1)}, u32[]{:S(2)}, u32[]{:S(2)}) %collective-permute-start.23) | collective-permute-done | bytes 49184 | tf_op jit(solution)/shard_map/ppermute | solution.py:515
  67.5 4.4 %shard_map.168 = (f32[8,3,16,128]{3,2,1,0:T(8,128)S(1)}, f32[8,3,16,128]{3,2,1,0:T(8,128)S(1)}, f32[16,3,24,128]{3,2,1,0:T(8,128)S(1)}, f32[8,40,128]{2,1,0:T(8,...) custom-call(f32[10]{0:T(128)S(1)} %broadcast_select_fusion.refs_0_, ...), custom_call_target="tpu_custom_call" | custom-call | tf_op jit(solution)/shard_map/pallas_call | solution.py:403
  72.1 4.7 %collective-permute-start.25 = (f32[8,40,128]{2,1,0:T(8,128)S(1)}, f32[8,40,128]{2,1,0:T(8,128)S(1)}, u32[]{:S(2)}, u32[]{:S(2)}) collective-permute-start(f32[8,40,128]{2,1,0:T(8,128)S(1)} %get-tuple-element.80), channel_id=1, source_target_pairs={{0,4},{1,5},{2,6},{3,7},{4,0},{5,1},{6,2},{7,3},{8,12},{9,13},{10,... | collective-permute-start | bytes 491528 | tf_op jit(solution)/shard_map/ppermute | solution.py:512
  76.8 1.5 %collective-permute-start.27 = (f32[8,24,128]{2,1,0:T(8,128)S(1)}, f32[8,24,128]{2,1,0:T(8,128)S(1)}, u32[]{:S(2)}, u32[]{:S(2)}) collective-permute-start(f32[8,24,128]{2,1,0:T(8,128)S(1)} %get-tuple-element.81), channel_id=1, source_target_pairs={{0,2},{1,3},{2,0},{3,1},{4,6},{5,7},{6,4},{7,5},{8,10},{9,11},{10,... | collective-permute-start | bytes 294920 | tf_op jit(solution)/shard_map/ppermute | solution.py:513
  78.3 3.6 %collective-permute-done.28.refs_9_ = f32[4,24,128]{2,1,0:T(8,128)S(1)} collective-permute-done((f32[4,24,128]{2,1,0:T(8,128)S(1)}, f32[4,24,128]{2,1,0:T(8,128)S(1)}, u32[]{:S(2)}, u32[]{:S(2)}) %collective-permute-start.28) | collective-permute-done | bytes 49184 | tf_op jit(solution)/shard_map/ppermute | solution.py:515
  81.9 0.6 collective-permute-done.27.refs_8_
  82.6 4.3 %shard_map.169 = (f32[8,3,16,128]{3,2,1,0:T(8,128)S(1)}, f32[8,3,16,128]{3,2,1,0:T(8,128)S(1)}) custom-call(f32[10]{0:T(128)S(1)} %broadcast_select_fusion.refs_0_, s32[3]{0:T(128)S(1)} %pad_add_fusion.refs_1_, f32[8,3,16,128]{3,2,1,0:T(8,128)S(1)} %get-tuple-element.78.refs_2_.refs_7_, f32[16,3,24,128]{3,2,1,0:T(8,128)S(1)} %get-tuple-element.79.refs_3_, ...), custom_call_target="tpu_custom_call" | custom-call | tf_op jit(solution)/shard_map/pallas_call | solution.py:403
  86.9 0.8 shard_map.170
  87.8 1.9 %collective-permute-done.30.theirs = f32[5,8,3,8,128]{4,3,2,1,0:T(8,128)S(1)} collective-permute-done((f32[5,8,3,8,128]{4,3,2,1,0:T(8,128)S(1)}, f32[5,8,3,8,128]{4,3,2,1,0:T(8,128)S(1)}, u32[]{:S(2)}, u32[]{:S(2)}) %collective-permute-start.30) | collective-permute-done | bytes 491552 | tf_op jit(solution)/shard_map/ppermute | solution.py:543
  89.7 0.9 shard_map.171
  (73 shorter events, 3.5 us)
Async XLA Ops:
  1.3 1.5 %collective-permute-start.1 = (f32[16,64]{1,0:T(8,128)S(1)}, f32[16,64]{1,0:T(8,128)S(1)}, u32[]{:S(2)}, u32[]{:S(2)}) collective-permute-start(f32[16,64]{1,0:T(8,128)S(1)} %pad_maximum_fusion.4), channel_id=1, source_target_pairs={{0,1},{1,0},{2,3},{3,2},{4,5},{5,4},{6,7},{7,6},{8,9},{9,8},{10,11... | collective-permute-start | bytes 12296 | tf_op jit(solution)/shard_map/ppermute | solution.py:420
  3.0 4.3 %collective-permute-start.2 = (f32[1,16,128]{2,1,0:T(8,128)S(1)}, f32[1,16,128]{2,1,0:T(8,128)S(1)}, u32[]{:S(2)}, u32[]{:S(2)}) collective-permute-start(f32[1,16,128]{2,1,0:T(8,128)S(1)} %maximum_bitcast_fusion), channel_id=1, source_target_pairs={{0,2},{1,3},{2,0},{3,1},{4,6},{5,7},{6,4},{7,5},{8,10},{9,11},{10,... | collective-permute-start | bytes 24584 | tf_op jit(solution)/shard_map/ppermute | solution.py:435
  5.6 4.5 %copy-start.4 = (f32[8,8,320]{2,1,0:T(8,128)S(1)}, f32[8,8,320]{2,1,0:T(8,128)}, u32[]{:S(2)}) copy-start(f32[8,8,320]{2,1,0:T(8,128)} %refs_3_.1) | copy-start | bytes 245764
  5.7 4.4 %collective-permute-start = (f32[3,8,8,320]{3,2,1,0:T(8,128)S(1)}, f32[3,8,8,320]{3,2,1,0:T(8,128)S(1)}, u32[]{:S(2)}, u32[]{:S(2)}) collective-permute-start(f32[3,8,8,320]{3,2,1,0:T(8,128)S(1)} %pad_maximum_fusion), channel_id=1, source_target_pairs={{0,1},{1,0},{2,3},{3,2},{4,5},{5,4},{6,7},{7,6},{8,9},{9,8},{10,11... | collective-permute-start | bytes 737288 | tf_op jit(solution)/shard_map/ppermute | solution.py:470
  7.2 5.1 %collective-permute-start.3 = (f32[2,16,128]{2,1,0:T(8,128)S(1)}, f32[2,16,128]{2,1,0:T(8,128)S(1)}, u32[]{:S(2)}, u32[]{:S(2)}) collective-permute-start(f32[2,16,128]{2,1,0:T(8,128)S(1)} %pad_maximum_fusion.3), channel_id=1, source_target_pairs={{0,4},{1,5},{2,6},{3,7},{4,0},{5,1},{6,2},{7,3},{8,12},{9,13},{10,... | collective-permute-start | bytes 49160 | tf_op jit(solution)/shard_map/ppermute | solution.py:435
  10.3 13.6 %collective-permute-start.7 = (f32[24,24,128]{2,1,0:T(8,128)S(1)}, f32[24,24,128]{2,1,0:T(8,128)S(1)}, u32[]{:S(2)}, u32[]{:S(2)}) collective-permute-start(f32[24,24,128]{2,1,0:T(8,128)S(1)} %get-tuple-element.52), channel_id=1, source_target_pairs={{0,2},{1,3},{2,0},{3,1},{4,6},{5,7},{6,4},{7,5},{8,10},{9,11},{10,... | collective-permute-start | bytes 884744 | tf_op jit(solution)/shard_map/ppermute | solution.py:513
  11.9 12.0 %collective-permute-start.5 = (f32[16,40,128]{2,1,0:T(8,128)S(1)}, f32[16,40,128]{2,1,0:T(8,128)S(1)}, u32[]{:S(2)}, u32[]{:S(2)}) collective-permute-start(f32[16,40,128]{2,1,0:T(8,128)S(1)} %get-tuple-element.50), channel_id=1, source_target_pairs={{0,4},{1,5},{2,6},{3,7},{4,0},{5,1},{6,2},{7,3},{8,12},{9,13},{10,... | collective-permute-start | bytes 983048 | tf_op jit(solution)/shard_map/ppermute | solution.py:512
  12.3 11.6 %collective-permute-start.6 = (f32[16,40,128]{2,1,0:T(8,128)S(1)}, f32[16,40,128]{2,1,0:T(8,128)S(1)}, u32[]{:S(2)}, u32[]{:S(2)}) collective-permute-start(f32[16,40,128]{2,1,0:T(8,128)S(1)} %get-tuple-element.51), channel_id=1, source_target_pairs={{0,1},{1,0},{2,3},{3,2},{4,8},{5,9},{6,10},{7,11},{8,4},{9,5},{10,... | collective-permute-start | bytes 983048 | tf_op jit(solution)/shard_map/ppermute | solution.py:512
  12.3 10.0 %collective-permute-start.4 = (f32[4,16,128]{2,1,0:T(8,128)S(1)}, f32[4,16,128]{2,1,0:T(8,128)S(1)}, u32[]{:S(2)}, u32[]{:S(2)}) collective-permute-start(f32[4,16,128]{2,1,0:T(8,128)S(1)} %pad_maximum_fusion.2), channel_id=1, source_target_pairs={{0,8},{1,9},{2,10},{3,11},{4,12},{5,13},{6,14},{7,15},{8,0},{9,1},... | collective-permute-start | bytes 98312 | tf_op jit(solution)/shard_map/ppermute | solution.py:435
  15.4 8.4 %collective-permute-start.8 = (f32[4,24,128]{2,1,0:T(8,128)S(1)}, f32[4,24,128]{2,1,0:T(8,128)S(1)}, u32[]{:S(2)}, u32[]{:S(2)}) collective-permute-start(f32[4,24,128]{2,1,0:T(8,128)S(1)} %get-tuple-element.53), channel_id=1, source_target_pairs={{0,6},{1,7},{2,4},{3,5},{4,2},{5,3},{6,0},{7,1},{8,14},{9,15},{10,... | collective-permute-start | bytes 147464 | tf_op jit(solution)/shard_map/ppermute | solution.py:515
  22.3 1.5 %collective-permute-start.9 = (f32[4,24,128]{2,1,0:T(8,128)S(1)}, f32[4,24,128]{2,1,0:T(8,128)S(1)}, u32[]{:S(2)}, u32[]{:S(2)}) collective-permute-start(f32[4,24,128]{2,1,0:T(8,128)S(1)} %get-tuple-element.54), channel_id=1, source_target_pairs={{0,1},{1,0},{2,3},{3,2},{4,10},{5,11},{6,8},{7,9},{8,6},{9,7},{10,... | collective-permute-start | bytes 147464 | tf_op jit(solution)/shard_map/ppermute | solution.py:515
  28.5 10.8 %collective-permute-start.11 = (f32[8,40,128]{2,1,0:T(8,128)S(1)}, f32[8,40,128]{2,1,0:T(8,128)S(1)}, u32[]{:S(2)}, u32[]{:S(2)}) collective-permute-start(f32[8,40,128]{2,1,0:T(8,128)S(1)} %get-tuple-element.59), channel_id=1, source_target_pairs={{0,1},{1,0},{2,3},{3,2},{4,8},{5,9},{6,10},{7,11},{8,4},{9,5},{10,... | collective-permute-start | bytes 491528 | tf_op jit(solution)/shard_map/ppermute | solution.py:512
  29.1 10.2 %collective-permute-start.10 = (f32[8,40,128]{2,1,0:T(8,128)S(1)}, f32[8,40,128]{2,1,0:T(8,128)S(1)}, u32[]{:S(2)}, u32[]{:S(2)}) collective-permute-start(f32[8,40,128]{2,1,0:T(8,128)S(1)} %get-tuple-element.59), channel_id=1, source_target_pairs={{0,4},{1,5},{2,6},{3,7},{4,0},{5,1},{6,2},{7,3},{8,12},{9,13},{10,... | collective-permute-start | bytes 491528 | tf_op jit(solution)/shard_map/ppermute | solution.py:512
  33.8 5.5 %collective-permute-start.12 = (f32[8,24,128]{2,1,0:T(8,128)S(1)}, f32[8,24,128]{2,1,0:T(8,128)S(1)}, u32[]{:S(2)}, u32[]{:S(2)}) collective-permute-start(f32[8,24,128]{2,1,0:T(8,128)S(1)} %get-tuple-element.60), channel_id=1, source_target_pairs={{0,2},{1,3},{2,0},{3,1},{4,6},{5,7},{6,4},{7,5},{8,10},{9,11},{10,... | collective-permute-start | bytes 294920 | tf_op jit(solution)/shard_map/ppermute | solution.py:513
  34.3 5.0 %collective-permute-start.13 = (f32[4,24,128]{2,1,0:T(8,128)S(1)}, f32[4,24,128]{2,1,0:T(8,128)S(1)}, u32[]{:S(2)}, u32[]{:S(2)}) collective-permute-start(f32[4,24,128]{2,1,0:T(8,128)S(1)} %get-tuple-element.61), channel_id=1, source_target_pairs={{0,6},{1,7},{2,4},{3,5},{4,2},{5,3},{6,0},{7,1},{8,14},{9,15},{10,... | collective-permute-start | bytes 147464 | tf_op jit(solution)/shard_map/ppermute | solution.py:515
  35.4 3.9 %collective-permute-start.14 = (f32[4,24,128]{2,1,0:T(8,128)S(1)}, f32[4,24,128]{2,1,0:T(8,128)S(1)}, u32[]{:S(2)}, u32[]{:S(2)}) collective-permute-start(f32[4,24,128]{2,1,0:T(8,128)S(1)} %get-tuple-element.62), channel_id=1, source_target_pairs={{0,1},{1,0},{2,3},{3,2},{4,10},{5,11},{6,8},{7,9},{8,6},{9,7},{10,... | collective-permute-start | bytes 147464 | tf_op jit(solution)/shard_map/ppermute | solution.py:515
  43.8 10.5 %collective-permute-start.16 = (f32[8,40,128]{2,1,0:T(8,128)S(1)}, f32[8,40,128]{2,1,0:T(8,128)S(1)}, u32[]{:S(2)}, u32[]{:S(2)}) collective-permute-start(f32[8,40,128]{2,1,0:T(8,128)S(1)} %get-tuple-element.66), channel_id=1, source_target_pairs={{0,1},{1,0},{2,3},{3,2},{4,8},{5,9},{6,10},{7,11},{8,4},{9,5},{10,... | collective-permute-start | bytes 491528 | tf_op jit(solution)/shard_map/ppermute | solution.py:512
  43.8 10.4 %collective-permute-start.15 = (f32[8,40,128]{2,1,0:T(8,128)S(1)}, f32[8,40,128]{2,1,0:T(8,128)S(1)}, u32[]{:S(2)}, u32[]{:S(2)}) collective-permute-start(f32[8,40,128]{2,1,0:T(8,128)S(1)} %get-tuple-element.66), channel_id=1, source_target_pairs={{0,4},{1,5},{2,6},{3,7},{4,0},{5,1},{6,2},{7,3},{8,12},{9,13},{10,... | collective-permute-start | bytes 491528 | tf_op jit(solution)/shard_map/ppermute | solution.py:512
  48.8 5.5 %collective-permute-start.17 = (f32[8,24,128]{2,1,0:T(8,128)S(1)}, f32[8,24,128]{2,1,0:T(8,128)S(1)}, u32[]{:S(2)}, u32[]{:S(2)}) collective-permute-start(f32[8,24,128]{2,1,0:T(8,128)S(1)} %get-tuple-element.67), channel_id=1, source_target_pairs={{0,2},{1,3},{2,0},{3,1},{4,6},{5,7},{6,4},{7,5},{8,10},{9,11},{10,... | collective-permute-start | bytes 294920 | tf_op jit(solution)/shard_map/ppermute | solution.py:513
  49.2 5.0 %collective-permute-start.18 = (f32[4,24,128]{2,1,0:T(8,128)S(1)}, f32[4,24,128]{2,1,0:T(8,128)S(1)}, u32[]{:S(2)}, u32[]{:S(2)}) collective-permute-start(f32[4,24,128]{2,1,0:T(8,128)S(1)} %get-tuple-element.68), channel_id=1, source_target_pairs={{0,6},{1,7},{2,4},{3,5},{4,2},{5,3},{6,0},{7,1},{8,14},{9,15},{10,... | collective-permute-start | bytes 147464 | tf_op jit(solution)/shard_map/ppermute | solution.py:515
  50.2 4.0 %collective-permute-start.19 = (f32[4,24,128]{2,1,0:T(8,128)S(1)}, f32[4,24,128]{2,1,0:T(8,128)S(1)}, u32[]{:S(2)}, u32[]{:S(2)}) collective-permute-start(f32[4,24,128]{2,1,0:T(8,128)S(1)} %get-tuple-element.69), channel_id=1, source_target_pairs={{0,1},{1,0},{2,3},{3,2},{4,10},{5,11},{6,8},{7,9},{8,6},{9,7},{10,... | collective-permute-start | bytes 147464 | tf_op jit(solution)/shard_map/ppermute | solution.py:515
  58.7 8.8 %collective-permute-start.21 = (f32[8,40,128]{2,1,0:T(8,128)S(1)}, f32[8,40,128]{2,1,0:T(8,128)S(1)}, u32[]{:S(2)}, u32[]{:S(2)}) collective-permute-start(f32[8,40,128]{2,1,0:T(8,128)S(1)} %get-tuple-element.73), channel_id=1, source_target_pairs={{0,1},{1,0},{2,3},{3,2},{4,8},{5,9},{6,10},{7,11},{8,4},{9,5},{10,... | collective-permute-start | bytes 491528 | tf_op jit(solution)/shard_map/ppermute | solution.py:512
  58.8 8.8 %collective-permute-start.20 = (f32[8,40,128]{2,1,0:T(8,128)S(1)}, f32[8,40,128]{2,1,0:T(8,128)S(1)}, u32[]{:S(2)}, u32[]{:S(2)}) collective-permute-start(f32[8,40,128]{2,1,0:T(8,128)S(1)} %get-tuple-element.73), channel_id=1, source_target_pairs={{0,4},{1,5},{2,6},{3,7},{4,0},{5,1},{6,2},{7,3},{8,12},{9,13},{10,... | collective-permute-start | bytes 491528 | tf_op jit(solution)/shard_map/ppermute | solution.py:512
  61.9 5.7 %collective-permute-start.22 = (f32[8,24,128]{2,1,0:T(8,128)S(1)}, f32[8,24,128]{2,1,0:T(8,128)S(1)}, u32[]{:S(2)}, u32[]{:S(2)}) collective-permute-start(f32[8,24,128]{2,1,0:T(8,128)S(1)} %get-tuple-element.74), channel_id=1, source_target_pairs={{0,2},{1,3},{2,0},{3,1},{4,6},{5,7},{6,4},{7,5},{8,10},{9,11},{10,... | collective-permute-start | bytes 294920 | tf_op jit(solution)/shard_map/ppermute | solution.py:513
  62.4 5.2 %collective-permute-start.23 = (f32[4,24,128]{2,1,0:T(8,128)S(1)}, f32[4,24,128]{2,1,0:T(8,128)S(1)}, u32[]{:S(2)}, u32[]{:S(2)}) collective-permute-start(f32[4,24,128]{2,1,0:T(8,128)S(1)} %get-tuple-element.75), channel_id=1, source_target_pairs={{0,6},{1,7},{2,4},{3,5},{4,2},{5,3},{6,0},{7,1},{8,14},{9,15},{10,... | collective-permute-start | bytes 147464 | tf_op jit(solution)/shard_map/ppermute | solution.py:515
  63.4 4.1 %collective-permute-start.24 = (f32[4,24,128]{2,1,0:T(8,128)S(1)}, f32[4,24,128]{2,1,0:T(8,128)S(1)}, u32[]{:S(2)}, u32[]{:S(2)}) collective-permute-start(f32[4,24,128]{2,1,0:T(8,128)S(1)} %get-tuple-element.76), channel_id=1, source_target_pairs={{0,1},{1,0},{2,3},{3,2},{4,10},{5,11},{6,8},{7,9},{8,6},{9,7},{10,... | collective-permute-start | bytes 147464 | tf_op jit(solution)/shard_map/ppermute | solution.py:515
  72.0 10.6 %collective-permute-start.26 = (f32[8,40,128]{2,1,0:T(8,128)S(1)}, f32[8,40,128]{2,1,0:T(8,128)S(1)}, u32[]{:S(2)}, u32[]{:S(2)}) collective-permute-start(f32[8,40,128]{2,1,0:T(8,128)S(1)} %get-tuple-element.80), channel_id=1, source_target_pairs={{0,1},{1,0},{2,3},{3,2},{4,8},{5,9},{6,10},{7,11},{8,4},{9,5},{10,... | collective-permute-start | bytes 491528 | tf_op jit(solution)/shard_map/ppermute | solution.py:512
  72.1 10.5 %collective-permute-start.25 = (f32[8,40,128]{2,1,0:T(8,128)S(1)}, f32[8,40,128]{2,1,0:T(8,128)S(1)}, u32[]{:S(2)}, u32[]{:S(2)}) collective-permute-start(f32[8,40,128]{2,1,0:T(8,128)S(1)} %get-tuple-element.80), channel_id=1, source_target_pairs={{0,4},{1,5},{2,6},{3,7},{4,0},{5,1},{6,2},{7,3},{8,12},{9,13},{10,... | collective-permute-start | bytes 491528 | tf_op jit(solution)/shard_map/ppermute | solution.py:512
  76.8 5.1 %collective-permute-start.28 = (f32[4,24,128]{2,1,0:T(8,128)S(1)}, f32[4,24,128]{2,1,0:T(8,128)S(1)}, u32[]{:S(2)}, u32[]{:S(2)}) collective-permute-start(f32[4,24,128]{2,1,0:T(8,128)S(1)} %get-tuple-element.82), channel_id=1, source_target_pairs={{0,6},{1,7},{2,4},{3,5},{4,2},{5,3},{6,0},{7,1},{8,14},{9,15},{10,... | collective-permute-start | bytes 147464 | tf_op jit(solution)/shard_map/ppermute | solution.py:515
  76.8 5.1 %collective-permute-start.29 = (f32[4,24,128]{2,1,0:T(8,128)S(1)}, f32[4,24,128]{2,1,0:T(8,128)S(1)}, u32[]{:S(2)}, u32[]{:S(2)}) collective-permute-start(f32[4,24,128]{2,1,0:T(8,128)S(1)} %get-tuple-element.83), channel_id=1, source_target_pairs={{0,1},{1,0},{2,3},{3,2},{4,10},{5,11},{6,8},{7,9},{8,6},{9,7},{10,... | collective-permute-start | bytes 147464 | tf_op jit(solution)/shard_map/ppermute | solution.py:515
  76.8 5.7 %collective-permute-start.27 = (f32[8,24,128]{2,1,0:T(8,128)S(1)}, f32[8,24,128]{2,1,0:T(8,128)S(1)}, u32[]{:S(2)}, u32[]{:S(2)}) collective-permute-start(f32[8,24,128]{2,1,0:T(8,128)S(1)} %get-tuple-element.81), channel_id=1, source_target_pairs={{0,2},{1,3},{2,0},{3,1},{4,6},{5,7},{6,4},{7,5},{8,10},{9,11},{10,... | collective-permute-start | bytes 294920 | tf_op jit(solution)/shard_map/ppermute | solution.py:513
  87.7 1.9 %collective-permute-start.30 = (f32[5,8,3,8,128]{4,3,2,1,0:T(8,128)S(1)}, f32[5,8,3,8,128]{4,3,2,1,0:T(8,128)S(1)}, u32[]{:S(2)}, u32[]{:S(2)}) collective-permute-start(f32[5,8,3,8,128]{4,3,2,1,0:T(8,128)S(1)} %get-tuple-element.87), channel_id=1, source_target_pairs={{0,1},{1,0},{2,3},{3,2},{4,5},{5,4},{6,7},{7,6},{8,9},{9,8},{10,11... | collective-permute-start | bytes 1474568 | tf_op jit(solution)/shard_map/ppermute | solution.py:543
  (9 other events, 28.3 us)

commit v2 on v1

--- a/solution.py
+++ b/solution.py
@@ -115,14 +115,20 @@
 
 def write_d_message(ref, source, lay, right, high):
     start = jnp.where(right, lay.bx - REACH, 0)
-    for x in range(REACH):
+    upper = lax.broadcasted_iota(jnp.int32, (ROWS, LANES), 0) < REACH
+    for x in range(REACH // 2):
         for t in range(lay.zt):
-            rows = jnp.where(
-                high,
-                source[start + x, t, lay.cy - ROWS : lay.cy, :],
-                source[start + x, t, 0:ROWS, :],
+            a, b = (
+                jnp.where(
+                    high,
+                    source[start + plane, t, lay.cy - ROWS : lay.cy, :],
+                    source[start + plane, t, 0:ROWS, :],
+                )
+                for plane in (x, x + REACH // 2)
             )
-            ref[x, t * ROWS : (t + 1) * ROWS, :] = rows
+            last = jnp.where(upper, pltpu.roll(a, REACH, 0), b)
+            first = jnp.where(upper, a, pltpu.roll(b, REACH, 0))
+            ref[x, t * ROWS : (t + 1) * ROWS, :] = jnp.where(high, last, first)
 
 
 def prepare_kernel(lay, *refs):
@@ -249,35 +255,36 @@
     own_x, own_y = HALO, HALO
 
     buffer[own_x : own_x + bx, :, own_y : own_y + cy, :] = p[...]
-    for is_right, start in ((False, 0), (True, own_x + bx)):
-        wants = [v & (r if is_right else ~r) for r, v in z_sides]
+    if nz < 2:
+        buffer[0:own_x] = jnp.zeros((own_x,) + buffer.shape[1:], jnp.float32)
+        buffer[own_x + bx :] = jnp.zeros((own_x,) + buffer.shape[1:], jnp.float32)
+    if ny < 2:
+        empty = (bx + 2 * REACH, zt, HALO, LANES)
+        buffer[own_x - REACH : own_x + bx + REACH, :, 0:own_y, :] = jnp.zeros(empty, jnp.float32)
+        buffer[own_x - REACH : own_x + bx + REACH, :, own_y + cy :, :] = jnp.zeros(empty, jnp.float32)
+    for (right, valid), message in zip(z_sides, z_in):
+        start = jnp.where(right, own_x + bx, 0)
+        skip = jnp.where(right, 0, bx - HALO)
         for x in range(HALO):
-            row = x if is_right else bx - HALO + x
-            block = sum((jnp.where(w, m[row], 0.0) for w, m in zip(wants, z_in)), jnp.zeros((lay.zrows, LANES), jnp.float32))
+            block = jnp.where(valid, message[skip + x], 0.0)
             for t, tile in enumerate(unpack(block, lay, cy)):
                 buffer[start + x, t, own_y : own_y + cy, :] = tile
-    for is_high, start in ((False, 0), (True, own_y + cy)):
-        wants = [v & (h if is_high else ~h) for h, v in y_sides]
+    for (high, valid), message in zip(y_sides, y_in):
+        start = pl.multiple_of(jnp.where(high, own_y + cy, own_y - ROWS), ROWS)
         for x in range(bx):
             for t in range(zt):
-                rows = slice(t * ROWS, (t + 1) * ROWS)
-                buffer[own_x + x, t, start : start + ROWS, :] = sum(
-                    (jnp.where(w, m[x, rows, :], 0.0) for w, m in zip(wants, y_in)),
-                    jnp.zeros((ROWS, LANES), jnp.float32),
-                )
-        for is_right, x_start in ((False, own_x - REACH), (True, own_x + bx)):
-            corner = [
-                v & u & (r if is_right else ~r) & (h if is_high else ~h)
-                for r, v in z_sides
-                for h, u in y_sides
-            ]
-            for x in range(REACH):
-                for t in range(zt):
-                    rows = slice(t * ROWS, (t + 1) * ROWS)
-                    buffer[x_start + x, t, start : start + ROWS, :] = sum(
-                        (jnp.where(w, m[x, rows, :], 0.0) for w, m in zip(corner, d_in)),
-                        jnp.zeros((ROWS, LANES), jnp.float32),
-                    )
+                rows = message[x, t * ROWS : (t + 1) * ROWS, :]
+                buffer[own_x + x, t, pl.ds(start, ROWS), :] = jnp.where(valid, rows, 0.0)
+    corners = [(r, h, u & v) for r, u in z_sides for h, v in y_sides]
+    for (right, high, valid), message in zip(corners, d_in):
+        x_start = jnp.where(right, own_x + bx, own_x - REACH)
+        start = pl.multiple_of(jnp.where(high, own_y + cy, own_y - ROWS), ROWS)
+        for x in range(REACH // 2):
+            for t in range(zt):
+                rows = jnp.where(valid, message[x, t * ROWS : (t + 1) * ROWS, :], 0.0)
+                turned = pltpu.roll(rows, REACH, 0)
+                buffer[x_start + x, t, pl.ds(start, ROWS), :] = jnp.where(high, rows, turned)
+                buffer[x_start + x + REACH // 2, t, pl.ds(start, ROWS), :] = jnp.where(high, turned, rows)
 
     if first:
         for lead, own, ext in ((0, q, q_ext), (1, s, s_out)):
@@ -285,11 +292,10 @@
             for x in range(bx):
                 for t in range(zt):
                     ext[REACH + x, t, REACH : REACH + cy, :] = own[x, t]
-            for is_right, start in ((False, 0), (True, REACH + bx)):
-                wants = [v & (r if is_right else ~r) for r, v in z_sides]
+            for (right, valid), message in zip(z_sides, z_in):
+                start = jnp.where(right, REACH + bx, 0)
                 for x in range(REACH):
-                    row = bx + lead * REACH + x
-                    block = sum((jnp.where(w, m[row], 0.0) for w, m in zip(wants, z_in)), jnp.zeros((lay.zrows, LANES), jnp.float32))
+                    block = jnp.where(valid, message[bx + lead * REACH + x], 0.0)
                     for t, tile in enumerate(unpack(block, lay, cy)):
                         ext[start + x, t, REACH : REACH + cy, :] = tile
             for is_high, start, cut in ((False, 0, ROWS - REACH), (True, REACH + cy, 0)):
@@ -318,20 +324,20 @@
             )
             target[x, tile] += jnp.where(here, speed_rows(x, tile) * amount, 0.0)
 
-    def step_one(x, carry):
+    for x in range(lay.ex):
+        inside = REACH <= x < REACH + bx
+        y, count = (0, lay.ey) if inside else (REACH, cy)
         out = advance(
-            lay, buffer, x + REACH, REACH, lay.ey,
-            [q[x, t] for t in range(zt)], [s[x, t] for t in range(zt)],
-            injected(x, lay.ey, 0, lay.steps - 1 - time),
+            lay, buffer, x + REACH, y + REACH, count,
+            [q[x, t, y : y + count, :] for t in range(zt)],
+            [s[x, t, y : y + count, :] for t in range(zt)],
+            injected(x, count, y, lay.steps - 1 - time),
         )
         for t in range(zt):
-            q_out[x, t] = out[t]
-        return carry
-
-    lax.fori_loop(0, lay.ex, step_one, 0)
+            q_out[x, t, y : y + count, :] = out[t]
     add_source(q_out, lambda x, t: s[x, t], where[0] + REACH, where[1] + REACH, lay.ex, lay.ey, wavelet[time])
 
-    def step_two(x, carry):
+    for x in range(bx):
         out = advance(
             lay, q_out, x + REACH, REACH, cy,
             [p[x, t] for t in range(zt)],
@@ -341,9 +347,6 @@
         for t in range(zt):
             latest[x, t] = out[t]
             middle[x, t] = q_out[x + REACH, t, REACH : REACH + cy, :]
-        return carry
-
-    lax.fori_loop(0, bx, step_two, 0)
     add_source(
         latest, lambda x, t: s[x + REACH, t, REACH : REACH + cy, :], where[0], where[1], bx, cy, wavelet[time + 1]
     )
@@ -488,7 +491,7 @@
     y_rows = lay.zt * ROWS
     z_shape = (lay.bx, lay.zrows, LANES)
     y_shape = (lay.bx, y_rows, LANES)
-    d_shape = (REACH, y_rows, LANES)
+    d_shape = (REACH // 2, y_rows, LANES)
 
     outs = [(block, f32)] * 3 + [((lay.bx + 2 * REACH, lay.zrows, LANES), f32)] * nz
     outs += [((3 * lay.bx, y_rows, LANES), f32)] * ny + [(d_shape, f32)] * (nz * ny)

time: 90.8 us -> 79.7 us (0.88)
  Pallas kernels: 25.6 us -> 16.1 us
  waiting for transfers between devices: 24.9 us -> 23.8 us
    pallas_call x9, Pallas kernels: 25.6 us -> 16.1 us  [call(): pl.pallas_call(kernel, out_shape=[jax.ShapeDtypeStruct(shape, dtype) for...]
    ppermute x10, waiting for transfers between devices: 15.5 us -> 14.4 us  [body(): d_in = [lax.ppermute(m, AXES, pairs) for m, pairs in zip(d_out, diagonals)]]
  transfers between devices with their start and end apart: 31 -> 31, of which waited for: 8 -> 8; matrix products, arithmetic and copies ran while one was open for 1% -> 2% of each run, Pallas kernels for 2% -> 2%
where the time goes in v2:
time: 79.7 us; the launch traced here: 79.4 us
  starting transfers between devices  35.7 us (45%)
  waiting for transfers between devices  23.8 us (30%)
  Pallas kernels  16.1 us (20%)
  other arithmetic  1.88 us (2%)
  between operations  1.66 us (2%)
    ppermute x10, starting transfers between devices, body(): lax.ppermute(m, AXES, lay.z_permutation(pz))  18.2 us
    pallas_call x9, Pallas kernels, call(): pl.pallas_call(kernel, out_shape=[jax.ShapeDtypeStruct(shape, dtype) for...  16.1 us
    ppermute x10, waiting for transfers between devices, body(): d_in = [lax.ppermute(m, AXES, pairs) for m, pairs in zip(d_out, diagonals)]  14.4 us
    ppermute x3, starting transfers between devices, gather_traces(): message = jnp.concatenate([message, lax.ppermute(message, AXES, pairs)], 0)  7.81 us
    ppermute x3, waiting for transfers between devices, gather_traces(): message = jnp.concatenate([message, lax.ppermute(message, AXES, pairs)], 0)  6.91 us
    ppermute x5, starting transfers between devices, body(): lax.ppermute(m, AXES, lay.y_permutation(py))  4.57 us
    ppermute x10, starting transfers between devices, body(): d_in = [lax.ppermute(m, AXES, pairs) for m, pairs in zip(d_out, diagonals)]  4.44 us
    ppermute x1, waiting for transfers between devices, body(): theirs = lax.ppermute(theirs, AXES, lay.core_permutation())  1.85 us
  transfers between devices with their start and end apart: 31, of which 8 were waited for; matrix products, arithmetic and copies ran while one was open for 2% of the time, Pallas kernels for 2%

profile of v2, /device:TPU:0, one launch (start us, length us, event | category | flops | bytes accessed | tf_op | source)
XLA Modules:
  0.0 79.4 jit_solution(5535801884466423884)
XLA Ops:
  0.6 0.7 fusion.1
  1.9 1.0 %select_bitcast_fusion = (f32[1,8,8,320]{3,2,1,0:T(8,128)S(1)}, f32[1,8,8,320]{3,2,1,0:T(8,128)S(1)}) fusion(f32[8,8,320]{2,1,0:T(8,128)} %refs_3_.1, f32[8,8,320]{2,1,0:T(8,128)} %refs_1_.1, pred[]{:T(512)S(6)} %eq.9, f32[8,8,320]{2,1,0:T(8,128)} %refs_2_.1, f32[8,8,320]{2,1,0:T(8,128)} %refs_0_.1), kind=kLoop, calls=%fused_computation.1 | loop fusion | flops 40960 | bytes 491521 | tf_op jit(solution)/shard_map/stack | solution.py:466
  3.0 2.7 %collective-permute-start.2 = (f32[1,16,128]{2,1,0:T(8,128)S(1)}, f32[1,16,128]{2,1,0:T(8,128)S(1)}, u32[]{:S(2)}, u32[]{:S(2)}) collective-permute-start(f32[1,16,128]{2,1,0:T(8,128)S(1)} %maximum_bitcast_fusion), channel_id=1, source_target_pairs={{0,2},{1,3},{2,0},{3,1},{4,6},{5,7},{6,4},{7,5},{8,10},{9,11},{10,... | collective-permute-start | bytes 24584 | tf_op jit(solution)/shard_map/ppermute | solution.py:438
  5.8 1.4 %collective-permute-done.2 = f32[1,16,128]{2,1,0:T(8,128)S(1)} collective-permute-done((f32[1,16,128]{2,1,0:T(8,128)S(1)}, f32[1,16,128]{2,1,0:T(8,128)S(1)}, u32[]{:S(2)}, u32[]{:S(2)}) %collective-permute-start.2) | collective-permute-done | bytes 8224 | tf_op jit(solution)/shard_map/ppermute | solution.py:438
  7.2 2.1 %collective-permute-start.3 = (f32[2,16,128]{2,1,0:T(8,128)S(1)}, f32[2,16,128]{2,1,0:T(8,128)S(1)}, u32[]{:S(2)}, u32[]{:S(2)}) collective-permute-start(f32[2,16,128]{2,1,0:T(8,128)S(1)} %pad_maximum_fusion.3), channel_id=1, source_target_pairs={{0,4},{1,5},{2,6},{3,7},{4,0},{5,1},{6,2},{7,3},{8,12},{9,13},{10,... | collective-permute-start | bytes 49160 | tf_op jit(solution)/shard_map/ppermute | solution.py:438
  10.3 1.6 %collective-permute-start.7 = (f32[24,24,128]{2,1,0:T(8,128)S(1)}, f32[24,24,128]{2,1,0:T(8,128)S(1)}, u32[]{:S(2)}, u32[]{:S(2)}) collective-permute-start(f32[24,24,128]{2,1,0:T(8,128)S(1)} %get-tuple-element.52), channel_id=1, source_target_pairs={{0,2},{1,3},{2,0},{3,1},{4,6},{5,7},{6,4},{7,5},{8,10},{9,11},{10,... | collective-permute-start | bytes 884744 | tf_op jit(solution)/shard_map/ppermute | solution.py:516
  12.3 3.0 %collective-permute-start.4 = (f32[4,16,128]{2,1,0:T(8,128)S(1)}, f32[4,16,128]{2,1,0:T(8,128)S(1)}, u32[]{:S(2)}, u32[]{:S(2)}) collective-permute-start(f32[4,16,128]{2,1,0:T(8,128)S(1)} %pad_maximum_fusion.2), channel_id=1, source_target_pairs={{0,8},{1,9},{2,10},{3,11},{4,12},{5,13},{6,14},{7,15},{8,0},{9,1},... | collective-permute-start | bytes 98312 | tf_op jit(solution)/shard_map/ppermute | solution.py:438
  15.4 1.4 %collective-permute-start.8 = (f32[2,24,128]{2,1,0:T(8,128)S(1)}, f32[2,24,128]{2,1,0:T(8,128)S(1)}, u32[]{:S(2)}, u32[]{:S(2)}) collective-permute-start(f32[2,24,128]{2,1,0:T(8,128)S(1)} %get-tuple-element.53), channel_id=1, source_target_pairs={{0,6},{1,7},{2,4},{3,5},{4,2},{5,3},{6,0},{7,1},{8,14},{9,15},{10,... | collective-permute-start | bytes 73736 | tf_op jit(solution)/shard_map/ppermute | solution.py:518
  16.9 5.5 %collective-permute-done.4 = f32[4,16,128]{2,1,0:T(8,128)S(1)} collective-permute-done((f32[4,16,128]{2,1,0:T(8,128)S(1)}, f32[4,16,128]{2,1,0:T(8,128)S(1)}, u32[]{:S(2)}, u32[]{:S(2)}) %collective-permute-start.4) | collective-permute-done | bytes 32800 | tf_op jit(solution)/shard_map/ppermute | solution.py:438
  22.4 1.5 %shard_map.164.refs_5_ = f32[16,24,128]{2,1,0:T(8,128)S(1)} custom-call(f32[8,16,128]{2,1,0:T(8,128)S(1)} %pad_maximum_fusion.1.gathered), custom_call_target="tpu_custom_call" | custom-call | tf_op jit(solution)/shard_map/pallas_call | solution.py:406
  23.9 2.6 %shard_map.165 = (f32[8,3,16,128]{3,2,1,0:T(8,128)S(1)}, f32[8,3,16,128]{3,2,1,0:T(8,128)S(1)}, f32[16,3,24,128]{3,2,1,0:T(8,128)S(1)}, f32[8,40,128]{2,1,0:T(8,...) custom-call(f32[10]{0:T(128)S(1)} %broadcast_select_fusion.refs_0_, ...), custom_call_target="tpu_custom_call" | custom-call | tf_op jit(solution)/shard_map/pallas_call | solution.py:406
  26.5 0.6 collective-permute-start.11
  27.1 4.1 %collective-permute-start.10 = (f32[8,40,128]{2,1,0:T(8,128)S(1)}, f32[8,40,128]{2,1,0:T(8,128)S(1)}, u32[]{:S(2)}, u32[]{:S(2)}) collective-permute-start(f32[8,40,128]{2,1,0:T(8,128)S(1)} %get-tuple-element.59), channel_id=1, source_target_pairs={{0,4},{1,5},{2,6},{3,7},{4,0},{5,1},{6,2},{7,3},{8,12},{9,13},{10,... | collective-permute-start | bytes 491528 | tf_op jit(solution)/shard_map/ppermute | solution.py:515
  31.7 1.0 %collective-permute-start.13 = (f32[2,24,128]{2,1,0:T(8,128)S(1)}, f32[2,24,128]{2,1,0:T(8,128)S(1)}, u32[]{:S(2)}, u32[]{:S(2)}) collective-permute-start(f32[2,24,128]{2,1,0:T(8,128)S(1)} %get-tuple-element.61), channel_id=1, source_target_pairs={{0,6},{1,7},{2,4},{3,5},{4,2},{5,3},{6,0},{7,1},{8,14},{9,15},{10,... | collective-permute-start | bytes 73736 | tf_op jit(solution)/shard_map/ppermute | solution.py:518
  32.7 3.7 %collective-permute-done.13.refs_9_ = f32[2,24,128]{2,1,0:T(8,128)S(1)} collective-permute-done((f32[2,24,128]{2,1,0:T(8,128)S(1)}, f32[2,24,128]{2,1,0:T(8,128)S(1)}, u32[]{:S(2)}, u32[]{:S(2)}) %collective-permute-start.13) | collective-permute-done | bytes 24608 | tf_op jit(solution)/shard_map/ppermute | solution.py:518
  36.5 2.5 %shard_map.166 = (f32[8,3,16,128]{3,2,1,0:T(8,128)S(1)}, f32[8,3,16,128]{3,2,1,0:T(8,128)S(1)}, f32[16,3,24,128]{3,2,1,0:T(8,128)S(1)}, f32[8,40,128]{2,1,0:T(8,...) custom-call(f32[10]{0:T(128)S(1)} %broadcast_select_fusion.refs_0_, ...), custom_call_target="tpu_custom_call" | custom-call | tf_op jit(solution)/shard_map/pallas_call | solution.py:406
  39.1 4.9 %collective-permute-start.15 = (f32[8,40,128]{2,1,0:T(8,128)S(1)}, f32[8,40,128]{2,1,0:T(8,128)S(1)}, u32[]{:S(2)}, u32[]{:S(2)}) collective-permute-start(f32[8,40,128]{2,1,0:T(8,128)S(1)} %get-tuple-element.66), channel_id=1, source_target_pairs={{0,4},{1,5},{2,6},{3,7},{4,0},{5,1},{6,2},{7,3},{8,12},{9,13},{10,... | collective-permute-start | bytes 491528 | tf_op jit(solution)/shard_map/ppermute | solution.py:515
  44.5 0.9 %collective-permute-start.18 = (f32[2,24,128]{2,1,0:T(8,128)S(1)}, f32[2,24,128]{2,1,0:T(8,128)S(1)}, u32[]{:S(2)}, u32[]{:S(2)}) collective-permute-start(f32[2,24,128]{2,1,0:T(8,128)S(1)} %get-tuple-element.68), channel_id=1, source_target_pairs={{0,6},{1,7},{2,4},{3,5},{4,2},{5,3},{6,0},{7,1},{8,14},{9,15},{10,... | collective-permute-start | bytes 73736 | tf_op jit(solution)/shard_map/ppermute | solution.py:518
  45.5 3.8 %collective-permute-done.18.refs_9_ = f32[2,24,128]{2,1,0:T(8,128)S(1)} collective-permute-done((f32[2,24,128]{2,1,0:T(8,128)S(1)}, f32[2,24,128]{2,1,0:T(8,128)S(1)}, u32[]{:S(2)}, u32[]{:S(2)}) %collective-permute-start.18) | collective-permute-done | bytes 24608 | tf_op jit(solution)/shard_map/ppermute | solution.py:518
  49.3 2.5 %shard_map.167 = (f32[8,3,16,128]{3,2,1,0:T(8,128)S(1)}, f32[8,3,16,128]{3,2,1,0:T(8,128)S(1)}, f32[16,3,24,128]{3,2,1,0:T(8,128)S(1)}, f32[8,40,128]{2,1,0:T(8,...) custom-call(f32[10]{0:T(128)S(1)} %broadcast_select_fusion.refs_0_, ...), custom_call_target="tpu_custom_call" | custom-call | tf_op jit(solution)/shard_map/pallas_call | solution.py:406
  51.9 3.0 %collective-permute-start.20 = (f32[8,40,128]{2,1,0:T(8,128)S(1)}, f32[8,40,128]{2,1,0:T(8,128)S(1)}, u32[]{:S(2)}, u32[]{:S(2)}) collective-permute-start(f32[8,40,128]{2,1,0:T(8,128)S(1)} %get-tuple-element.73), channel_id=1, source_target_pairs={{0,4},{1,5},{2,6},{3,7},{4,0},{5,1},{6,2},{7,3},{8,12},{9,13},{10,... | collective-permute-start | bytes 491528 | tf_op jit(solution)/shard_map/ppermute | solution.py:515
  55.4 1.0 %collective-permute-start.23 = (f32[2,24,128]{2,1,0:T(8,128)S(1)}, f32[2,24,128]{2,1,0:T(8,128)S(1)}, u32[]{:S(2)}, u32[]{:S(2)}) collective-permute-start(f32[2,24,128]{2,1,0:T(8,128)S(1)} %get-tuple-element.75), channel_id=1, source_target_pairs={{0,6},{1,7},{2,4},{3,5},{4,2},{5,3},{6,0},{7,1},{8,14},{9,15},{10,... | collective-permute-start | bytes 73736 | tf_op jit(solution)/shard_map/ppermute | solution.py:518
  56.6 3.5 %collective-permute-done.23.refs_9_ = f32[2,24,128]{2,1,0:T(8,128)S(1)} collective-permute-done((f32[2,24,128]{2,1,0:T(8,128)S(1)}, f32[2,24,128]{2,1,0:T(8,128)S(1)}, u32[]{:S(2)}, u32[]{:S(2)}) %collective-permute-start.23) | collective-permute-done | bytes 24608 | tf_op jit(solution)/shard_map/ppermute | solution.py:518
  60.2 2.7 %shard_map.168 = (f32[8,3,16,128]{3,2,1,0:T(8,128)S(1)}, f32[8,3,16,128]{3,2,1,0:T(8,128)S(1)}, f32[16,3,24,128]{3,2,1,0:T(8,128)S(1)}, f32[8,40,128]{2,1,0:T(8,...) custom-call(f32[10]{0:T(128)S(1)} %broadcast_select_fusion.refs_0_, ...), custom_call_target="tpu_custom_call" | custom-call | tf_op jit(solution)/shard_map/pallas_call | solution.py:406
  62.9 4.9 %collective-permute-start.25 = (f32[8,40,128]{2,1,0:T(8,128)S(1)}, f32[8,40,128]{2,1,0:T(8,128)S(1)}, u32[]{:S(2)}, u32[]{:S(2)}) collective-permute-start(f32[8,40,128]{2,1,0:T(8,128)S(1)} %get-tuple-element.80), channel_id=1, source_target_pairs={{0,4},{1,5},{2,6},{3,7},{4,0},{5,1},{6,2},{7,3},{8,12},{9,13},{10,... | collective-permute-start | bytes 491528 | tf_op jit(solution)/shard_map/ppermute | solution.py:515
  67.8 1.5 %collective-permute-start.27 = (f32[8,24,128]{2,1,0:T(8,128)S(1)}, f32[8,24,128]{2,1,0:T(8,128)S(1)}, u32[]{:S(2)}, u32[]{:S(2)}) collective-permute-start(f32[8,24,128]{2,1,0:T(8,128)S(1)} %get-tuple-element.81), channel_id=1, source_target_pairs={{0,2},{1,3},{2,0},{3,1},{4,6},{5,7},{6,4},{7,5},{8,10},{9,11},{10,... | collective-permute-start | bytes 294920 | tf_op jit(solution)/shard_map/ppermute | solution.py:516
  69.3 3.4 %collective-permute-done.28.refs_9_ = f32[2,24,128]{2,1,0:T(8,128)S(1)} collective-permute-done((f32[2,24,128]{2,1,0:T(8,128)S(1)}, f32[2,24,128]{2,1,0:T(8,128)S(1)}, u32[]{:S(2)}, u32[]{:S(2)}) %collective-permute-start.28) | collective-permute-done | bytes 24608 | tf_op jit(solution)/shard_map/ppermute | solution.py:518
  72.7 0.6 collective-permute-done.27.refs_8_
  73.3 2.4 %shard_map.169 = (f32[8,3,16,128]{3,2,1,0:T(8,128)S(1)}, f32[8,3,16,128]{3,2,1,0:T(8,128)S(1)}) custom-call(f32[10]{0:T(128)S(1)} %broadcast_select_fusion.refs_0_, s32[3]{0:T(128)S(1)} %pad_add_fusion.refs_1_, f32[8,3,16,128]{3,2,1,0:T(8,128)S(1)} %get-tuple-element.78.refs_2_.refs_7_, f32[16,3,24,128]{3,2,1,0:T(8,128)S(1)} %get-tuple-element.79.refs_3_, ...), custom_call_target="tpu_custom_call" | custom-call | tf_op jit(solution)/shard_map/pallas_call | solution.py:406
  75.7 0.8 %shard_map.170 = (f32[5,8,3,8,128]{4,3,2,1,0:T(8,128)S(1)}, f32[5,8,3,8,128]{4,3,2,1,0:T(8,128)S(1)}) custom-call(s32[3]{0:T(128)S(1)} %broadcast_select_fusion.1.times, f32[8,3,16,128]{3,2,1,0:T(8,128)S(1)} %get-tuple-element.55.refs_0_, f32[8,3,16,128]{3,2,1,0:T(8,128)S(1)} %get-tuple-element.56.refs_2_.refs_1_, ...), custom_call_target="tpu_custom_call" | custom-call | tf_op jit(solution)/shard_map/pallas_call | solution.py:406
  76.7 1.9 %collective-permute-done.30.theirs = f32[5,8,3,8,128]{4,3,2,1,0:T(8,128)S(1)} collective-permute-done((f32[5,8,3,8,128]{4,3,2,1,0:T(8,128)S(1)}, f32[5,8,3,8,128]{4,3,2,1,0:T(8,128)S(1)}, u32[]{:S(2)}, u32[]{:S(2)}) %collective-permute-start.30) | collective-permute-done | bytes 491552 | tf_op jit(solution)/shard_map/ppermute | solution.py:546
  78.5 0.9 %shard_map.171 = (f32[8,8,320]{2,1,0:T(8,128)}, f32[8,8,320]{2,1,0:T(8,128)}, f32[8,8,320]{2,1,0:T(8,128)}, f32[8,8,320]{2,1,0:T(8,128)}, bf16[4,8,8,320]{3,2,1,0:T(8,128)(2,1)}, /*index=5*/f32[8,8,320]{2,1,0:T(8,128)}) custom-call(f32[5,8,3,8,128]{4,3,2,1,0:T(8,128)S(1)} %get-tuple-element.86.own, f32[5,8,3,8,128]{4,3,2,1,0:T(8,128)S(1)} %collective-permute-done.30.theirs, ...), custom_call_target="tpu_custom_call" | custom-call | tf_op jit(solution)/shard_map/pallas_call | solution.py:406
  (73 shorter events, 3.6 us)
Async XLA Ops:
  1.3 1.5 %collective-permute-start.1 = (f32[16,64]{1,0:T(8,128)S(1)}, f32[16,64]{1,0:T(8,128)S(1)}, u32[]{:S(2)}, u32[]{:S(2)}) collective-permute-start(f32[16,64]{1,0:T(8,128)S(1)} %pad_maximum_fusion.4), channel_id=1, source_target_pairs={{0,1},{1,0},{2,3},{3,2},{4,5},{5,4},{6,7},{7,6},{8,9},{9,8},{10,11... | collective-permute-start | bytes 12296 | tf_op jit(solution)/shard_map/ppermute | solution.py:423
  3.0 4.3 %collective-permute-start.2 = (f32[1,16,128]{2,1,0:T(8,128)S(1)}, f32[1,16,128]{2,1,0:T(8,128)S(1)}, u32[]{:S(2)}, u32[]{:S(2)}) collective-permute-start(f32[1,16,128]{2,1,0:T(8,128)S(1)} %maximum_bitcast_fusion), channel_id=1, source_target_pairs={{0,2},{1,3},{2,0},{3,1},{4,6},{5,7},{6,4},{7,5},{8,10},{9,11},{10,... | collective-permute-start | bytes 24584 | tf_op jit(solution)/shard_map/ppermute | solution.py:438
  5.6 4.5 %copy-start.4 = (f32[8,8,320]{2,1,0:T(8,128)S(1)}, f32[8,8,320]{2,1,0:T(8,128)}, u32[]{:S(2)}) copy-start(f32[8,8,320]{2,1,0:T(8,128)} %refs_3_.1) | copy-start | bytes 245764
  5.7 4.4 %collective-permute-start = (f32[3,8,8,320]{3,2,1,0:T(8,128)S(1)}, f32[3,8,8,320]{3,2,1,0:T(8,128)S(1)}, u32[]{:S(2)}, u32[]{:S(2)}) collective-permute-start(f32[3,8,8,320]{3,2,1,0:T(8,128)S(1)} %pad_maximum_fusion), channel_id=1, source_target_pairs={{0,1},{1,0},{2,3},{3,2},{4,5},{5,4},{6,7},{7,6},{8,9},{9,8},{10,11... | collective-permute-start | bytes 737288 | tf_op jit(solution)/shard_map/ppermute | solution.py:473
  7.2 5.1 %collective-permute-start.3 = (f32[2,16,128]{2,1,0:T(8,128)S(1)}, f32[2,16,128]{2,1,0:T(8,128)S(1)}, u32[]{:S(2)}, u32[]{:S(2)}) collective-permute-start(f32[2,16,128]{2,1,0:T(8,128)S(1)} %pad_maximum_fusion.3), channel_id=1, source_target_pairs={{0,4},{1,5},{2,6},{3,7},{4,0},{5,1},{6,2},{7,3},{8,12},{9,13},{10,... | collective-permute-start | bytes 49160 | tf_op jit(solution)/shard_map/ppermute | solution.py:438
  10.3 13.5 %collective-permute-start.7 = (f32[24,24,128]{2,1,0:T(8,128)S(1)}, f32[24,24,128]{2,1,0:T(8,128)S(1)}, u32[]{:S(2)}, u32[]{:S(2)}) collective-permute-start(f32[24,24,128]{2,1,0:T(8,128)S(1)} %get-tuple-element.52), channel_id=1, source_target_pairs={{0,2},{1,3},{2,0},{3,1},{4,6},{5,7},{6,4},{7,5},{8,10},{9,11},{10,... | collective-permute-start | bytes 884744 | tf_op jit(solution)/shard_map/ppermute | solution.py:516
  11.9 12.0 %collective-permute-start.5 = (f32[16,40,128]{2,1,0:T(8,128)S(1)}, f32[16,40,128]{2,1,0:T(8,128)S(1)}, u32[]{:S(2)}, u32[]{:S(2)}) collective-permute-start(f32[16,40,128]{2,1,0:T(8,128)S(1)} %get-tuple-element.50), channel_id=1, source_target_pairs={{0,4},{1,5},{2,6},{3,7},{4,0},{5,1},{6,2},{7,3},{8,12},{9,13},{10,... | collective-permute-start | bytes 983048 | tf_op jit(solution)/shard_map/ppermute | solution.py:515
  12.3 11.6 %collective-permute-start.6 = (f32[16,40,128]{2,1,0:T(8,128)S(1)}, f32[16,40,128]{2,1,0:T(8,128)S(1)}, u32[]{:S(2)}, u32[]{:S(2)}) collective-permute-start(f32[16,40,128]{2,1,0:T(8,128)S(1)} %get-tuple-element.51), channel_id=1, source_target_pairs={{0,1},{1,0},{2,3},{3,2},{4,8},{5,9},{6,10},{7,11},{8,4},{9,5},{10,... | collective-permute-start | bytes 983048 | tf_op jit(solution)/shard_map/ppermute | solution.py:515
  12.3 10.0 %collective-permute-start.4 = (f32[4,16,128]{2,1,0:T(8,128)S(1)}, f32[4,16,128]{2,1,0:T(8,128)S(1)}, u32[]{:S(2)}, u32[]{:S(2)}) collective-permute-start(f32[4,16,128]{2,1,0:T(8,128)S(1)} %pad_maximum_fusion.2), channel_id=1, source_target_pairs={{0,8},{1,9},{2,10},{3,11},{4,12},{5,13},{6,14},{7,15},{8,0},{9,1},... | collective-permute-start | bytes 98312 | tf_op jit(solution)/shard_map/ppermute | solution.py:438
  15.4 8.4 %collective-permute-start.8 = (f32[2,24,128]{2,1,0:T(8,128)S(1)}, f32[2,24,128]{2,1,0:T(8,128)S(1)}, u32[]{:S(2)}, u32[]{:S(2)}) collective-permute-start(f32[2,24,128]{2,1,0:T(8,128)S(1)} %get-tuple-element.53), channel_id=1, source_target_pairs={{0,6},{1,7},{2,4},{3,5},{4,2},{5,3},{6,0},{7,1},{8,14},{9,15},{10,... | collective-permute-start | bytes 73736 | tf_op jit(solution)/shard_map/ppermute | solution.py:518
  22.4 1.5 %collective-permute-start.9 = (f32[2,24,128]{2,1,0:T(8,128)S(1)}, f32[2,24,128]{2,1,0:T(8,128)S(1)}, u32[]{:S(2)}, u32[]{:S(2)}) collective-permute-start(f32[2,24,128]{2,1,0:T(8,128)S(1)} %get-tuple-element.54), channel_id=1, source_target_pairs={{0,1},{1,0},{2,3},{3,2},{4,10},{5,11},{6,8},{7,9},{8,6},{9,7},{10,... | collective-permute-start | bytes 73736 | tf_op jit(solution)/shard_map/ppermute | solution.py:518
  26.5 10.0 %collective-permute-start.11 = (f32[8,40,128]{2,1,0:T(8,128)S(1)}, f32[8,40,128]{2,1,0:T(8,128)S(1)}, u32[]{:S(2)}, u32[]{:S(2)}) collective-permute-start(f32[8,40,128]{2,1,0:T(8,128)S(1)} %get-tuple-element.59), channel_id=1, source_target_pairs={{0,1},{1,0},{2,3},{3,2},{4,8},{5,9},{6,10},{7,11},{8,4},{9,5},{10,... | collective-permute-start | bytes 491528 | tf_op jit(solution)/shard_map/ppermute | solution.py:515
  27.1 9.4 %collective-permute-start.10 = (f32[8,40,128]{2,1,0:T(8,128)S(1)}, f32[8,40,128]{2,1,0:T(8,128)S(1)}, u32[]{:S(2)}, u32[]{:S(2)}) collective-permute-start(f32[8,40,128]{2,1,0:T(8,128)S(1)} %get-tuple-element.59), channel_id=1, source_target_pairs={{0,4},{1,5},{2,6},{3,7},{4,0},{5,1},{6,2},{7,3},{8,12},{9,13},{10,... | collective-permute-start | bytes 491528 | tf_op jit(solution)/shard_map/ppermute | solution.py:515
  31.2 5.2 %collective-permute-start.12 = (f32[8,24,128]{2,1,0:T(8,128)S(1)}, f32[8,24,128]{2,1,0:T(8,128)S(1)}, u32[]{:S(2)}, u32[]{:S(2)}) collective-permute-start(f32[8,24,128]{2,1,0:T(8,128)S(1)} %get-tuple-element.60), channel_id=1, source_target_pairs={{0,2},{1,3},{2,0},{3,1},{4,6},{5,7},{6,4},{7,5},{8,10},{9,11},{10,... | collective-permute-start | bytes 294920 | tf_op jit(solution)/shard_map/ppermute | solution.py:516
  31.7 4.7 %collective-permute-start.13 = (f32[2,24,128]{2,1,0:T(8,128)S(1)}, f32[2,24,128]{2,1,0:T(8,128)S(1)}, u32[]{:S(2)}, u32[]{:S(2)}) collective-permute-start(f32[2,24,128]{2,1,0:T(8,128)S(1)} %get-tuple-element.61), channel_id=1, source_target_pairs={{0,6},{1,7},{2,4},{3,5},{4,2},{5,3},{6,0},{7,1},{8,14},{9,15},{10,... | collective-permute-start | bytes 73736 | tf_op jit(solution)/shard_map/ppermute | solution.py:518
  32.7 3.7 %collective-permute-start.14 = (f32[2,24,128]{2,1,0:T(8,128)S(1)}, f32[2,24,128]{2,1,0:T(8,128)S(1)}, u32[]{:S(2)}, u32[]{:S(2)}) collective-permute-start(f32[2,24,128]{2,1,0:T(8,128)S(1)} %get-tuple-element.62), channel_id=1, source_target_pairs={{0,1},{1,0},{2,3},{3,2},{4,10},{5,11},{6,8},{7,9},{8,6},{9,7},{10,... | collective-permute-start | bytes 73736 | tf_op jit(solution)/shard_map/ppermute | solution.py:518
  39.0 10.2 %collective-permute-start.16 = (f32[8,40,128]{2,1,0:T(8,128)S(1)}, f32[8,40,128]{2,1,0:T(8,128)S(1)}, u32[]{:S(2)}, u32[]{:S(2)}) collective-permute-start(f32[8,40,128]{2,1,0:T(8,128)S(1)} %get-tuple-element.66), channel_id=1, source_target_pairs={{0,1},{1,0},{2,3},{3,2},{4,8},{5,9},{6,10},{7,11},{8,4},{9,5},{10,... | collective-permute-start | bytes 491528 | tf_op jit(solution)/shard_map/ppermute | solution.py:515
  39.1 10.2 %collective-permute-start.15 = (f32[8,40,128]{2,1,0:T(8,128)S(1)}, f32[8,40,128]{2,1,0:T(8,128)S(1)}, u32[]{:S(2)}, u32[]{:S(2)}) collective-permute-start(f32[8,40,128]{2,1,0:T(8,128)S(1)} %get-tuple-element.66), channel_id=1, source_target_pairs={{0,4},{1,5},{2,6},{3,7},{4,0},{5,1},{6,2},{7,3},{8,12},{9,13},{10,... | collective-permute-start | bytes 491528 | tf_op jit(solution)/shard_map/ppermute | solution.py:515
  44.0 5.2 %collective-permute-start.17 = (f32[8,24,128]{2,1,0:T(8,128)S(1)}, f32[8,24,128]{2,1,0:T(8,128)S(1)}, u32[]{:S(2)}, u32[]{:S(2)}) collective-permute-start(f32[8,24,128]{2,1,0:T(8,128)S(1)} %get-tuple-element.67), channel_id=1, source_target_pairs={{0,2},{1,3},{2,0},{3,1},{4,6},{5,7},{6,4},{7,5},{8,10},{9,11},{10,... | collective-permute-start | bytes 294920 | tf_op jit(solution)/shard_map/ppermute | solution.py:516
  44.5 4.7 %collective-permute-start.18 = (f32[2,24,128]{2,1,0:T(8,128)S(1)}, f32[2,24,128]{2,1,0:T(8,128)S(1)}, u32[]{:S(2)}, u32[]{:S(2)}) collective-permute-start(f32[2,24,128]{2,1,0:T(8,128)S(1)} %get-tuple-element.68), channel_id=1, source_target_pairs={{0,6},{1,7},{2,4},{3,5},{4,2},{5,3},{6,0},{7,1},{8,14},{9,15},{10,... | collective-permute-start | bytes 73736 | tf_op jit(solution)/shard_map/ppermute | solution.py:518
  45.5 3.8 %collective-permute-start.19 = (f32[2,24,128]{2,1,0:T(8,128)S(1)}, f32[2,24,128]{2,1,0:T(8,128)S(1)}, u32[]{:S(2)}, u32[]{:S(2)}) collective-permute-start(f32[2,24,128]{2,1,0:T(8,128)S(1)} %get-tuple-element.69), channel_id=1, source_target_pairs={{0,1},{1,0},{2,3},{3,2},{4,10},{5,11},{6,8},{7,9},{8,6},{9,7},{10,... | collective-permute-start | bytes 73736 | tf_op jit(solution)/shard_map/ppermute | solution.py:518
  51.8 8.4 %collective-permute-start.21 = (f32[8,40,128]{2,1,0:T(8,128)S(1)}, f32[8,40,128]{2,1,0:T(8,128)S(1)}, u32[]{:S(2)}, u32[]{:S(2)}) collective-permute-start(f32[8,40,128]{2,1,0:T(8,128)S(1)} %get-tuple-element.73), channel_id=1, source_target_pairs={{0,1},{1,0},{2,3},{3,2},{4,8},{5,9},{6,10},{7,11},{8,4},{9,5},{10,... | collective-permute-start | bytes 491528 | tf_op jit(solution)/shard_map/ppermute | solution.py:515
  51.9 8.3 %collective-permute-start.20 = (f32[8,40,128]{2,1,0:T(8,128)S(1)}, f32[8,40,128]{2,1,0:T(8,128)S(1)}, u32[]{:S(2)}, u32[]{:S(2)}) collective-permute-start(f32[8,40,128]{2,1,0:T(8,128)S(1)} %get-tuple-element.73), channel_id=1, source_target_pairs={{0,4},{1,5},{2,6},{3,7},{4,0},{5,1},{6,2},{7,3},{8,12},{9,13},{10,... | collective-permute-start | bytes 491528 | tf_op jit(solution)/shard_map/ppermute | solution.py:515
  54.9 5.3 %collective-permute-start.22 = (f32[8,24,128]{2,1,0:T(8,128)S(1)}, f32[8,24,128]{2,1,0:T(8,128)S(1)}, u32[]{:S(2)}, u32[]{:S(2)}) collective-permute-start(f32[8,24,128]{2,1,0:T(8,128)S(1)} %get-tuple-element.74), channel_id=1, source_target_pairs={{0,2},{1,3},{2,0},{3,1},{4,6},{5,7},{6,4},{7,5},{8,10},{9,11},{10,... | collective-permute-start | bytes 294920 | tf_op jit(solution)/shard_map/ppermute | solution.py:516
  55.4 4.7 %collective-permute-start.23 = (f32[2,24,128]{2,1,0:T(8,128)S(1)}, f32[2,24,128]{2,1,0:T(8,128)S(1)}, u32[]{:S(2)}, u32[]{:S(2)}) collective-permute-start(f32[2,24,128]{2,1,0:T(8,128)S(1)} %get-tuple-element.75), channel_id=1, source_target_pairs={{0,6},{1,7},{2,4},{3,5},{4,2},{5,3},{6,0},{7,1},{8,14},{9,15},{10,... | collective-permute-start | bytes 73736 | tf_op jit(solution)/shard_map/ppermute | solution.py:518
  56.4 3.7 %collective-permute-start.24 = (f32[2,24,128]{2,1,0:T(8,128)S(1)}, f32[2,24,128]{2,1,0:T(8,128)S(1)}, u32[]{:S(2)}, u32[]{:S(2)}) collective-permute-start(f32[2,24,128]{2,1,0:T(8,128)S(1)} %get-tuple-element.76), channel_id=1, source_target_pairs={{0,1},{1,0},{2,3},{3,2},{4,10},{5,11},{6,8},{7,9},{8,6},{9,7},{10,... | collective-permute-start | bytes 73736 | tf_op jit(solution)/shard_map/ppermute | solution.py:518
  62.9 10.5 %collective-permute-start.26 = (f32[8,40,128]{2,1,0:T(8,128)S(1)}, f32[8,40,128]{2,1,0:T(8,128)S(1)}, u32[]{:S(2)}, u32[]{:S(2)}) collective-permute-start(f32[8,40,128]{2,1,0:T(8,128)S(1)} %get-tuple-element.80), channel_id=1, source_target_pairs={{0,1},{1,0},{2,3},{3,2},{4,8},{5,9},{6,10},{7,11},{8,4},{9,5},{10,... | collective-permute-start | bytes 491528 | tf_op jit(solution)/shard_map/ppermute | solution.py:515
  62.9 10.4 %collective-permute-start.25 = (f32[8,40,128]{2,1,0:T(8,128)S(1)}, f32[8,40,128]{2,1,0:T(8,128)S(1)}, u32[]{:S(2)}, u32[]{:S(2)}) collective-permute-start(f32[8,40,128]{2,1,0:T(8,128)S(1)} %get-tuple-element.80), channel_id=1, source_target_pairs={{0,4},{1,5},{2,6},{3,7},{4,0},{5,1},{6,2},{7,3},{8,12},{9,13},{10,... | collective-permute-start | bytes 491528 | tf_op jit(solution)/shard_map/ppermute | solution.py:515
  67.8 4.8 %collective-permute-start.28 = (f32[2,24,128]{2,1,0:T(8,128)S(1)}, f32[2,24,128]{2,1,0:T(8,128)S(1)}, u32[]{:S(2)}, u32[]{:S(2)}) collective-permute-start(f32[2,24,128]{2,1,0:T(8,128)S(1)} %get-tuple-element.82), channel_id=1, source_target_pairs={{0,6},{1,7},{2,4},{3,5},{4,2},{5,3},{6,0},{7,1},{8,14},{9,15},{10,... | collective-permute-start | bytes 73736 | tf_op jit(solution)/shard_map/ppermute | solution.py:518
  67.8 4.8 %collective-permute-start.29 = (f32[2,24,128]{2,1,0:T(8,128)S(1)}, f32[2,24,128]{2,1,0:T(8,128)S(1)}, u32[]{:S(2)}, u32[]{:S(2)}) collective-permute-start(f32[2,24,128]{2,1,0:T(8,128)S(1)} %get-tuple-element.83), channel_id=1, source_target_pairs={{0,1},{1,0},{2,3},{3,2},{4,10},{5,11},{6,8},{7,9},{8,6},{9,7},{10,... | collective-permute-start | bytes 73736 | tf_op jit(solution)/shard_map/ppermute | solution.py:518
  67.8 5.5 %collective-permute-start.27 = (f32[8,24,128]{2,1,0:T(8,128)S(1)}, f32[8,24,128]{2,1,0:T(8,128)S(1)}, u32[]{:S(2)}, u32[]{:S(2)}) collective-permute-start(f32[8,24,128]{2,1,0:T(8,128)S(1)} %get-tuple-element.81), channel_id=1, source_target_pairs={{0,2},{1,3},{2,0},{3,1},{4,6},{5,7},{6,4},{7,5},{8,10},{9,11},{10,... | collective-permute-start | bytes 294920 | tf_op jit(solution)/shard_map/ppermute | solution.py:516
  76.6 1.9 %collective-permute-start.30 = (f32[5,8,3,8,128]{4,3,2,1,0:T(8,128)S(1)}, f32[5,8,3,8,128]{4,3,2,1,0:T(8,128)S(1)}, u32[]{:S(2)}, u32[]{:S(2)}) collective-permute-start(f32[5,8,3,8,128]{4,3,2,1,0:T(8,128)S(1)} %get-tuple-element.87), channel_id=1, source_target_pairs={{0,1},{1,0},{2,3},{3,2},{4,5},{5,4},{6,7},{7,6},{8,9},{9,8},{10,11... | collective-permute-start | bytes 1474568 | tf_op jit(solution)/shard_map/ppermute | solution.py:546
  (9 other events, 28.3 us)

commit v3 on v2

--- a/solution.py
+++ b/solution.py
@@ -27,6 +27,7 @@
         self.packed = 0 < self.rest <= LANES // 2
         self.ex, self.ey = block_x + 2 * REACH, self.cy + 2 * REACH
         self.zrows = self.cy * (self.zt - 1) + self.cy // 2 if self.packed else self.cy * self.zt
+        self.trace_rows = pl.cdiv(steps + 2, 2 * ROWS) * 2 * ROWS
         self.z_parities = [p for p in (0, 1) if p + 1 < self.nx]
         self.y_parities = [p for p in (0, 1) if p + 1 < self.columns]
         assert self.ny % 2 == 0 and block_x >= HALO and block_y % ROWS == 0 and steps % 2 == 0
@@ -55,6 +56,20 @@
         return self.permutation(
             lambda x, c: (x + (1 if x % 2 == pz else -1), c + (1 if c % 2 == py else -1))
         )
+
+    def carriers(self, z_messages, y_messages, d_messages):
+        starts = (self.bx + 2 * REACH, 3 * self.bx, REACH // 2)
+        return [(m, start) for ms, start in zip((z_messages, y_messages, d_messages), starts) for m in ms]
+
+    def by_kind(self, messages):
+        z, y = bool(self.z_parities), bool(self.y_parities)
+        return messages[:z], messages[z : z + y], messages[z + y :]
+
+    def spot(self, message, start, group, part):
+        chunk = group * (self.trace_rows // ROWS) + part
+        per_plane = message.shape[1] // ROWS
+        row = chunk % per_plane * ROWS
+        return start + chunk // per_plane, row if isinstance(row, int) else pl.multiple_of(row, ROWS)
 
     def core_permutation(self):
         return self.permutation(lambda x, c: (-1, -1))
@@ -131,8 +146,39 @@
             ref[x, t * ROWS : (t + 1) * ROWS, :] = jnp.where(high, last, first)
 
 
+def load_kernel(lay, src_now, src_prev, rec_now, rec_prev, speed, traces, cells, mine, swap, message, *scratch):
+    held, samples, numbers, semaphores = scratch
+    copies = [
+        (src_now, held.at[0]),
+        (rec_now, held.at[1]),
+        (src_prev, held.at[2]),
+        (rec_prev, held.at[3]),
+        (speed, mine.at[2]),
+        (speed, swap.at[2]),
+        (traces, samples),
+        (cells, numbers),
+    ]
+    copies = [pltpu.make_async_copy(a, b, semaphores.at[i]) for i, (a, b) in enumerate(copies)]
+    for copy in copies:
+        copy.start()
+    for copy in copies:
+        copy.wait()
+    _, _, core = lay.place()
+    for index in range(2):
+        for x in range(lay.bx):
+            source, receiver = held[2 * index, x], held[2 * index + 1, x]
+            mine[index, x] = jnp.where(core == 0, source, receiver)
+            swap[index, x] = jnp.where(core == 0, receiver, source)
+    cell = numbers[...].astype(jnp.float32)
+    row = jnp.floor((cell + 0.5) * (1.0 / (lay.by * lay.ny)))
+    message[...] = jnp.zeros_like(message)
+    message[0 : lay.steps, :] = samples[...]
+    message[lay.steps : lay.steps + 1, :] = row
+    message[lay.steps + 1 : lay.steps + 2, :] = cell - row * (lay.by * lay.ny)
+
+
 def prepare_kernel(lay, *refs):
-    (src_now, src_prev, rec_now, rec_prev, speed, other), refs = refs[:6], refs[6:]
+    (own, other), refs = refs[:2], refs[2:]
     (p, q, s), refs = refs[:3], refs[3:]
     nz, ny = len(lay.z_parities), len(lay.y_parities)
     z_messages, refs = refs[:nz], refs[nz:]
@@ -142,12 +188,12 @@
     edge = (lay.zt - 1) * LANES
     for ref in (p, q, s):
         ref[:, lay.zt - 1, :, :] = jnp.zeros((lay.bx, lay.cy, LANES), jnp.float32)
-    for index, (ref, a, b) in enumerate(((p, src_now, rec_now), (q, src_prev, rec_prev), (s, speed, speed))):
+    for index, ref in enumerate((p, q, s)):
         for x in range(lay.bx):
             for t in range(lay.zt):
                 width = LANES if t + 1 < lay.zt else lay.rest
                 lanes = slice(t * LANES, t * LANES + width)
-                mine = a[x, :, lanes] if a is b else jnp.where(first, a[x, :, lanes], b[x, :, lanes])
+                mine = own[index, x, :, lanes]
                 theirs = other[index, x, :, lanes]
                 ref[x, t, 0 : lay.by, 0:width] = jnp.where(first, mine, theirs)
                 ref[x, t, lay.by : lay.cy, 0:width] = jnp.where(first, theirs, mine)
@@ -171,15 +217,25 @@
         write_d_message(message, p, lay, right, high)
 
 
-def planes_kernel(lay, gathered, planes, total):
+def append_kernel(lay, *refs):
+    groups, messages = refs[0], refs[1 + (len(refs) - 1) // 2 :]
+    for message, start in lay.carriers(*lay.by_kind(messages)):
+        for group in range(groups.shape[0]):
+            for part in range(lay.trace_rows // ROWS):
+                plane, row = lay.spot(message, start, group, part)
+                message[plane, row : row + ROWS, :] = groups[group, part * ROWS : (part + 1) * ROWS, :]
+
+
+def planes_kernel(lay, *refs):
+    groups, messages, (planes, total) = refs[0], refs[1:-2], refs[-2:]
+    carriers = lay.carriers(*lay.by_kind(messages))
     gx, column, core = lay.place()
     start_x, start_y = gx * lay.bx - REACH, column * lay.cy - REACH
     cells = lay.ex * lay.ey
-    padded = gathered.shape[1]
+    padded = lay.trace_rows
     total[...] = jnp.zeros_like(total)
 
-    def add(index, carry):
-        values = gathered[index]
+    def add(values):
         x = values[lay.steps : lay.steps + 1, :].astype(jnp.int32) - start_x
         y = values[lay.steps + 1 : lay.steps + 2, :].astype(jnp.int32) - start_y
         inside = (x >= 0) & (x < lay.ex) & (y >= 0) & (y < lay.ey)
@@ -195,9 +251,18 @@
         total[...] += lax.dot_general(
             chosen, parts, (((1,), (1,)), ((), ())), preferred_element_type=jnp.float32
         )
+
+    def add_groups(group, carry):
+        add(groups[group])
+        for message, start in carriers:
+            parts = []
+            for part in range(padded // ROWS):
+                plane, row = lay.spot(message, start, group, part)
+                parts.append(message[plane, pl.ds(row, ROWS), :])
+            add(jnp.concatenate(parts, 0))
         return carry
 
-    lax.fori_loop(0, gathered.shape[0], add, 0)
+    lax.fori_loop(0, groups.shape[0], add_groups, 0, unroll=groups.shape[0] <= 2)
     summed = total[...]
     summed = (
         summed + pltpu.roll(summed, LANES - padded, 1) + pltpu.roll(summed, LANES - 2 * padded, 1)
@@ -206,7 +271,7 @@
     planes[...] = summed.reshape(lay.ex, lay.ey, LANES)
 
 
-def advance(lay, field, x, y, rows, before, speed, injected):
+def advance(lay, field, x, y, rows, before, speed):
     lane = lane_ids(rows)
     centre = [field[x, t, y : y + rows, :] for t in range(lay.zt)]
     sums = []
@@ -226,42 +291,34 @@
         drive = 3.0 * STENCIL_COEFFS[0] * centre[t]
         for k in range(REACH):
             drive += STENCIL_COEFFS[k + 1] * sums[k][t]
-        if t == 0:
-            drive += injected
         out.append(2.0 * centre[t] - before[t] + speed[t] * drive)
     return out
 
 
-def round_kernel(lay, time, first, last, *refs):
+def side_kernel(lay, time, *refs):
     nz, ny = len(lay.z_parities), len(lay.y_parities)
-    (wavelet, where, p, q, s, planes), refs = refs[:6], refs[6:]
+    (p, q, s), refs = refs[:3], refs[3:]
+    first = time == 0
+    if not first:
+        p = p.at[time - 1]
     z_in, refs = refs[:nz], refs[nz:]
     y_in, refs = refs[:ny], refs[ny:]
-    d_in, refs = refs[: nz * ny], refs[nz * ny :]
-    (middle, latest), refs = refs[:2], refs[2:]
-    if last:
-        q_out, buffer = refs[:2]
-    else:
-        (q_out, z_out), refs = refs[:2], refs[2:]
-        y_out, refs = refs[:ny], refs[ny:]
-        d_out, refs = refs[: nz * ny], refs[nz * ny :]
-        if first:
-            s_out, q_ext, buffer = refs
-        else:
-            (buffer,) = refs
+    stepped, buffer = refs[0], refs[-1]
     z_sides = [lay.z_side(pz) for pz in lay.z_parities]
     y_sides = [lay.y_side(py) for py in lay.y_parities]
     bx, cy, zt = lay.bx, lay.cy, lay.zt
     own_x, own_y = HALO, HALO
 
     buffer[own_x : own_x + bx, :, own_y : own_y + cy, :] = p[...]
+    around = ((own_x - REACH, own_x), (own_x + bx, own_x + bx + REACH))
+    for low, high in around if ny == 2 else ((own_x - REACH, own_x + bx + REACH),):
+        empty = jnp.zeros((high - low, zt, HALO, LANES), jnp.float32)
+        buffer[low:high, :, 0:own_y, :] = empty
+        buffer[low:high, :, own_y + cy :, :] = empty
     if nz < 2:
-        buffer[0:own_x] = jnp.zeros((own_x,) + buffer.shape[1:], jnp.float32)
-        buffer[own_x + bx :] = jnp.zeros((own_x,) + buffer.shape[1:], jnp.float32)
-    if ny < 2:
-        empty = (bx + 2 * REACH, zt, HALO, LANES)
-        buffer[own_x - REACH : own_x + bx + REACH, :, 0:own_y, :] = jnp.zeros(empty, jnp.float32)
-        buffer[own_x - REACH : own_x + bx + REACH, :, own_y + cy :, :] = jnp.zeros(empty, jnp.float32)
+        empty = jnp.zeros((own_x, zt, cy, LANES), jnp.float32)
+        buffer[0:own_x, :, own_y : own_y + cy, :] = empty
+        buffer[own_x + bx :, :, own_y : own_y + cy, :] = empty
     for (right, valid), message in zip(z_sides, z_in):
         start = jnp.where(right, own_x + bx, 0)
         skip = jnp.where(right, 0, bx - HALO)
@@ -275,18 +332,9 @@
             for t in range(zt):
                 rows = message[x, t * ROWS : (t + 1) * ROWS, :]
                 buffer[own_x + x, t, pl.ds(start, ROWS), :] = jnp.where(valid, rows, 0.0)
-    corners = [(r, h, u & v) for r, u in z_sides for h, v in y_sides]
-    for (right, high, valid), message in zip(corners, d_in):
-        x_start = jnp.where(right, own_x + bx, own_x - REACH)
-        start = pl.multiple_of(jnp.where(high, own_y + cy, own_y - ROWS), ROWS)
-        for x in range(REACH // 2):
-            for t in range(zt):
-                rows = jnp.where(valid, message[x, t * ROWS : (t + 1) * ROWS, :], 0.0)
-                turned = pltpu.roll(rows, REACH, 0)
-                buffer[x_start + x, t, pl.ds(start, ROWS), :] = jnp.where(high, rows, turned)
-                buffer[x_start + x + REACH // 2, t, pl.ds(start, ROWS), :] = jnp.where(high, turned, rows)
 
     if first:
+        s_out, q_ext = refs[1:3]
         for lead, own, ext in ((0, q, q_ext), (1, s, s_out)):
             ext[...] = jnp.zeros_like(ext)
             for x in range(bx):
@@ -309,21 +357,6 @@
                         )
         q, s = q_ext, s_out
 
-    def injected(x, rows, y, back):
-        values = pltpu.roll(planes[x], LANES - back, 1) if back else planes[x]
-        return jnp.where(lane_ids(lay.ey) == 0, values, 0.0)[y : y + rows]
-
-    def add_source(target, speed_rows, x, y, count_x, count_y, amount):
-        @pl.when((x >= 0) & (x < count_x) & (y >= 0) & (y < count_y))
-        def _():
-            depth = where[2]
-            tile, lane = depth // LANES, depth % LANES
-            shape = (count_y, LANES)
-            here = (lax.broadcasted_iota(jnp.int32, shape, 0) == y) & (
-                lax.broadcasted_iota(jnp.int32, shape, 1) == lane
-            )
-            target[x, tile] += jnp.where(here, speed_rows(x, tile) * amount, 0.0)
-
     for x in range(lay.ex):
         inside = REACH <= x < REACH + bx
         y, count = (0, lay.ey) if inside else (REACH, cy)
@@ -331,27 +364,116 @@
             lay, buffer, x + REACH, y + REACH, count,
             [q[x, t, y : y + count, :] for t in range(zt)],
             [s[x, t, y : y + count, :] for t in range(zt)],
-            injected(x, count, y, lay.steps - 1 - time),
         )
         for t in range(zt):
-            q_out[x, t, y : y + count, :] = out[t]
-    add_source(q_out, lambda x, t: s[x, t], where[0] + REACH, where[1] + REACH, lay.ex, lay.ey, wavelet[time])
+            stepped[x, t, y : y + count, :] = out[t]
+
+
+def add_corner(lay, field, s, message, right, high, valid, corner):
+    empty = jnp.zeros((REACH, lay.zt, ROWS, LANES), jnp.float32)
+    corner[:, :, 0:ROWS, :] = empty
+    corner[:, :, 2 * ROWS :, :] = empty
+    upper = lax.broadcasted_iota(jnp.int32, (ROWS, LANES), 0) < REACH
+    near = jnp.where(upper, 1.0, 0.0)
+    keep = jnp.where(valid, jnp.where(high, near, 1.0 - near), 0.0)
+    for x in range(REACH // 2):
+        for t in range(lay.zt):
+            rows = message[x, t * ROWS : (t + 1) * ROWS, :]
+            turned = pltpu.roll(rows, REACH, 0)
+            corner[x, t, ROWS : 2 * ROWS, :] = jnp.where(high, rows, turned) * keep
+            corner[x + REACH // 2, t, ROWS : 2 * ROWS, :] = jnp.where(high, turned, rows) * keep
+    high_share, low_share = jnp.where(high, 1.0, 0.0), jnp.where(high, 0.0, 1.0)
+    planes_start = jnp.where(right, REACH + lay.bx, 0)
+    rows_start = jnp.where(right, lay.bx, REACH)
+    for x in range(REACH):
+        for t in range(lay.zt):
+            above = sum(STENCIL_COEFFS[k] * corner[x, t, k : k + ROWS, :] for k in range(1, REACH + 1))
+            below = sum(
+                STENCIL_COEFFS[k] * corner[x, t, 2 * ROWS - k : 3 * ROWS - k, :] for k in range(1, REACH + 1)
+            )
+            for share, amount, start in (
+                (high_share, above, REACH + lay.cy - ROWS),
+                (low_share, below, REACH),
+            ):
+                rows = slice(start, start + ROWS)
+                field[planes_start + x, t, rows, :] += s[planes_start + x, t, rows, :] * (amount * share)
+            for share, start, cut in (
+                (high_share, lay.ey - ROWS, REACH),
+                (low_share, 0, 2 * ROWS - REACH),
+            ):
+                source = [corner[j, t, cut : cut + ROWS, :] for j in range(REACH)]
+                from_left = sum(STENCIL_COEFFS[x + REACH - j] * source[j] for j in range(x, REACH))
+                from_right = sum(STENCIL_COEFFS[REACH + j - x] * source[j] for j in range(x + 1))
+                amount = jnp.where(right, from_right, from_left) * share
+                rows = slice(start, start + ROWS)
+                field[rows_start + x, t, rows, :] += s[rows_start + x, t, rows, :] * amount
+
+
+def round_kernel(lay, time, *refs):
+    nz, ny = len(lay.z_parities), len(lay.y_parities)
+    last = time + 2 == lay.steps
+    plan, refs = (refs[0], refs[1:]) if last else (None, refs)
+    (wavelet, source_cell, stepped, s, planes, p), refs = refs[:6], refs[6:]
+    d_in, refs = refs[: nz * ny], refs[nz * ny :]
+    (field, history), refs = refs[:2], refs[2:]
+    corner = refs[-1]
+    latest = history.at[time + 1]
+    if time:
+        p = history.at[time - 1]
+    gx, column, core = lay.place()
+    cell, grid_y = source_cell[0], lay.by * lay.ny
+    source_x = cell // (grid_y * lay.depth) - gx * lay.bx
+    source_y = cell // lay.depth % grid_y - column * lay.cy
+    source_z = cell % lay.depth
+    z_sides = [lay.z_side(pz) for pz in lay.z_parities]
+    y_sides = [lay.y_side(py) for py in lay.y_parities]
+    bx, cy, zt = lay.bx, lay.cy, lay.zt
+
+    def injected(x, rows, y, back):
+        values = pltpu.roll(planes[x], LANES - back, 1) if back else planes[x]
+        return jnp.where(lane_ids(lay.ey) == 0, values, 0.0)[y : y + rows]
+
+    def add_source(target, speed_rows, x, y, count_x, count_y, amount):
+        @pl.when((core == 0) & (x >= 0) & (x < count_x) & (y >= 0) & (y < count_y))
+        def _():
+            tile, lane = source_z // LANES, source_z % LANES
+            shape = (count_y, LANES)
+            here = (lax.broadcasted_iota(jnp.int32, shape, 0) == y) & (
+                lax.broadcasted_iota(jnp.int32, shape, 1) == lane
+            )
+            target[x, tile] += jnp.where(here, speed_rows(x, tile) * amount, 0.0)
+
+    corners = [(r, h, u & v) for r, u in z_sides for h, v in y_sides]
+    for (right, high, valid), message in zip(corners, d_in):
+        add_corner(lay, field, s, message, right, high, valid, corner)
+    for x in range(lay.ex):
+        field[x, 0] += s[x, 0] * injected(x, lay.ey, 0, lay.steps - 1 - time)
+    add_source(field, lambda x, t: s[x, t], source_x + REACH, source_y + REACH, lay.ex, lay.ey, wavelet[time])
 
     for x in range(bx):
-        out = advance(
-            lay, q_out, x + REACH, REACH, cy,
-            [p[x, t] for t in range(zt)],
-            [s[x + REACH, t, REACH : REACH + cy, :] for t in range(zt)],
-            injected(x + REACH, cy, REACH, lay.steps - 2 - time),
-        )
+        speed = [s[x + REACH, t, REACH : REACH + cy, :] for t in range(zt)]
+        out = advance(lay, field, x + REACH, REACH, cy, [p[x, t] for t in range(zt)], speed)
+        out[0] += speed[0] * injected(x + REACH, cy, REACH, lay.steps - 2 - time)
         for t in range(zt):
             latest[x, t] = out[t]
-            middle[x, t] = q_out[x + REACH, t, REACH : REACH + cy, :]
+            history[time, x, t] = field[x + REACH, t, REACH : REACH + cy, :]
     add_source(
-        latest, lambda x, t: s[x + REACH, t, REACH : REACH + cy, :], where[0], where[1], bx, cy, wavelet[time + 1]
+        latest, lambda x, t: s[x + REACH, t, REACH : REACH + cy, :], source_x, source_y, bx, cy, wavelet[time + 1]
     )
 
-    if not last:
+    if last:
+        own, theirs = refs[:2]
+        kept = [lay.steps - 2, lay.steps - 1, 0]
+        for slot in range(1, lay.slots - 1):
+            kept.append(jnp.where(core == 0, plan[slot], lay.steps - 1 - plan[lay.slots - 1 - slot]))
+        for index, moment in enumerate(kept):
+            for x in range(bx):
+                for t in range(zt):
+                    low, high = history[moment, x, t, 0 : lay.by, :], history[moment, x, t, lay.by : cy, :]
+                    own[index, x, t] = jnp.where(core == 0, low, high)
+                    theirs[index, x, t] = jnp.where(core == 0, high, low)
+    else:
+        z_out, y_out, d_out = refs[0], refs[1 : 1 + ny], refs[1 + ny : 1 + ny + nz * ny]
         for x in range(bx):
             store_packed(z_out, x, [latest[x, t] for t in range(zt)], lay, cy)
         for message, (high, _) in zip(y_out, y_sides):
@@ -359,24 +481,6 @@
         corners = [(right, high) for right, _ in z_sides for high, _ in y_sides]
         for message, (right, high) in zip(d_out, corners):
             write_d_message(message, latest, lay, right, high)
-
-
-def collect_kernel(lay, times, *refs):
-    fields, own, theirs = refs[: lay.steps], refs[lay.steps], refs[lay.steps + 1]
-    _, _, core = lay.place()
-
-    def put(index, field):
-        for x in range(lay.bx):
-            for t in range(lay.zt):
-                low, high = field[x, t, 0 : lay.by, :], field[x, t, lay.by : lay.cy, :]
-                own[index, x, t] = jnp.where(core == 0, low, high)
-                theirs[index, x, t] = jnp.where(core == 0, high, low)
-
-    put(0, fields[lay.steps - 2])
-    put(1, fields[lay.steps - 1])
-    for slot in range(lay.slots - 1):
-        for time in range(lay.steps):
-            pl.when(times[slot] == time)(functools.partial(put, 2 + slot, fields[time]))
 
 
 def finish_kernel(lay, own, theirs, stored, image_before, *outs):
@@ -400,39 +504,41 @@
             image[x, :, lanes] = total
 
 
-def call(kernel, outs, operands, scratch=(), scalars=0):
+def call(kernel, outs, operands, scratch=(), scalars=0, aliases={}, from_hbm=False):
     in_specs = [pl.BlockSpec(memory_space=pltpu.SMEM)] * scalars
-    in_specs += [pl.BlockSpec(memory_space=pltpu.VMEM)] * (len(operands) - scalars)
+    space = pltpu.HBM if from_hbm else pltpu.VMEM
+    if from_hbm:
+        operands = [pltpu.with_memory_space_constraint(x, pltpu.HBM) for x in operands]
+    in_specs += [pl.BlockSpec(memory_space=space)] * (len(operands) - scalars)
     return pl.pallas_call(
         kernel,
         out_shape=[jax.ShapeDtypeStruct(shape, dtype) for shape, dtype in outs],
         in_specs=in_specs,
         out_specs=[pl.BlockSpec(memory_space=pltpu.VMEM)] * len(outs),
         scratch_shapes=list(scratch),
-        compiler_params=pltpu.CompilerParams(vmem_limit_bytes=16 * 1024 * 1024),
+        input_output_aliases=aliases,
+        compiler_params=pltpu.CompilerParams(vmem_limit_bytes=6 * 1024 * 1024),
     )(*operands)
 
 
-def gather_traces(lay, traces, receiver_cells):
-    grid_y = lay.by * lay.ny
-    cells = receiver_cells
-    rows = [traces, (cells // grid_y).astype(jnp.float32), (cells % grid_y).astype(jnp.float32)]
-    padded = pl.cdiv(lay.steps + 2, 2 * ROWS) * 2 * ROWS
-    rows.append(jnp.zeros((padded - lay.steps - 2, traces.shape[1]), jnp.float32))
-    message = jnp.concatenate(rows, 0)
+def share_in_chip(lay, message):
     other = lax.ppermute(message, AXES, lay.core_permutation())
     message = jnp.concatenate([message, other], 1)[None]
     if message.shape[2] != LANES:
         spare = -message.shape[2] % LANES
-        fill = jnp.full((1, padded, spare), -1e6, jnp.float32)
+        fill = jnp.full((1, lay.trace_rows, spare), -1e6, jnp.float32)
         message = jnp.concatenate([message, fill], 2)
-        message = message.reshape(padded, -1, LANES).transpose(1, 0, 2)
+        message = message.reshape(lay.trace_rows, -1, LANES).transpose(1, 0, 2)
+    return message
+
+
+def spread(lay, message):
     for count, move in (
         (lay.columns, lambda x, c, bit: (x, c ^ bit)),
         (lay.nx, lambda x, c, bit: (x ^ bit, c)),
     ):
         assert count & (count - 1) == 0
-        bit = 1
+        bit = 2
         while bit < count:
             pairs = lay.permutation(functools.partial(move, bit=bit))
             message = jnp.concatenate([message, lax.ppermute(message, AXES, pairs)], 0)
@@ -458,32 +564,26 @@
     steps, slots = wavelet.shape[0], plan.shape[0]
     lay = Layout(mesh, *source_now.shape, steps, slots)
     f32 = jnp.float32
-    gx, gy = lax.axis_index("gx"), lax.axis_index("gy")
-    column, core = gy // 2, gy % 2
-    first = core == 0
+    first = lax.axis_index("gy") % 2 == 0
     nz, ny = len(lay.z_parities), len(lay.y_parities)
 
-    swapped = jnp.stack(
+    half = (3, *source_now.shape)
+    inputs = [source_now, source_prev, receiver_now, receiver_prev, speed_squared, traces, receiver_cells]
+    mine, swapped, message = call(
+        functools.partial(load_kernel, lay),
+        [(half, f32), (half, f32), ((lay.trace_rows, traces.shape[1]), f32)],
+        inputs,
         [
-            jnp.where(first, receiver_now, source_now),
-            jnp.where(first, receiver_prev, source_prev),
-            speed_squared,
-        ]
+            pltpu.VMEM((4, *source_now.shape), f32),
+            pltpu.VMEM(traces.shape, f32),
+            pltpu.VMEM(receiver_cells.shape, jnp.int32),
+            pltpu.SemaphoreType.DMA((8,)),
+        ],
+        from_hbm=True,
     )
     swapped = lax.ppermute(swapped, AXES, lay.core_permutation())
-    gathered = gather_traces(lay, traces, receiver_cells)
-
-    grid_y = lay.by * lay.ny
-    cell = source_cell[0]
-    where = jnp.stack(
-        [
-            cell // (grid_y * lay.depth) - gx * lay.bx,
-            cell // lay.depth % grid_y - column * lay.cy,
-            cell % lay.depth,
-        ]
-    ).astype(jnp.int32)
-    amounts = jnp.where(first, wavelet, 0.0)
-    times = jnp.where(first, plan[:-1], (steps - 1 - plan[1:])[::-1])
+    groups = share_in_chip(lay, message)
+    groups = spread(lay, groups)
 
     block = (lay.bx, lay.zt, lay.cy, LANES)
     ext = (lay.ex, lay.zt, lay.ey, LANES)
@@ -493,56 +593,77 @@
     y_shape = (lay.bx, y_rows, LANES)
     d_shape = (REACH // 2, y_rows, LANES)
 
-    outs = [(block, f32)] * 3 + [((lay.bx + 2 * REACH, lay.zrows, LANES), f32)] * nz
-    outs += [((3 * lay.bx, y_rows, LANES), f32)] * ny + [(d_shape, f32)] * (nz * ny)
+    def carrying(planes, rows, first):
+        more = pl.cdiv(groups.shape[0] * lay.trace_rows, rows) if first else 0
+        return (planes + more, rows, LANES), f32
+
+    outs = [(block, f32)] * 3
+    outs += [carrying(lay.bx + 2 * REACH, lay.zrows, pz == 0) for pz in lay.z_parities]
+    outs += [carrying(3 * lay.bx, y_rows, py == 0) for py in lay.y_parities]
+    outs += [carrying(REACH // 2, y_rows, pz + py == 0) for pz in lay.z_parities for py in lay.y_parities]
     made = call(
         functools.partial(prepare_kernel, lay),
         outs,
-        [source_now, source_prev, receiver_now, receiver_prev, speed_squared, swapped],
+        [mine, swapped],
     )
     (p, q, s), made = made[:3], made[3:]
     z_out, y_out, d_out = made[:nz], made[nz : nz + ny], made[nz + ny :]
-    (planes,) = call(
-        functools.partial(planes_kernel, lay),
-        [((lay.ex, lay.ey, LANES), f32)],
-        [gathered],
-        [pltpu.VMEM((lay.ex * lay.ey, LANES), f32)],
-    )
-
-    fields = []
+    filled = z_out[:1] + y_out[:1] + d_out[:1]
+    if filled:
+        filled = call(
+            functools.partial(append_kernel, lay),
+            [(m.shape, f32) for m in filled],
+            [groups, *filled],
+            aliases={1 + i: i for i in range(len(filled))},
+        )
+        z, y, d = lay.by_kind(filled)
+        z_out, y_out, d_out = z + z_out[1:], y + y_out[1:], d + d_out[1:]
+
     for time in range(0, steps, 2):
         begin, end = time == 0, time + 2 == steps
         z_in = [lax.ppermute(m, AXES, lay.z_permutation(pz)) for m, pz in zip(z_out, lay.z_parities)]
         y_in = [lax.ppermute(m, AXES, lay.y_permutation(py)) for m, py in zip(y_out, lay.y_parities)]
         diagonals = [lay.d_permutation(pz, py) for pz in lay.z_parities for py in lay.y_parities]
         d_in = [lax.ppermute(m, AXES, pairs) for m, pairs in zip(d_out, diagonals)]
-        outs, scratch = [(block, f32)] * 2, []
+        made = call(
+            functools.partial(side_kernel, lay, time),
+            [(ext, f32)] * (2 if begin else 1),
+            [p, q, s, *z_in, *y_in],
+            [pltpu.VMEM(ext, f32)] * begin + [pltpu.VMEM(field, f32)],
+        )
+        stepped = made[0]
+        if begin:
+            s = made[1]
+            groups, stepped = lax.optimization_barrier((groups, stepped))
+            carried = z_in[:1] + y_in[:1] + d_in[:1]
+            (planes,) = call(
+                functools.partial(planes_kernel, lay),
+                [((lay.ex, lay.ey, LANES), f32)],
+                [groups, *carried],
+                [pltpu.VMEM((lay.ex * lay.ey, LANES), f32)],
+            )
+        outs = [(ext, f32), ((steps, *block), f32)]
         if end:
-            scratch.append(pltpu.VMEM(ext, f32))
+            outs += [((slots + 1, lay.bx, lay.zt, lay.by, LANES), f32)] * 2
         else:
-            outs += [(ext, f32), (z_shape, f32)] + [(y_shape, f32)] * ny + [(d_shape, f32)] * (nz * ny)
-            if begin:
-                outs.append((ext, f32))
-                scratch.append(pltpu.VMEM(ext, f32))
-        scratch.append(pltpu.VMEM(field, f32))
+            outs += [(z_shape, f32)] + [(y_shape, f32)] * ny + [(d_shape, f32)] * (nz * ny)
+        scalars = [plan] * end + [wavelet, source_cell]
+        operands = scalars + [stepped, s, planes, p, *d_in]
         made = call(
-            functools.partial(round_kernel, lay, time, begin, end),
+            functools.partial(round_kernel, lay, time),
             outs,
-            [amounts, where, p, q, s, planes, *z_in, *y_in, *d_in],
-            scratch,
-            scalars=2,
+            operands,
+            [pltpu.VMEM((REACH, lay.zt, 3 * ROWS, LANES), f32)],
+            scalars=len(scalars),
+            aliases={len(scalars): 0} | ({} if begin else {len(scalars) + 3: 1}),
         )
-        fields += made[:2]
-        if not end:
-            p, q, z_out = made[1], made[2], [made[3]] * nz
-            y_out, d_out = made[4 : 4 + ny], made[4 + ny : 4 + ny + nz * ny]
-            if begin:
-                s = made[-1]
-
-    kept = (slots + 1, lay.bx, lay.zt, lay.by, LANES)
-    own, theirs = call(
-        functools.partial(collect_kernel, lay), [(kept, f32)] * 2, [times, *fields], scalars=1
-    )
+        q, p = made[:2]
+        if end:
+            own, theirs = made[2:]
+        else:
+            z_out = [made[2]] * nz
+            y_out, d_out = made[3 : 3 + ny], made[3 + ny :]
+
     theirs = lax.ppermute(theirs, AXES, lay.core_permutation())
     shape = source_now.shape
     return tuple(

time: 79.7 us -> 72.2 us (0.906)
  starting transfers between devices: 35.7 us -> 29.6 us
  other arithmetic: 1.88 us -> 0.08 us
  Pallas kernels: 16.1 us -> 16.9 us
    ppermute x5, waiting for transfers between devices: 0.65 us -> 17.4 us  [body(): lax.ppermute(m, AXES, lay.y_permutation(py))]
    ppermute x10, waiting for transfers between devices: 14.4 us -> 1.25 us  [body(): d_in = [lax.ppermute(m, AXES, pairs) for m, pairs in zip(d_out, diagonals)]]
    ppermute x10, starting transfers between devices: 18.2 us -> 13.3 us  [body(): lax.ppermute(m, AXES, lay.z_permutation(pz))]
    ppermute x4 -> x2, starting transfers between devices: 8.33 us -> 4.04 us  [the longest x1 3.96 us: spread(): message = jnp.concatenate([message, lax.ppermute(message, AXES, pairs)], 0)]
    ppermute x4 -> x2, waiting for transfers between devices: 6.91 us -> 2.77 us  [the longest x1 1.63 us: spread(): message = jnp.concatenate([message, lax.ppermute(message, AXES, pairs)], 0)]
    ppermute x5, starting transfers between devices: 4.57 us -> 8.34 us  [body(): lax.ppermute(m, AXES, lay.y_permutation(py))]
    another operation x3 -> x0, other arithmetic: 1.1 us -> none  [the longest x2 1.03 us: body(): jnp.stack([jnp.where(first, receiver_now, source_now), jnp.where(first, r...]
    ppermute x10, starting transfers between devices: 4.44 us -> 3.33 us  [body(): d_in = [lax.ppermute(m, AXES, pairs) for m, pairs in zip(d_out, diagonals)]]
  transfers between devices with their start and end apart: 31 -> 29, of which waited for: 8 -> 12; matrix products, arithmetic and copies ran while one was open for 2% -> 0% of each run, Pallas kernels for 2% -> 10%
where the time goes in v3:
time: 72.2 us; the launch traced here: 72 us
  starting transfers between devices  29.6 us (41%)
  waiting for transfers between devices  23.9 us (33%)
  Pallas kernels  16.9 us (23%)
  between operations  1.47 us (2%)
    ppermute x5, waiting for transfers between devices, body(): lax.ppermute(m, AXES, lay.y_permutation(py))  17.4 us
    pallas_call x15, Pallas kernels, call(): pl.pallas_call(kernel, out_shape=[jax.ShapeDtypeStruct(shape, dtype) for...  16.9 us
    ppermute x10, starting transfers between devices, body(): lax.ppermute(m, AXES, lay.z_permutation(pz))  13.3 us
    ppermute x5, starting transfers between devices, body(): lax.ppermute(m, AXES, lay.y_permutation(py))  8.34 us
    ppermute x1, starting transfers between devices, spread(): message = jnp.concatenate([message, lax.ppermute(message, AXES, pairs)], 0)  3.96 us
    ppermute x10, starting transfers between devices, body(): d_in = [lax.ppermute(m, AXES, pairs) for m, pairs in zip(d_out, diagonals)]  3.33 us
    ppermute x1, waiting for transfers between devices, body(): theirs = lax.ppermute(theirs, AXES, lay.core_permutation())  1.85 us
    ppermute x1, waiting for transfers between devices, spread(): message = jnp.concatenate([message, lax.ppermute(message, AXES, pairs)], 0)  1.63 us
  transfers between devices with their start and end apart: 29, of which 12 were waited for; matrix products, arithmetic and copies ran while one was open for 0% of the time, Pallas kernels for 10%

profile of v3, /device:TPU:0, one launch (start us, length us, event | category | flops | bytes accessed | tf_op | source)
XLA Modules:
  0.0 72.0 jit_solution(13293557566360951430)
XLA Ops:
  0.6 1.2 %shard_map.163 = (f32[3,8,8,320]{3,2,1,0:T(8,128)S(1)}, f32[3,8,8,320]{3,2,1,0:T(8,128)S(1)}, f32[16,64]{1,0:T(8,128)S(1)}) custom-call(f32[8,8,320]{2,1,0:T(8,128)} %src_now.1, f32[8,8,320]{2,1,0:T(8,128)} %src_prev.1, f32[8,8,320]{2,1,0:T(8,128)} %rec_now.1, f32[8,8,320]{2,1,0:T(8,128)} %rec_prev.1, f32[8,8,320]{2,1,0:T(8,128)} %speed.1, f32[10,64]{1,0:T(8,128)} %traces.1, ...), custom_call_target="tpu_custom_call" | custom-call | tf_op jit(solution)/shard_map/pallas_call | solution.py:513
  2.5 1.1 %collective-permute-done = f32[16,64]{1,0:T(8,128)S(1)} collective-permute-done((f32[16,64]{1,0:T(8,128)S(1)}, f32[16,64]{1,0:T(8,128)S(1)}, u32[]{:S(2)}, u32[]{:S(2)}) %collective-permute-start) | collective-permute-done | bytes 4128 | tf_op jit(solution)/shard_map/ppermute | solution.py:525
  3.7 4.0 %collective-permute-start.1 = (f32[1,16,128]{2,1,0:T(8,128)S(1)}, f32[1,16,128]{2,1,0:T(8,128)S(1)}, u32[]{:S(2)}, u32[]{:S(2)}) collective-permute-start(f32[1,16,128]{2,1,0:T(8,128)S(1)} %maximum_bitcast_fusion), channel_id=1, source_target_pairs={{0,8},{1,9},{2,10},{3,11},{4,12},{5,13},{6,14},{7,15},{8,0},{9,1},... | collective-permute-start | bytes 24584 | tf_op jit(solution)/shard_map/ppermute | solution.py:544
  7.7 1.6 %collective-permute-done.1 = f32[1,16,128]{2,1,0:T(8,128)S(1)} collective-permute-done((f32[1,16,128]{2,1,0:T(8,128)S(1)}, f32[1,16,128]{2,1,0:T(8,128)S(1)}, u32[]{:S(2)}, u32[]{:S(2)}) %collective-permute-start.1) | collective-permute-done | bytes 8224 | tf_op jit(solution)/shard_map/ppermute | solution.py:544
  9.5 2.0 %collective-permute-start.3 = (f32[17,40,128]{2,1,0:T(8,128)S(1)}, f32[17,40,128]{2,1,0:T(8,128)S(1)}, u32[]{:S(2)}, u32[]{:S(2)}) collective-permute-start(f32[17,40,128]{2,1,0:T(8,128)S(1)} %get-tuple-element.59), channel_id=1, source_target_pairs={{0,4},{1,5},{2,6},{3,7},{4,0},{5,1},{6,2},{7,3},{8,12},{9,13},{10,... | collective-permute-start | bytes 1044488 | tf_op jit(solution)/shard_map/ppermute | solution.py:624
  11.5 1.5 %collective-permute-start.5 = (f32[26,24,128]{2,1,0:T(8,128)S(1)}, f32[26,24,128]{2,1,0:T(8,128)S(1)}, u32[]{:S(2)}, u32[]{:S(2)}) collective-permute-start(f32[26,24,128]{2,1,0:T(8,128)S(1)} %get-tuple-element.61), channel_id=1, source_target_pairs={{0,2},{1,3},{2,0},{3,1},{4,6},{5,7},{6,4},{7,5},{8,10},{9,11},{10,... | collective-permute-start | bytes 958472 | tf_op jit(solution)/shard_map/ppermute | solution.py:625
  13.0 3.1 %collective-permute-start.6 = (f32[4,24,128]{2,1,0:T(8,128)S(1)}, f32[4,24,128]{2,1,0:T(8,128)S(1)}, u32[]{:S(2)}, u32[]{:S(2)}) collective-permute-start(f32[4,24,128]{2,1,0:T(8,128)S(1)} %get-tuple-element.66), channel_id=1, source_target_pairs={{0,6},{1,7},{2,4},{3,5},{4,2},{5,3},{6,0},{7,1},{8,14},{9,15},{10,... | collective-permute-start | bytes 147464 | tf_op jit(solution)/shard_map/ppermute | solution.py:627
  16.7 5.7 %collective-permute-done.5.refs_5_.refs_2_ = f32[26,24,128]{2,1,0:T(8,128)S(1)} collective-permute-done((f32[26,24,128]{2,1,0:T(8,128)S(1)}, f32[26,24,128]{2,1,0:T(8,128)S(1)}, u32[]{:S(2)}, u32[]{:S(2)}) %collective-permute-start.5) | collective-permute-done | bytes 319520 | tf_op jit(solution)/shard_map/ppermute | solution.py:625
  22.5 1.4 %shard_map.166 = (f32[16,3,24,128]{3,2,1,0:T(8,128)S(1)}, f32[16,3,24,128]{3,2,1,0:T(8,128)S(1)}) custom-call(f32[8,3,16,128]{3,2,1,0:T(8,128)S(1)} %get-tuple-element.53.refs_0_.refs_5_, f32[8,3,16,128]{3,2,1,0:T(8,128)S(1)} %get-tuple-element.54.refs_1_, f32[8,3,16,128]{3,2,1,0:T(8,128)S(1)} %get-tuple-element.55.refs_2_, ...), custom_call_target="tpu_custom_call" | custom-call | tf_op jit(solution)/shard_map/pallas_call | solution.py:513
  24.4 1.5 %shard_map.168 = (f32[16,3,24,128]{3,2,1,0:T(8,128)S(1)}, f32[10,8,3,16,128]{4,3,2,1,0:T(8,128)S(1)}, f32[8,40,128]{2,1,0:T(8,128)S(1)}, f32[8,24,128]{2,1,0:T(8...) custom-call(f32[10]{0:T(128)S(1)} %copy-done.2, ...), custom_call_target="tpu_custom_call", output_to_operand_aliasing={{0}: (2, {})} | custom-call | tf_op jit(solution)/shard_map/pallas_call | solution.py:513
  25.9 1.7 %collective-permute-start.8 = (f32[8,40,128]{2,1,0:T(8,128)S(1)}, f32[8,40,128]{2,1,0:T(8,128)S(1)}, u32[]{:S(2)}, u32[]{:S(2)}) collective-permute-start(f32[8,40,128]{2,1,0:T(8,128)S(1)} %get-tuple-element.70), channel_id=1, source_target_pairs={{0,4},{1,5},{2,6},{3,7},{4,0},{5,1},{6,2},{7,3},{8,12},{9,13},{10,... | collective-permute-start | bytes 491528 | tf_op jit(solution)/shard_map/ppermute | solution.py:624
  27.6 1.7 %collective-permute-start.10 = (f32[8,24,128]{2,1,0:T(8,128)S(1)}, f32[8,24,128]{2,1,0:T(8,128)S(1)}, u32[]{:S(2)}, u32[]{:S(2)}) collective-permute-start(f32[8,24,128]{2,1,0:T(8,128)S(1)} %get-tuple-element.71), channel_id=1, source_target_pairs={{0,2},{1,3},{2,0},{3,1},{4,6},{5,7},{6,4},{7,5},{8,10},{9,11},{10,... | collective-permute-start | bytes 294920 | tf_op jit(solution)/shard_map/ppermute | solution.py:625
  29.5 2.7 %collective-permute-done.10.refs_5_ = f32[8,24,128]{2,1,0:T(8,128)S(1)} collective-permute-done((f32[8,24,128]{2,1,0:T(8,128)S(1)}, f32[8,24,128]{2,1,0:T(8,128)S(1)}, u32[]{:S(2)}, u32[]{:S(2)}) %collective-permute-start.10) | collective-permute-done | bytes 98336 | tf_op jit(solution)/shard_map/ppermute | solution.py:625
  32.8 1.3 %shard_map.169.refs_2_ = f32[16,3,24,128]{3,2,1,0:T(8,128)S(1)} custom-call(f32[10,8,3,16,128]{4,3,2,1,0:T(8,128)S(1)} %get-tuple-element.68.refs_0_.refs_5_, f32[16,3,24,128]{3,2,1,0:T(8,128)S(1)} %get-tuple-element.69.refs_1_, f32[16,3,24,128]{3,2,1,0:T(8,128)S(1)} %get-tuple-element.64.refs_3_.refs_2_.refs_4_, ...), custom_call_target="tpu_custom_call" | custom-call | tf_op jit(solution)/shard_map/pallas_call | solution.py:513
  34.1 1.5 %shard_map.170 = (f32[16,3,24,128]{3,2,1,0:T(8,128)S(1)}, f32[10,8,3,16,128]{4,3,2,1,0:T(8,128)S(1)}, f32[8,40,128]{2,1,0:T(8,128)S(1)}, f32[8,24,128]{2,1,0:T(8...) custom-call(f32[10]{0:T(128)S(1)} %copy-done.2, ...), custom_call_target="tpu_custom_call", output_to_operand_aliasing={{0}: (2, {}), {1}: (5, {})} | custom-call | tf_op jit(solution)/shard_map/pallas_call | solution.py:513
  35.7 3.6 %collective-permute-start.13 = (f32[8,40,128]{2,1,0:T(8,128)S(1)}, f32[8,40,128]{2,1,0:T(8,128)S(1)}, u32[]{:S(2)}, u32[]{:S(2)}) collective-permute-start(f32[8,40,128]{2,1,0:T(8,128)S(1)} %get-tuple-element.76), channel_id=1, source_target_pairs={{0,4},{1,5},{2,6},{3,7},{4,0},{5,1},{6,2},{7,3},{8,12},{9,13},{10,... | collective-permute-start | bytes 491528 | tf_op jit(solution)/shard_map/ppermute | solution.py:624
  39.3 1.5 %collective-permute-start.15 = (f32[8,24,128]{2,1,0:T(8,128)S(1)}, f32[8,24,128]{2,1,0:T(8,128)S(1)}, u32[]{:S(2)}, u32[]{:S(2)}) collective-permute-start(f32[8,24,128]{2,1,0:T(8,128)S(1)} %get-tuple-element.77), channel_id=1, source_target_pairs={{0,2},{1,3},{2,0},{3,1},{4,6},{5,7},{6,4},{7,5},{8,10},{9,11},{10,... | collective-permute-start | bytes 294920 | tf_op jit(solution)/shard_map/ppermute | solution.py:625
  40.8 3.1 %collective-permute-done.15.refs_5_ = f32[8,24,128]{2,1,0:T(8,128)S(1)} collective-permute-done((f32[8,24,128]{2,1,0:T(8,128)S(1)}, f32[8,24,128]{2,1,0:T(8,128)S(1)}, u32[]{:S(2)}, u32[]{:S(2)}) %collective-permute-start.15) | collective-permute-done | bytes 98336 | tf_op jit(solution)/shard_map/ppermute | solution.py:625
  43.9 1.3 %shard_map.171.refs_2_ = f32[16,3,24,128]{3,2,1,0:T(8,128)S(1)} custom-call(f32[10,8,3,16,128]{4,3,2,1,0:T(8,128)S(1)} %get-tuple-element.74.refs_0_.refs_5_, f32[16,3,24,128]{3,2,1,0:T(8,128)S(1)} %get-tuple-element.75.refs_1_, f32[16,3,24,128]{3,2,1,0:T(8,128)S(1)} %get-tuple-element.64.refs_3_.refs_2_.refs_4_, ...), custom_call_target="tpu_custom_call" | custom-call | tf_op jit(solution)/shard_map/pallas_call | solution.py:513
  45.5 1.5 %shard_map.172 = (f32[16,3,24,128]{3,2,1,0:T(8,128)S(1)}, f32[10,8,3,16,128]{4,3,2,1,0:T(8,128)S(1)}, f32[8,40,128]{2,1,0:T(8,128)S(1)}, f32[8,24,128]{2,1,0:T(8...) custom-call(f32[10]{0:T(128)S(1)} %copy-done.2, ...), custom_call_target="tpu_custom_call", output_to_operand_aliasing={{0}: (2, {}), {1}: (5, {})} | custom-call | tf_op jit(solution)/shard_map/pallas_call | solution.py:513
  47.0 2.1 %collective-permute-start.18 = (f32[8,40,128]{2,1,0:T(8,128)S(1)}, f32[8,40,128]{2,1,0:T(8,128)S(1)}, u32[]{:S(2)}, u32[]{:S(2)}) collective-permute-start(f32[8,40,128]{2,1,0:T(8,128)S(1)} %get-tuple-element.82), channel_id=1, source_target_pairs={{0,4},{1,5},{2,6},{3,7},{4,0},{5,1},{6,2},{7,3},{8,12},{9,13},{10,... | collective-permute-start | bytes 491528 | tf_op jit(solution)/shard_map/ppermute | solution.py:624
  49.1 1.7 %collective-permute-start.20 = (f32[8,24,128]{2,1,0:T(8,128)S(1)}, f32[8,24,128]{2,1,0:T(8,128)S(1)}, u32[]{:S(2)}, u32[]{:S(2)}) collective-permute-start(f32[8,24,128]{2,1,0:T(8,128)S(1)} %get-tuple-element.83), channel_id=1, source_target_pairs={{0,2},{1,3},{2,0},{3,1},{4,6},{5,7},{6,4},{7,5},{8,10},{9,11},{10,... | collective-permute-start | bytes 294920 | tf_op jit(solution)/shard_map/ppermute | solution.py:625
  50.8 3.2 %collective-permute-done.20.refs_5_ = f32[8,24,128]{2,1,0:T(8,128)S(1)} collective-permute-done((f32[8,24,128]{2,1,0:T(8,128)S(1)}, f32[8,24,128]{2,1,0:T(8,128)S(1)}, u32[]{:S(2)}, u32[]{:S(2)}) %collective-permute-start.20) | collective-permute-done | bytes 98336 | tf_op jit(solution)/shard_map/ppermute | solution.py:625
  54.0 1.3 %shard_map.173.refs_2_ = f32[16,3,24,128]{3,2,1,0:T(8,128)S(1)} custom-call(f32[10,8,3,16,128]{4,3,2,1,0:T(8,128)S(1)} %get-tuple-element.80.refs_0_.refs_5_, f32[16,3,24,128]{3,2,1,0:T(8,128)S(1)} %get-tuple-element.81.refs_1_, f32[16,3,24,128]{3,2,1,0:T(8,128)S(1)} %get-tuple-element.64.refs_3_.refs_2_.refs_4_, ...), custom_call_target="tpu_custom_call" | custom-call | tf_op jit(solution)/shard_map/pallas_call | solution.py:513
  55.5 1.7 %shard_map.174 = (f32[16,3,24,128]{3,2,1,0:T(8,128)S(1)}, f32[10,8,3,16,128]{4,3,2,1,0:T(8,128)S(1)}, f32[8,40,128]{2,1,0:T(8,128)S(1)}, f32[8,24,128]{2,1,0:T(8...) custom-call(f32[10]{0:T(128)S(1)} %copy-done.2, ...), custom_call_target="tpu_custom_call", output_to_operand_aliasing={{0}: (2, {}), {1}: (5, {})} | custom-call | tf_op jit(solution)/shard_map/pallas_call | solution.py:513
  57.3 3.7 %collective-permute-start.23 = (f32[8,40,128]{2,1,0:T(8,128)S(1)}, f32[8,40,128]{2,1,0:T(8,128)S(1)}, u32[]{:S(2)}, u32[]{:S(2)}) collective-permute-start(f32[8,40,128]{2,1,0:T(8,128)S(1)} %get-tuple-element.88), channel_id=1, source_target_pairs={{0,4},{1,5},{2,6},{3,7},{4,0},{5,1},{6,2},{7,3},{8,12},{9,13},{10,... | collective-permute-start | bytes 491528 | tf_op jit(solution)/shard_map/ppermute | solution.py:624
  61.0 2.0 %collective-permute-start.25 = (f32[8,24,128]{2,1,0:T(8,128)S(1)}, f32[8,24,128]{2,1,0:T(8,128)S(1)}, u32[]{:S(2)}, u32[]{:S(2)}) collective-permute-start(f32[8,24,128]{2,1,0:T(8,128)S(1)} %get-tuple-element.89), channel_id=1, source_target_pairs={{0,2},{1,3},{2,0},{3,1},{4,6},{5,7},{6,4},{7,5},{8,10},{9,11},{10,... | collective-permute-start | bytes 294920 | tf_op jit(solution)/shard_map/ppermute | solution.py:625
  63.0 2.6 %collective-permute-done.25.refs_5_ = f32[8,24,128]{2,1,0:T(8,128)S(1)} collective-permute-done((f32[8,24,128]{2,1,0:T(8,128)S(1)}, f32[8,24,128]{2,1,0:T(8,128)S(1)}, u32[]{:S(2)}, u32[]{:S(2)}) %collective-permute-start.25) | collective-permute-done | bytes 98336 | tf_op jit(solution)/shard_map/ppermute | solution.py:625
  65.6 1.3 %shard_map.175.refs_3_ = f32[16,3,24,128]{3,2,1,0:T(8,128)S(1)} custom-call(f32[10,8,3,16,128]{4,3,2,1,0:T(8,128)S(1)} %get-tuple-element.86.refs_0_.refs_6_, f32[16,3,24,128]{3,2,1,0:T(8,128)S(1)} %get-tuple-element.87.refs_1_, f32[16,3,24,128]{3,2,1,0:T(8,128)S(1)} %get-tuple-element.64.refs_3_.refs_2_.refs_4_, ...), custom_call_target="tpu_custom_call" | custom-call | tf_op jit(solution)/shard_map/pallas_call | solution.py:513
  67.7 1.5 %shard_map.176 = (f32[16,3,24,128]{3,2,1,0:T(8,128)S(1)}, f32[10,8,3,16,128]{4,3,2,1,0:T(8,128)S(1)}, f32[5,8,3,8,128]{4,3,2,1,0:T(8,128)S(1)}, f32[5,8,3,8,128]{4,3,2,1,0:T(8,128)S(1)}) custom-call(s32[4]{0:T(128)S(1)} %copy-done.3, f32[10]{0:T(128)S(1)} %copy-done.2, s32[1]{0:T(128)S(6)} %copy.42.refs_1_.refs_2_, ...), custom_call_target="tpu_custom_call", output_to_operand_aliasing={{0}: (3, {}), {1}: (6, {})} | custom-call | tf_op jit(solution)/shard_map/pallas_call | solution.py:513
  69.2 1.9 %collective-permute-done.28.theirs = f32[5,8,3,8,128]{4,3,2,1,0:T(8,128)S(1)} collective-permute-done((f32[5,8,3,8,128]{4,3,2,1,0:T(8,128)S(1)}, f32[5,8,3,8,128]{4,3,2,1,0:T(8,128)S(1)}, u32[]{:S(2)}, u32[]{:S(2)}) %collective-permute-start.28) | collective-permute-done | bytes 491552 | tf_op jit(solution)/shard_map/ppermute | solution.py:667
  71.1 0.9 %shard_map.177 = (f32[8,8,320]{2,1,0:T(8,128)}, f32[8,8,320]{2,1,0:T(8,128)}, f32[8,8,320]{2,1,0:T(8,128)}, f32[8,8,320]{2,1,0:T(8,128)}, bf16[4,8,8,320]{3,2,1,0:T(8,128)(2,1)}, /*index=5*/f32[8,8,320]{2,1,0:T(8,128)}) custom-call(f32[5,8,3,8,128]{4,3,2,1,0:T(8,128)S(1)} %get-tuple-element.92.own, f32[5,8,3,8,128]{4,3,2,1,0:T(8,128)S(1)} %collective-permute-done.28.theirs, ...), custom_call_target="tpu_custom_call" | custom-call | tf_op jit(solution)/shard_map/pallas_call | solution.py:513
  (51 shorter events, 3.8 us)
Async XLA Ops:
  1.9 22.5 %copy-start.2 = (f32[10]{0:T(128)S(1)}, f32[10]{0:T(128)}, u32[]{:S(2)}) copy-start(f32[10]{0:T(128)} %refs_1_.5) | copy-start | bytes 124
  1.9 7.4 %collective-permute-start.2 = (f32[3,8,8,320]{3,2,1,0:T(8,128)S(1)}, f32[3,8,8,320]{3,2,1,0:T(8,128)S(1)}, u32[]{:S(2)}, u32[]{:S(2)}) collective-permute-start(f32[3,8,8,320]{3,2,1,0:T(8,128)S(1)} %get-tuple-element.52), channel_id=1, source_target_pairs={{0,1},{1,0},{2,3},{3,2},{4,5},{5,4},{6,7},{7,6},{8,9},{9,8},{10,11... | collective-permute-start | bytes 737288 | tf_op jit(solution)/shard_map/ppermute | solution.py:584
  2.4 1.2 %collective-permute-start = (f32[16,64]{1,0:T(8,128)S(1)}, f32[16,64]{1,0:T(8,128)S(1)}, u32[]{:S(2)}, u32[]{:S(2)}) collective-permute-start(f32[16,64]{1,0:T(8,128)S(1)} %get-tuple-element.50), channel_id=1, source_target_pairs={{0,1},{1,0},{2,3},{3,2},{4,5},{5,4},{6,7},{7,6},{8,9},{9,8},{10,11... | collective-permute-start | bytes 12296 | tf_op jit(solution)/shard_map/ppermute | solution.py:525
  3.7 5.6 %collective-permute-start.1 = (f32[1,16,128]{2,1,0:T(8,128)S(1)}, f32[1,16,128]{2,1,0:T(8,128)S(1)}, u32[]{:S(2)}, u32[]{:S(2)}) collective-permute-start(f32[1,16,128]{2,1,0:T(8,128)S(1)} %maximum_bitcast_fusion), channel_id=1, source_target_pairs={{0,8},{1,9},{2,10},{3,11},{4,12},{5,13},{6,14},{7,15},{8,0},{9,1},... | collective-permute-start | bytes 24584 | tf_op jit(solution)/shard_map/ppermute | solution.py:544
  9.5 13.0 %collective-permute-start.3 = (f32[17,40,128]{2,1,0:T(8,128)S(1)}, f32[17,40,128]{2,1,0:T(8,128)S(1)}, u32[]{:S(2)}, u32[]{:S(2)}) collective-permute-start(f32[17,40,128]{2,1,0:T(8,128)S(1)} %get-tuple-element.59), channel_id=1, source_target_pairs={{0,4},{1,5},{2,6},{3,7},{4,0},{5,1},{6,2},{7,3},{8,12},{9,13},{10,... | collective-permute-start | bytes 1044488 | tf_op jit(solution)/shard_map/ppermute | solution.py:624
  11.5 11.0 %collective-permute-start.4 = (f32[16,40,128]{2,1,0:T(8,128)S(1)}, f32[16,40,128]{2,1,0:T(8,128)S(1)}, u32[]{:S(2)}, u32[]{:S(2)}) collective-permute-start(f32[16,40,128]{2,1,0:T(8,128)S(1)} %get-tuple-element.60), channel_id=1, source_target_pairs={{0,1},{1,0},{2,3},{3,2},{4,8},{5,9},{6,10},{7,11},{8,4},{9,5},{10,... | collective-permute-start | bytes 983048 | tf_op jit(solution)/shard_map/ppermute | solution.py:624
  11.5 11.0 %collective-permute-start.5 = (f32[26,24,128]{2,1,0:T(8,128)S(1)}, f32[26,24,128]{2,1,0:T(8,128)S(1)}, u32[]{:S(2)}, u32[]{:S(2)}) collective-permute-start(f32[26,24,128]{2,1,0:T(8,128)S(1)} %get-tuple-element.61), channel_id=1, source_target_pairs={{0,2},{1,3},{2,0},{3,1},{4,6},{5,7},{6,4},{7,5},{8,10},{9,11},{10,... | collective-permute-start | bytes 958472 | tf_op jit(solution)/shard_map/ppermute | solution.py:625
  13.0 10.9 %collective-permute-start.6 = (f32[4,24,128]{2,1,0:T(8,128)S(1)}, f32[4,24,128]{2,1,0:T(8,128)S(1)}, u32[]{:S(2)}, u32[]{:S(2)}) collective-permute-start(f32[4,24,128]{2,1,0:T(8,128)S(1)} %get-tuple-element.66), channel_id=1, source_target_pairs={{0,6},{1,7},{2,4},{3,5},{4,2},{5,3},{6,0},{7,1},{8,14},{9,15},{10,... | collective-permute-start | bytes 147464 | tf_op jit(solution)/shard_map/ppermute | solution.py:627
  16.1 8.3 %collective-permute-start.7 = (f32[2,24,128]{2,1,0:T(8,128)S(1)}, f32[2,24,128]{2,1,0:T(8,128)S(1)}, u32[]{:S(2)}, u32[]{:S(2)}) collective-permute-start(f32[2,24,128]{2,1,0:T(8,128)S(1)} %get-tuple-element.67), channel_id=1, source_target_pairs={{0,1},{1,0},{2,3},{3,2},{4,10},{5,11},{6,8},{7,9},{8,6},{9,7},{10,... | collective-permute-start | bytes 73736 | tf_op jit(solution)/shard_map/ppermute | solution.py:627
  25.8 6.4 %collective-permute-start.9 = (f32[8,40,128]{2,1,0:T(8,128)S(1)}, f32[8,40,128]{2,1,0:T(8,128)S(1)}, u32[]{:S(2)}, u32[]{:S(2)}) collective-permute-start(f32[8,40,128]{2,1,0:T(8,128)S(1)} %get-tuple-element.70), channel_id=1, source_target_pairs={{0,1},{1,0},{2,3},{3,2},{4,8},{5,9},{6,10},{7,11},{8,4},{9,5},{10,... | collective-permute-start | bytes 491528 | tf_op jit(solution)/shard_map/ppermute | solution.py:624
  25.9 6.9 %collective-permute-start.8 = (f32[8,40,128]{2,1,0:T(8,128)S(1)}, f32[8,40,128]{2,1,0:T(8,128)S(1)}, u32[]{:S(2)}, u32[]{:S(2)}) collective-permute-start(f32[8,40,128]{2,1,0:T(8,128)S(1)} %get-tuple-element.70), channel_id=1, source_target_pairs={{0,4},{1,5},{2,6},{3,7},{4,0},{5,1},{6,2},{7,3},{8,12},{9,13},{10,... | collective-permute-start | bytes 491528 | tf_op jit(solution)/shard_map/ppermute | solution.py:624
  27.6 4.6 %collective-permute-start.10 = (f32[8,24,128]{2,1,0:T(8,128)S(1)}, f32[8,24,128]{2,1,0:T(8,128)S(1)}, u32[]{:S(2)}, u32[]{:S(2)}) collective-permute-start(f32[8,24,128]{2,1,0:T(8,128)S(1)} %get-tuple-element.71), channel_id=1, source_target_pairs={{0,2},{1,3},{2,0},{3,1},{4,6},{5,7},{6,4},{7,5},{8,10},{9,11},{10,... | collective-permute-start | bytes 294920 | tf_op jit(solution)/shard_map/ppermute | solution.py:625
  29.3 4.8 %collective-permute-start.11 = (f32[2,24,128]{2,1,0:T(8,128)S(1)}, f32[2,24,128]{2,1,0:T(8,128)S(1)}, u32[]{:S(2)}, u32[]{:S(2)}) collective-permute-start(f32[2,24,128]{2,1,0:T(8,128)S(1)} %get-tuple-element.72), channel_id=1, source_target_pairs={{0,6},{1,7},{2,4},{3,5},{4,2},{5,3},{6,0},{7,1},{8,14},{9,15},{10,... | collective-permute-start | bytes 73736 | tf_op jit(solution)/shard_map/ppermute | solution.py:627
  29.5 4.6 %collective-permute-start.12 = (f32[2,24,128]{2,1,0:T(8,128)S(1)}, f32[2,24,128]{2,1,0:T(8,128)S(1)}, u32[]{:S(2)}, u32[]{:S(2)}) collective-permute-start(f32[2,24,128]{2,1,0:T(8,128)S(1)} %get-tuple-element.73), channel_id=1, source_target_pairs={{0,1},{1,0},{2,3},{3,2},{4,10},{5,11},{6,8},{7,9},{8,6},{9,7},{10,... | collective-permute-start | bytes 73736 | tf_op jit(solution)/shard_map/ppermute | solution.py:627
  35.6 8.3 %collective-permute-start.14 = (f32[8,40,128]{2,1,0:T(8,128)S(1)}, f32[8,40,128]{2,1,0:T(8,128)S(1)}, u32[]{:S(2)}, u32[]{:S(2)}) collective-permute-start(f32[8,40,128]{2,1,0:T(8,128)S(1)} %get-tuple-element.76), channel_id=1, source_target_pairs={{0,1},{1,0},{2,3},{3,2},{4,8},{5,9},{6,10},{7,11},{8,4},{9,5},{10,... | collective-permute-start | bytes 491528 | tf_op jit(solution)/shard_map/ppermute | solution.py:624
  35.7 8.2 %collective-permute-start.13 = (f32[8,40,128]{2,1,0:T(8,128)S(1)}, f32[8,40,128]{2,1,0:T(8,128)S(1)}, u32[]{:S(2)}, u32[]{:S(2)}) collective-permute-start(f32[8,40,128]{2,1,0:T(8,128)S(1)} %get-tuple-element.76), channel_id=1, source_target_pairs={{0,4},{1,5},{2,6},{3,7},{4,0},{5,1},{6,2},{7,3},{8,12},{9,13},{10,... | collective-permute-start | bytes 491528 | tf_op jit(solution)/shard_map/ppermute | solution.py:624
  39.3 4.6 %collective-permute-start.15 = (f32[8,24,128]{2,1,0:T(8,128)S(1)}, f32[8,24,128]{2,1,0:T(8,128)S(1)}, u32[]{:S(2)}, u32[]{:S(2)}) collective-permute-start(f32[8,24,128]{2,1,0:T(8,128)S(1)} %get-tuple-element.77), channel_id=1, source_target_pairs={{0,2},{1,3},{2,0},{3,1},{4,6},{5,7},{6,4},{7,5},{8,10},{9,11},{10,... | collective-permute-start | bytes 294920 | tf_op jit(solution)/shard_map/ppermute | solution.py:625
  40.8 4.7 %collective-permute-start.16 = (f32[2,24,128]{2,1,0:T(8,128)S(1)}, f32[2,24,128]{2,1,0:T(8,128)S(1)}, u32[]{:S(2)}, u32[]{:S(2)}) collective-permute-start(f32[2,24,128]{2,1,0:T(8,128)S(1)} %get-tuple-element.78), channel_id=1, source_target_pairs={{0,6},{1,7},{2,4},{3,5},{4,2},{5,3},{6,0},{7,1},{8,14},{9,15},{10,... | collective-permute-start | bytes 73736 | tf_op jit(solution)/shard_map/ppermute | solution.py:627
  40.8 4.7 %collective-permute-start.17 = (f32[2,24,128]{2,1,0:T(8,128)S(1)}, f32[2,24,128]{2,1,0:T(8,128)S(1)}, u32[]{:S(2)}, u32[]{:S(2)}) collective-permute-start(f32[2,24,128]{2,1,0:T(8,128)S(1)} %get-tuple-element.79), channel_id=1, source_target_pairs={{0,1},{1,0},{2,3},{3,2},{4,10},{5,11},{6,8},{7,9},{8,6},{9,7},{10,... | collective-permute-start | bytes 73736 | tf_op jit(solution)/shard_map/ppermute | solution.py:627
  47.0 7.0 %collective-permute-start.19 = (f32[8,40,128]{2,1,0:T(8,128)S(1)}, f32[8,40,128]{2,1,0:T(8,128)S(1)}, u32[]{:S(2)}, u32[]{:S(2)}) collective-permute-start(f32[8,40,128]{2,1,0:T(8,128)S(1)} %get-tuple-element.82), channel_id=1, source_target_pairs={{0,1},{1,0},{2,3},{3,2},{4,8},{5,9},{6,10},{7,11},{8,4},{9,5},{10,... | collective-permute-start | bytes 491528 | tf_op jit(solution)/shard_map/ppermute | solution.py:624
  47.0 6.9 %collective-permute-start.18 = (f32[8,40,128]{2,1,0:T(8,128)S(1)}, f32[8,40,128]{2,1,0:T(8,128)S(1)}, u32[]{:S(2)}, u32[]{:S(2)}) collective-permute-start(f32[8,40,128]{2,1,0:T(8,128)S(1)} %get-tuple-element.82), channel_id=1, source_target_pairs={{0,4},{1,5},{2,6},{3,7},{4,0},{5,1},{6,2},{7,3},{8,12},{9,13},{10,... | collective-permute-start | bytes 491528 | tf_op jit(solution)/shard_map/ppermute | solution.py:624
  49.1 4.9 %collective-permute-start.20 = (f32[8,24,128]{2,1,0:T(8,128)S(1)}, f32[8,24,128]{2,1,0:T(8,128)S(1)}, u32[]{:S(2)}, u32[]{:S(2)}) collective-permute-start(f32[8,24,128]{2,1,0:T(8,128)S(1)} %get-tuple-element.83), channel_id=1, source_target_pairs={{0,2},{1,3},{2,0},{3,1},{4,6},{5,7},{6,4},{7,5},{8,10},{9,11},{10,... | collective-permute-start | bytes 294920 | tf_op jit(solution)/shard_map/ppermute | solution.py:625
  50.8 4.7 %collective-permute-start.21 = (f32[2,24,128]{2,1,0:T(8,128)S(1)}, f32[2,24,128]{2,1,0:T(8,128)S(1)}, u32[]{:S(2)}, u32[]{:S(2)}) collective-permute-start(f32[2,24,128]{2,1,0:T(8,128)S(1)} %get-tuple-element.84), channel_id=1, source_target_pairs={{0,6},{1,7},{2,4},{3,5},{4,2},{5,3},{6,0},{7,1},{8,14},{9,15},{10,... | collective-permute-start | bytes 73736 | tf_op jit(solution)/shard_map/ppermute | solution.py:627
  50.8 4.7 %collective-permute-start.22 = (f32[2,24,128]{2,1,0:T(8,128)S(1)}, f32[2,24,128]{2,1,0:T(8,128)S(1)}, u32[]{:S(2)}, u32[]{:S(2)}) collective-permute-start(f32[2,24,128]{2,1,0:T(8,128)S(1)} %get-tuple-element.85), channel_id=1, source_target_pairs={{0,1},{1,0},{2,3},{3,2},{4,10},{5,11},{6,8},{7,9},{8,6},{9,7},{10,... | collective-permute-start | bytes 73736 | tf_op jit(solution)/shard_map/ppermute | solution.py:627
  57.2 8.4 %collective-permute-start.24 = (f32[8,40,128]{2,1,0:T(8,128)S(1)}, f32[8,40,128]{2,1,0:T(8,128)S(1)}, u32[]{:S(2)}, u32[]{:S(2)}) collective-permute-start(f32[8,40,128]{2,1,0:T(8,128)S(1)} %get-tuple-element.88), channel_id=1, source_target_pairs={{0,1},{1,0},{2,3},{3,2},{4,8},{5,9},{6,10},{7,11},{8,4},{9,5},{10,... | collective-permute-start | bytes 491528 | tf_op jit(solution)/shard_map/ppermute | solution.py:624
  57.3 8.3 %collective-permute-start.23 = (f32[8,40,128]{2,1,0:T(8,128)S(1)}, f32[8,40,128]{2,1,0:T(8,128)S(1)}, u32[]{:S(2)}, u32[]{:S(2)}) collective-permute-start(f32[8,40,128]{2,1,0:T(8,128)S(1)} %get-tuple-element.88), channel_id=1, source_target_pairs={{0,4},{1,5},{2,6},{3,7},{4,0},{5,1},{6,2},{7,3},{8,12},{9,13},{10,... | collective-permute-start | bytes 491528 | tf_op jit(solution)/shard_map/ppermute | solution.py:624
  61.0 4.6 %collective-permute-start.25 = (f32[8,24,128]{2,1,0:T(8,128)S(1)}, f32[8,24,128]{2,1,0:T(8,128)S(1)}, u32[]{:S(2)}, u32[]{:S(2)}) collective-permute-start(f32[8,24,128]{2,1,0:T(8,128)S(1)} %get-tuple-element.89), channel_id=1, source_target_pairs={{0,2},{1,3},{2,0},{3,1},{4,6},{5,7},{6,4},{7,5},{8,10},{9,11},{10,... | collective-permute-start | bytes 294920 | tf_op jit(solution)/shard_map/ppermute | solution.py:625
  63.0 4.7 %collective-permute-start.26 = (f32[2,24,128]{2,1,0:T(8,128)S(1)}, f32[2,24,128]{2,1,0:T(8,128)S(1)}, u32[]{:S(2)}, u32[]{:S(2)}) collective-permute-start(f32[2,24,128]{2,1,0:T(8,128)S(1)} %get-tuple-element.90), channel_id=1, source_target_pairs={{0,6},{1,7},{2,4},{3,5},{4,2},{5,3},{6,0},{7,1},{8,14},{9,15},{10,... | collective-permute-start | bytes 73736 | tf_op jit(solution)/shard_map/ppermute | solution.py:627
  63.0 4.7 %collective-permute-start.27 = (f32[2,24,128]{2,1,0:T(8,128)S(1)}, f32[2,24,128]{2,1,0:T(8,128)S(1)}, u32[]{:S(2)}, u32[]{:S(2)}) collective-permute-start(f32[2,24,128]{2,1,0:T(8,128)S(1)} %get-tuple-element.91), channel_id=1, source_target_pairs={{0,1},{1,0},{2,3},{3,2},{4,10},{5,11},{6,8},{7,9},{8,6},{9,7},{10,... | collective-permute-start | bytes 73736 | tf_op jit(solution)/shard_map/ppermute | solution.py:627
  66.9 4.1 %copy-start = (bf16[4,8,8,320]{3,2,1,0:T(8,128)(2,1)S(1)}, bf16[4,8,8,320]{3,2,1,0:T(8,128)(2,1)}, u32[]{:S(2)}) copy-start(bf16[4,8,8,320]{3,2,1,0:T(8,128)(2,1)} %stored.1) | copy-start | bytes 491524
  67.0 4.1 %copy-start.1 = (f32[8,8,320]{2,1,0:T(8,128)S(1)}, f32[8,8,320]{2,1,0:T(8,128)}, u32[]{:S(2)}) copy-start(f32[8,8,320]{2,1,0:T(8,128)} %image_before.1) | copy-start | bytes 245764
  69.2 1.9 %collective-permute-start.28 = (f32[5,8,3,8,128]{4,3,2,1,0:T(8,128)S(1)}, f32[5,8,3,8,128]{4,3,2,1,0:T(8,128)S(1)}, u32[]{:S(2)}, u32[]{:S(2)}) collective-permute-start(f32[5,8,3,8,128]{4,3,2,1,0:T(8,128)S(1)} %get-tuple-element.93), channel_id=1, source_target_pairs={{0,1},{1,0},{2,3},{3,2},{4,5},{5,4},{6,7},{7,6},{8,9},{9,8},{10,11... | collective-permute-start | bytes 1474568 | tf_op jit(solution)/shard_map/ppermute | solution.py:667
  (1 other events, 2.1 us)

commit v4 on v3

--- a/solution.py
+++ b/solution.py
@@ -68,8 +68,7 @@
     def spot(self, message, start, group, part):
         chunk = group * (self.trace_rows // ROWS) + part
         per_plane = message.shape[1] // ROWS
-        row = chunk % per_plane * ROWS
-        return start + chunk // per_plane, row if isinstance(row, int) else pl.multiple_of(row, ROWS)
+        return start + chunk // per_plane, chunk % per_plane * ROWS
 
     def core_permutation(self):
         return self.permutation(lambda x, c: (-1, -1))
@@ -226,9 +225,18 @@
                 message[plane, row : row + ROWS, :] = groups[group, part * ROWS : (part + 1) * ROWS, :]
 
 
-def planes_kernel(lay, *refs):
-    groups, messages, (planes, total) = refs[0], refs[1:-2], refs[-2:]
-    carriers = lay.carriers(*lay.by_kind(messages))
+def extract_kernel(lay, *refs):
+    groups, messages, out = refs[1], refs[2:-1], refs[-1]
+    count = groups.shape[0]
+    out[0:count] = groups[...]
+    for index, (message, start) in enumerate(lay.carriers(*lay.by_kind(messages))):
+        for group in range(count):
+            for part in range(lay.trace_rows // ROWS):
+                plane, row = lay.spot(message, start, group, part)
+                out[(index + 1) * count + group, part * ROWS : (part + 1) * ROWS, :] = message[plane, row : row + ROWS, :]
+
+
+def planes_kernel(lay, groups, planes, total):
     gx, column, core = lay.place()
     start_x, start_y = gx * lay.bx - REACH, column * lay.cy - REACH
     cells = lay.ex * lay.ey
@@ -252,17 +260,11 @@
             chosen, parts, (((1,), (1,)), ((), ())), preferred_element_type=jnp.float32
         )
 
-    def add_groups(group, carry):
+    def add_group(group, carry):
         add(groups[group])
-        for message, start in carriers:
-            parts = []
-            for part in range(padded // ROWS):
-                plane, row = lay.spot(message, start, group, part)
-                parts.append(message[plane, pl.ds(row, ROWS), :])
-            add(jnp.concatenate(parts, 0))
         return carry
 
-    lax.fori_loop(0, groups.shape[0], add_groups, 0, unroll=groups.shape[0] <= 2)
+    lax.fori_loop(0, groups.shape[0], add_group, 0, unroll=groups.shape[0] <= 2 * ROWS)
     summed = total[...]
     summed = (
         summed + pltpu.roll(summed, LANES - padded, 1) + pltpu.roll(summed, LANES - 2 * padded, 1)
@@ -412,8 +414,7 @@
 def round_kernel(lay, time, *refs):
     nz, ny = len(lay.z_parities), len(lay.y_parities)
     last = time + 2 == lay.steps
-    plan, refs = (refs[0], refs[1:]) if last else (None, refs)
-    (wavelet, source_cell, stepped, s, planes, p), refs = refs[:6], refs[6:]
+    (source_cell, plan, wavelet, stepped, s, planes, p), refs = refs[:7], refs[7:]
     d_in, refs = refs[: nz * ny], refs[nz * ny :]
     (field, history), refs = refs[:2], refs[2:]
     corner = refs[-1]
@@ -448,7 +449,7 @@
         add_corner(lay, field, s, message, right, high, valid, corner)
     for x in range(lay.ex):
         field[x, 0] += s[x, 0] * injected(x, lay.ey, 0, lay.steps - 1 - time)
-    add_source(field, lambda x, t: s[x, t], source_x + REACH, source_y + REACH, lay.ex, lay.ey, wavelet[time])
+    add_source(field, lambda x, t: s[x, t], source_x + REACH, source_y + REACH, lay.ex, lay.ey, wavelet[:, time : time + 1])
 
     for x in range(bx):
         speed = [s[x + REACH, t, REACH : REACH + cy, :] for t in range(zt)]
@@ -458,18 +459,31 @@
             latest[x, t] = out[t]
             history[time, x, t] = field[x + REACH, t, REACH : REACH + cy, :]
     add_source(
-        latest, lambda x, t: s[x + REACH, t, REACH : REACH + cy, :], source_x, source_y, bx, cy, wavelet[time + 1]
+        latest, lambda x, t: s[x + REACH, t, REACH : REACH + cy, :], source_x, source_y, bx, cy, wavelet[:, time + 1 : time + 2]
     )
 
     if last:
         own, theirs = refs[:2]
-        kept = [lay.steps - 2, lay.steps - 1, 0]
+
+        def kept(index, x, t):
+            if index < 3:
+                return history[(lay.steps - 2, lay.steps - 1, 0)[index], x, t]
+            slot = index - 2
+            rows = history[slot, x, t]
+            for moment in range(slot + 1, lay.steps - lay.slots + slot + 1):
+                rows = jnp.where(moments[slot] == moment, history[moment, x, t], rows)
+            return rows
+
+        moments = {}
         for slot in range(1, lay.slots - 1):
-            kept.append(jnp.where(core == 0, plan[slot], lay.steps - 1 - plan[lay.slots - 1 - slot]))
-        for index, moment in enumerate(kept):
+            mirrored = lay.slots - 1 - slot
+            moment = jnp.where(core == 0, plan[:, slot : slot + 1], lay.steps - 1 - plan[:, mirrored : mirrored + 1])
+            moments[slot] = jnp.broadcast_to(moment, (cy, LANES))
+        for index in range(lay.slots + 1):
             for x in range(bx):
                 for t in range(zt):
-                    low, high = history[moment, x, t, 0 : lay.by, :], history[moment, x, t, lay.by : cy, :]
+                    rows = kept(index, x, t)
+                    low, high = rows[0 : lay.by], rows[lay.by :]
                     own[index, x, t] = jnp.where(core == 0, low, high)
                     theirs[index, x, t] = jnp.where(core == 0, high, low)
     else:
@@ -583,8 +597,6 @@
     )
     swapped = lax.ppermute(swapped, AXES, lay.core_permutation())
     groups = share_in_chip(lay, message)
-    groups = spread(lay, groups)
-
     block = (lay.bx, lay.zt, lay.cy, LANES)
     ext = (lay.ex, lay.zt, lay.ey, LANES)
     field = (lay.bx + 2 * HALO, lay.zt, lay.cy + 2 * HALO, LANES)
@@ -625,6 +637,16 @@
         y_in = [lax.ppermute(m, AXES, lay.y_permutation(py)) for m, py in zip(y_out, lay.y_parities)]
         diagonals = [lay.d_permutation(pz, py) for pz in lay.z_parities for py in lay.y_parities]
         d_in = [lax.ppermute(m, AXES, pairs) for m, pairs in zip(d_out, diagonals)]
+        if begin:
+            d_in = list(lax.optimization_barrier(tuple(d_in)))
+            carried = z_in[:1] + y_in[:1] + d_in[:1]
+            (gathered,) = call(
+                functools.partial(extract_kernel, lay),
+                [((groups.shape[0] * (1 + len(carried)), *groups.shape[1:]), f32)],
+                [source_cell, groups, *carried],
+                scalars=1,
+            )
+            gathered = spread(lay, gathered)
         made = call(
             functools.partial(side_kernel, lay, time),
             [(ext, f32)] * (2 if begin else 1),
@@ -634,12 +656,11 @@
         stepped = made[0]
         if begin:
             s = made[1]
-            groups, stepped = lax.optimization_barrier((groups, stepped))
-            carried = z_in[:1] + y_in[:1] + d_in[:1]
+            gathered, stepped = lax.optimization_barrier((gathered, stepped))
             (planes,) = call(
                 functools.partial(planes_kernel, lay),
                 [((lay.ex, lay.ey, LANES), f32)],
-                [groups, *carried],
+                [gathered],
                 [pltpu.VMEM((lay.ex * lay.ey, LANES), f32)],
             )
         outs = [(ext, f32), ((steps, *block), f32)]
@@ -647,15 +668,13 @@
             outs += [((slots + 1, lay.bx, lay.zt, lay.by, LANES), f32)] * 2
         else:
             outs += [(z_shape, f32)] + [(y_shape, f32)] * ny + [(d_shape, f32)] * (nz * ny)
-        scalars = [plan] * end + [wavelet, source_cell]
-        operands = scalars + [stepped, s, planes, p, *d_in]
         made = call(
             functools.partial(round_kernel, lay, time),
             outs,
-            operands,
+            [source_cell, plan[None], wavelet[None], stepped, s, planes, p, *d_in],
             [pltpu.VMEM((REACH, lay.zt, 3 * ROWS, LANES), f32)],
-            scalars=len(scalars),
-            aliases={len(scalars): 0} | ({} if begin else {len(scalars) + 3: 1}),
+            scalars=1,
+            aliases={3: 0} | ({} if begin else {6: 1}),
         )
         q, p = made[:2]
         if end:

time: 72.2 us -> 68.5 us (0.949)
  Pallas kernels: 16.9 us -> 14.4 us
  waiting for transfers between devices: 23.9 us -> 21.9 us
  starting transfers between devices: 29.6 us -> 30.7 us
    ppermute x5, waiting for transfers between devices: 17.4 us -> 13 us  [body(): lax.ppermute(m, AXES, lay.y_permutation(py))]
    ppermute x10, waiting for transfers between devices: 1.25 us -> 5.28 us  [body(): d_in = [lax.ppermute(m, AXES, pairs) for m, pairs in zip(d_out, diagonals)]]
    ppermute x10, starting transfers between devices: 13.3 us -> 15.9 us  [body(): lax.ppermute(m, AXES, lay.z_permutation(pz))]
    pallas_call x15 -> x16, Pallas kernels: 16.9 us -> 14.4 us  [call(): pl.pallas_call(kernel, out_shape=[jax.ShapeDtypeStruct(shape, dtype) for...]
    ppermute x5, starting transfers between devices: 8.34 us -> 6.4 us  [body(): lax.ppermute(m, AXES, lay.y_permutation(py))]
    ppermute x1, waiting for transfers between devices: 1.63 us -> 0.52 us  [spread(): message = jnp.concatenate([message, lax.ppermute(message, AXES, pairs)], 0)]
    ppermute x10, starting transfers between devices: 3.33 us -> 4.16 us  [body(): d_in = [lax.ppermute(m, AXES, pairs) for m, pairs in zip(d_out, diagonals)]]
  transfers between devices with their start and end apart: 29 -> 29, of which waited for: 12 -> 10; matrix products, arithmetic and copies ran while one was open for 0% -> 0% of each run, Pallas kernels for 10% -> 10%
where the time goes in v4:
time: 68.5 us
  starting transfers between devices  30.7 us (45%)
  waiting for transfers between devices  21.9 us (32%)
  Pallas kernels  14.4 us (21%)
  between operations  1.49 us (2%)
    ppermute x10, starting transfers between devices, body(): lax.ppermute(m, AXES, lay.z_permutation(pz))  15.9 us
    pallas_call x16, Pallas kernels, call(): pl.pallas_call(kernel, out_shape=[jax.ShapeDtypeStruct(shape, dtype) for...  14.4 us
    ppermute x5, waiting for transfers between devices, body(): lax.ppermute(m, AXES, lay.y_permutation(py))  13 us
    ppermute x5, starting transfers between devices, body(): lax.ppermute(m, AXES, lay.y_permutation(py))  6.4 us
    ppermute x10, waiting for transfers between devices, body(): d_in = [lax.ppermute(m, AXES, pairs) for m, pairs in zip(d_out, diagonals)]  5.28 us
    ppermute x10, starting transfers between devices, body(): d_in = [lax.ppermute(m, AXES, pairs) for m, pairs in zip(d_out, diagonals)]  4.16 us
    ppermute x1, starting transfers between devices, spread(): message = jnp.concatenate([message, lax.ppermute(message, AXES, pairs)], 0)  3.52 us
    ppermute x1, waiting for transfers between devices, body(): theirs = lax.ppermute(theirs, AXES, lay.core_permutation())  1.85 us
  transfers between devices with their start and end apart: 29, of which 10 were waited for; matrix products, arithmetic and copies ran while one was open for 0% of the time, Pallas kernels for 10%

profile of v4, /device:TPU:0, one launch (start us, length us, event | category | flops | bytes accessed | tf_op | source)
XLA Modules:
  0.0 68.5 jit_solution(14301372097135967242)
XLA Ops:
  0.6 1.2 %shard_map.163 = (f32[3,8,8,320]{3,2,1,0:T(8,128)S(1)}, f32[3,8,8,320]{3,2,1,0:T(8,128)S(1)}, f32[16,64]{1,0:T(8,128)S(1)}) custom-call(f32[8,8,320]{2,1,0:T(8,128)} %src_now.1, f32[8,8,320]{2,1,0:T(8,128)} %src_prev.1, f32[8,8,320]{2,1,0:T(8,128)} %rec_now.1, f32[8,8,320]{2,1,0:T(8,128)} %rec_prev.1, f32[8,8,320]{2,1,0:T(8,128)} %speed.1, f32[10,64]{1,0:T(8,128)} %traces.1, ...), custom_call_target="tpu_custom_call" | custom-call | tf_op jit(solution)/shard_map/pallas_call | solution.py:527
  2.5 1.1 %collective-permute-done = f32[16,64]{1,0:T(8,128)S(1)} collective-permute-done((f32[16,64]{1,0:T(8,128)S(1)}, f32[16,64]{1,0:T(8,128)S(1)}, u32[]{:S(2)}, u32[]{:S(2)}) %collective-permute-start) | collective-permute-done | bytes 4128 | tf_op jit(solution)/shard_map/ppermute | solution.py:539
  3.9 3.0 %collective-permute-start.2 = (f32[17,40,128]{2,1,0:T(8,128)S(1)}, f32[17,40,128]{2,1,0:T(8,128)S(1)}, u32[]{:S(2)}, u32[]{:S(2)}) collective-permute-start(f32[17,40,128]{2,1,0:T(8,128)S(1)} %get-tuple-element.58), channel_id=1, source_target_pairs={{0,4},{1,5},{2,6},{3,7},{4,0},{5,1},{6,2},{7,3},{8,12},{9,13},{10,... | collective-permute-start | bytes 1044488 | tf_op jit(solution)/shard_map/ppermute | solution.py:636
  6.9 1.5 %collective-permute-start.3 = (f32[25,24,128]{2,1,0:T(8,128)S(1)}, f32[25,24,128]{2,1,0:T(8,128)S(1)}, u32[]{:S(2)}, u32[]{:S(2)}) collective-permute-start(f32[25,24,128]{2,1,0:T(8,128)S(1)} %get-tuple-element.59), channel_id=1, source_target_pairs={{0,2},{1,3},{2,0},{3,1},{4,6},{5,7},{6,4},{7,5},{8,10},{9,11},{10,... | collective-permute-start | bytes 921608 | tf_op jit(solution)/shard_map/ppermute | solution.py:637
  8.4 3.1 %collective-permute-start.4 = (f32[3,24,128]{2,1,0:T(8,128)S(1)}, f32[3,24,128]{2,1,0:T(8,128)S(1)}, u32[]{:S(2)}, u32[]{:S(2)}) collective-permute-start(f32[3,24,128]{2,1,0:T(8,128)S(1)} %get-tuple-element.60), channel_id=1, source_target_pairs={{0,6},{1,7},{2,4},{3,5},{4,2},{5,3},{6,0},{7,1},{8,14},{9,15},{10,... | collective-permute-start | bytes 110600 | tf_op jit(solution)/shard_map/ppermute | solution.py:639
  12.2 0.5 collective-permute-done.5.refs_8_
  12.7 4.5 %collective-permute-done.4.refs_4_.refs_7_ = f32[3,24,128]{2,1,0:T(8,128)S(1)} collective-permute-done((f32[3,24,128]{2,1,0:T(8,128)S(1)}, f32[3,24,128]{2,1,0:T(8,128)S(1)}, u32[]{:S(2)}, u32[]{:S(2)}) %collective-permute-start.4) | collective-permute-done | bytes 36896 | tf_op jit(solution)/shard_map/ppermute | solution.py:639
  17.2 3.5 %collective-permute-start.6 = (f32[4,16,128]{2,1,0:T(8,128)S(1)}, f32[4,16,128]{2,1,0:T(8,128)S(1)}, u32[]{:S(2)}, u32[]{:S(2)}) collective-permute-start(f32[4,16,128]{2,1,0:T(8,128)S(1)} %shard_map.166), channel_id=1, source_target_pairs={{0,8},{1,9},{2,10},{3,11},{4,12},{5,13},{6,14},{7,15},{8,0},{9,1},... | collective-permute-start | bytes 98312 | tf_op jit(solution)/shard_map/ppermute | solution.py:558
  20.8 1.4 %shard_map.167 = (f32[16,3,24,128]{3,2,1,0:T(8,128)S(1)}, f32[16,3,24,128]{3,2,1,0:T(8,128)S(1)}) custom-call(f32[8,3,16,128]{3,2,1,0:T(8,128)S(1)} %get-tuple-element.63.refs_0_.refs_6_, f32[8,3,16,128]{3,2,1,0:T(8,128)S(1)} %get-tuple-element.64.refs_1_, f32[8,3,16,128]{3,2,1,0:T(8,128)S(1)} %get-tuple-element.65.refs_2_, ...), custom_call_target="tpu_custom_call" | custom-call | tf_op jit(solution)/shard_map/pallas_call | solution.py:527
  23.2 0.9 %shard_map.169 = (f32[16,3,24,128]{3,2,1,0:T(8,128)S(1)}, f32[10,8,3,16,128]{4,3,2,1,0:T(8,128)S(1)}, f32[8,40,128]{2,1,0:T(8,128)S(1)}, f32[8,24,128]{2,1,0:T(8...) custom-call(s32[1]{0:T(128)S(6)} %copy.42.refs_0_, ...), custom_call_target="tpu_custom_call", output_to_operand_aliasing={{0}: (3, {})} | custom-call | tf_op jit(solution)/shard_map/pallas_call | solution.py:527
  24.2 3.5 %collective-permute-start.8 = (f32[8,40,128]{2,1,0:T(8,128)S(1)}, f32[8,40,128]{2,1,0:T(8,128)S(1)}, u32[]{:S(2)}, u32[]{:S(2)}) collective-permute-start(f32[8,40,128]{2,1,0:T(8,128)S(1)} %get-tuple-element.74), channel_id=1, source_target_pairs={{0,4},{1,5},{2,6},{3,7},{4,0},{5,1},{6,2},{7,3},{8,12},{9,13},{10,... | collective-permute-start | bytes 491528 | tf_op jit(solution)/shard_map/ppermute | solution.py:636
  27.7 1.4 %collective-permute-start.10 = (f32[8,24,128]{2,1,0:T(8,128)S(1)}, f32[8,24,128]{2,1,0:T(8,128)S(1)}, u32[]{:S(2)}, u32[]{:S(2)}) collective-permute-start(f32[8,24,128]{2,1,0:T(8,128)S(1)} %get-tuple-element.75), channel_id=1, source_target_pairs={{0,2},{1,3},{2,0},{3,1},{4,6},{5,7},{6,4},{7,5},{8,10},{9,11},{10,... | collective-permute-start | bytes 294920 | tf_op jit(solution)/shard_map/ppermute | solution.py:637
  29.2 3.1 %collective-permute-done.10.refs_5_ = f32[8,24,128]{2,1,0:T(8,128)S(1)} collective-permute-done((f32[8,24,128]{2,1,0:T(8,128)S(1)}, f32[8,24,128]{2,1,0:T(8,128)S(1)}, u32[]{:S(2)}, u32[]{:S(2)}) %collective-permute-start.10) | collective-permute-done | bytes 98336 | tf_op jit(solution)/shard_map/ppermute | solution.py:637
  32.3 1.3 %shard_map.170.refs_3_ = f32[16,3,24,128]{3,2,1,0:T(8,128)S(1)} custom-call(f32[10,8,3,16,128]{4,3,2,1,0:T(8,128)S(1)} %get-tuple-element.72.refs_0_.refs_6_, f32[16,3,24,128]{3,2,1,0:T(8,128)S(1)} %get-tuple-element.73.refs_1_, f32[16,3,24,128]{3,2,1,0:T(8,128)S(1)} %get-tuple-element.69.refs_4_.refs_2_, f32[8,40,128]{2,1,0:T(8,128)S(1)} %collective-permute-done.8.refs_3_, ...), custom_call_target="tpu_custom_call" | custom-call | tf_op jit(solution)/shard_map/pallas_call | solution.py:527
  33.8 0.9 %shard_map.171 = (f32[16,3,24,128]{3,2,1,0:T(8,128)S(1)}, f32[10,8,3,16,128]{4,3,2,1,0:T(8,128)S(1)}, f32[8,40,128]{2,1,0:T(8,128)S(1)}, f32[8,24,128]{2,1,0:T(8...) custom-call(s32[1]{0:T(128)S(6)} %copy.42.refs_0_, ...), custom_call_target="tpu_custom_call", output_to_operand_aliasing={{0}: (3, {}), {1}: (6, {})} | custom-call | tf_op jit(solution)/shard_map/pallas_call | solution.py:527
  34.8 2.4 %collective-permute-start.13 = (f32[8,40,128]{2,1,0:T(8,128)S(1)}, f32[8,40,128]{2,1,0:T(8,128)S(1)}, u32[]{:S(2)}, u32[]{:S(2)}) collective-permute-start(f32[8,40,128]{2,1,0:T(8,128)S(1)} %get-tuple-element.80), channel_id=1, source_target_pairs={{0,4},{1,5},{2,6},{3,7},{4,0},{5,1},{6,2},{7,3},{8,12},{9,13},{10,... | collective-permute-start | bytes 491528 | tf_op jit(solution)/shard_map/ppermute | solution.py:636
  37.3 1.3 %collective-permute-start.15 = (f32[8,24,128]{2,1,0:T(8,128)S(1)}, f32[8,24,128]{2,1,0:T(8,128)S(1)}, u32[]{:S(2)}, u32[]{:S(2)}) collective-permute-start(f32[8,24,128]{2,1,0:T(8,128)S(1)} %get-tuple-element.81), channel_id=1, source_target_pairs={{0,2},{1,3},{2,0},{3,1},{4,6},{5,7},{6,4},{7,5},{8,10},{9,11},{10,... | collective-permute-start | bytes 294920 | tf_op jit(solution)/shard_map/ppermute | solution.py:637
  38.8 3.4 %collective-permute-done.15.refs_5_ = f32[8,24,128]{2,1,0:T(8,128)S(1)} collective-permute-done((f32[8,24,128]{2,1,0:T(8,128)S(1)}, f32[8,24,128]{2,1,0:T(8,128)S(1)}, u32[]{:S(2)}, u32[]{:S(2)}) %collective-permute-start.15) | collective-permute-done | bytes 98336 | tf_op jit(solution)/shard_map/ppermute | solution.py:637
  42.2 1.3 %shard_map.172.refs_3_ = f32[16,3,24,128]{3,2,1,0:T(8,128)S(1)} custom-call(f32[10,8,3,16,128]{4,3,2,1,0:T(8,128)S(1)} %get-tuple-element.78.refs_0_.refs_6_, f32[16,3,24,128]{3,2,1,0:T(8,128)S(1)} %get-tuple-element.79.refs_1_, f32[16,3,24,128]{3,2,1,0:T(8,128)S(1)} %get-tuple-element.69.refs_4_.refs_2_, f32[8,40,128]{2,1,0:T(8,128)S(1)} %collective-permute-done.13.refs_3_, ...), custom_call_target="tpu_custom_call" | custom-call | tf_op jit(solution)/shard_map/pallas_call | solution.py:527
  43.5 0.9 %shard_map.173 = (f32[16,3,24,128]{3,2,1,0:T(8,128)S(1)}, f32[10,8,3,16,128]{4,3,2,1,0:T(8,128)S(1)}, f32[8,40,128]{2,1,0:T(8,128)S(1)}, f32[8,24,128]{2,1,0:T(8...) custom-call(s32[1]{0:T(128)S(6)} %copy.42.refs_0_, ...), custom_call_target="tpu_custom_call", output_to_operand_aliasing={{0}: (3, {}), {1}: (6, {})} | custom-call | tf_op jit(solution)/shard_map/pallas_call | solution.py:527
  44.5 4.0 %collective-permute-start.18 = (f32[8,40,128]{2,1,0:T(8,128)S(1)}, f32[8,40,128]{2,1,0:T(8,128)S(1)}, u32[]{:S(2)}, u32[]{:S(2)}) collective-permute-start(f32[8,40,128]{2,1,0:T(8,128)S(1)} %get-tuple-element.86), channel_id=1, source_target_pairs={{0,4},{1,5},{2,6},{3,7},{4,0},{5,1},{6,2},{7,3},{8,12},{9,13},{10,... | collective-permute-start | bytes 491528 | tf_op jit(solution)/shard_map/ppermute | solution.py:636
  48.5 1.1 %collective-permute-start.20 = (f32[8,24,128]{2,1,0:T(8,128)S(1)}, f32[8,24,128]{2,1,0:T(8,128)S(1)}, u32[]{:S(2)}, u32[]{:S(2)}) collective-permute-start(f32[8,24,128]{2,1,0:T(8,128)S(1)} %get-tuple-element.87), channel_id=1, source_target_pairs={{0,2},{1,3},{2,0},{3,1},{4,6},{5,7},{6,4},{7,5},{8,10},{9,11},{10,... | collective-permute-start | bytes 294920 | tf_op jit(solution)/shard_map/ppermute | solution.py:637
  50.0 3.1 %collective-permute-done.20.refs_5_ = f32[8,24,128]{2,1,0:T(8,128)S(1)} collective-permute-done((f32[8,24,128]{2,1,0:T(8,128)S(1)}, f32[8,24,128]{2,1,0:T(8,128)S(1)}, u32[]{:S(2)}, u32[]{:S(2)}) %collective-permute-start.20) | collective-permute-done | bytes 98336 | tf_op jit(solution)/shard_map/ppermute | solution.py:637
  53.2 1.3 %shard_map.174.refs_3_ = f32[16,3,24,128]{3,2,1,0:T(8,128)S(1)} custom-call(f32[10,8,3,16,128]{4,3,2,1,0:T(8,128)S(1)} %get-tuple-element.84.refs_0_.refs_6_, f32[16,3,24,128]{3,2,1,0:T(8,128)S(1)} %get-tuple-element.85.refs_1_, f32[16,3,24,128]{3,2,1,0:T(8,128)S(1)} %get-tuple-element.69.refs_4_.refs_2_, f32[8,40,128]{2,1,0:T(8,128)S(1)} %collective-permute-done.18.refs_3_, ...), custom_call_target="tpu_custom_call" | custom-call | tf_op jit(solution)/shard_map/pallas_call | solution.py:527
  54.5 1.1 %shard_map.175 = (f32[16,3,24,128]{3,2,1,0:T(8,128)S(1)}, f32[10,8,3,16,128]{4,3,2,1,0:T(8,128)S(1)}, f32[8,40,128]{2,1,0:T(8,128)S(1)}, f32[8,24,128]{2,1,0:T(8...) custom-call(s32[1]{0:T(128)S(6)} %copy.42.refs_0_, ...), custom_call_target="tpu_custom_call", output_to_operand_aliasing={{0}: (3, {}), {1}: (6, {})} | custom-call | tf_op jit(solution)/shard_map/pallas_call | solution.py:527
  55.6 2.7 %collective-permute-start.23 = (f32[8,40,128]{2,1,0:T(8,128)S(1)}, f32[8,40,128]{2,1,0:T(8,128)S(1)}, u32[]{:S(2)}, u32[]{:S(2)}) collective-permute-start(f32[8,40,128]{2,1,0:T(8,128)S(1)} %get-tuple-element.92), channel_id=1, source_target_pairs={{0,4},{1,5},{2,6},{3,7},{4,0},{5,1},{6,2},{7,3},{8,12},{9,13},{10,... | collective-permute-start | bytes 491528 | tf_op jit(solution)/shard_map/ppermute | solution.py:636
  58.3 1.0 %collective-permute-start.25 = (f32[8,24,128]{2,1,0:T(8,128)S(1)}, f32[8,24,128]{2,1,0:T(8,128)S(1)}, u32[]{:S(2)}, u32[]{:S(2)}) collective-permute-start(f32[8,24,128]{2,1,0:T(8,128)S(1)} %get-tuple-element.93), channel_id=1, source_target_pairs={{0,2},{1,3},{2,0},{3,1},{4,6},{5,7},{6,4},{7,5},{8,10},{9,11},{10,... | collective-permute-start | bytes 294920 | tf_op jit(solution)/shard_map/ppermute | solution.py:637
  59.8 3.3 %collective-permute-done.25.refs_5_ = f32[8,24,128]{2,1,0:T(8,128)S(1)} collective-permute-done((f32[8,24,128]{2,1,0:T(8,128)S(1)}, f32[8,24,128]{2,1,0:T(8,128)S(1)}, u32[]{:S(2)}, u32[]{:S(2)}) %collective-permute-start.25) | collective-permute-done | bytes 98336 | tf_op jit(solution)/shard_map/ppermute | solution.py:637
  63.2 1.3 %shard_map.176.refs_3_ = f32[16,3,24,128]{3,2,1,0:T(8,128)S(1)} custom-call(f32[10,8,3,16,128]{4,3,2,1,0:T(8,128)S(1)} %get-tuple-element.90.refs_0_.refs_6_, f32[16,3,24,128]{3,2,1,0:T(8,128)S(1)} %get-tuple-element.91.refs_1_, f32[16,3,24,128]{3,2,1,0:T(8,128)S(1)} %get-tuple-element.69.refs_4_.refs_2_, f32[8,40,128]{2,1,0:T(8,128)S(1)} %collective-permute-done.23.refs_3_, ...), custom_call_target="tpu_custom_call" | custom-call | tf_op jit(solution)/shard_map/pallas_call | solution.py:527
  64.6 1.1 %shard_map.177 = (f32[16,3,24,128]{3,2,1,0:T(8,128)S(1)}, f32[10,8,3,16,128]{4,3,2,1,0:T(8,128)S(1)}, f32[5,8,3,8,128]{4,3,2,1,0:T(8,128)S(1)}, f32[5,8,3,8,128]{4,3,2,1,0:T(8,128)S(1)}) custom-call(s32[1]{0:T(128)S(6)} %copy.42.refs_0_, s32[1,4]{1,0:T(1,128)S(1)} %bitcast.8, f32[1,10]{1,0:T(1,128)S(1)} %bitcast.13, ...), custom_call_target="tpu_custom_call", output_to_operand_aliasing={{0}: (3, {}), {1}: (6, {})} | custom-call | tf_op jit(solution)/shard_map/pallas_call | solution.py:527
  65.7 1.9 %collective-permute-done.28.theirs = f32[5,8,3,8,128]{4,3,2,1,0:T(8,128)S(1)} collective-permute-done((f32[5,8,3,8,128]{4,3,2,1,0:T(8,128)S(1)}, f32[5,8,3,8,128]{4,3,2,1,0:T(8,128)S(1)}, u32[]{:S(2)}, u32[]{:S(2)}) %collective-permute-start.28) | collective-permute-done | bytes 491552 | tf_op jit(solution)/shard_map/ppermute | solution.py:686
  67.6 0.9 %shard_map.178 = (f32[8,8,320]{2,1,0:T(8,128)}, f32[8,8,320]{2,1,0:T(8,128)}, f32[8,8,320]{2,1,0:T(8,128)}, f32[8,8,320]{2,1,0:T(8,128)}, bf16[4,8,8,320]{3,2,1,0:T(8,128)(2,1)}, /*index=5*/f32[8,8,320]{2,1,0:T(8,128)}) custom-call(f32[5,8,3,8,128]{4,3,2,1,0:T(8,128)S(1)} %get-tuple-element.96.own, f32[5,8,3,8,128]{4,3,2,1,0:T(8,128)S(1)} %collective-permute-done.28.theirs, ...), custom_call_target="tpu_custom_call" | custom-call | tf_op jit(solution)/shard_map/pallas_call | solution.py:527
  (52 shorter events, 3.5 us)
Async XLA Ops:
  1.9 1.8 %collective-permute-start.1 = (f32[3,8,8,320]{3,2,1,0:T(8,128)S(1)}, f32[3,8,8,320]{3,2,1,0:T(8,128)S(1)}, u32[]{:S(2)}, u32[]{:S(2)}) collective-permute-start(f32[3,8,8,320]{3,2,1,0:T(8,128)S(1)} %get-tuple-element.54), channel_id=1, source_target_pairs={{0,1},{1,0},{2,3},{3,2},{4,5},{5,4},{6,7},{7,6},{8,9},{9,8},{10,11... | collective-permute-start | bytes 737288 | tf_op jit(solution)/shard_map/ppermute | solution.py:598
  2.4 1.2 %collective-permute-start = (f32[16,64]{1,0:T(8,128)S(1)}, f32[16,64]{1,0:T(8,128)S(1)}, u32[]{:S(2)}, u32[]{:S(2)}) collective-permute-start(f32[16,64]{1,0:T(8,128)S(1)} %get-tuple-element.52), channel_id=1, source_target_pairs={{0,1},{1,0},{2,3},{3,2},{4,5},{5,4},{6,7},{7,6},{8,9},{9,8},{10,11... | collective-permute-start | bytes 12296 | tf_op jit(solution)/shard_map/ppermute | solution.py:539
  3.7 19.5 %copy-start.2 = (s32[4]{0:T(128)S(1)}, s32[4]{0:T(128)}, u32[]{:S(2)}) copy-start(s32[4]{0:T(128)} %param.21) | copy-start | bytes 52
  3.7 19.5 %copy-start.3 = (f32[10]{0:T(128)S(1)}, f32[10]{0:T(128)}, u32[]{:S(2)}) copy-start(f32[10]{0:T(128)} %param.17) | copy-start | bytes 124
  3.9 13.3 %collective-permute-start.2 = (f32[17,40,128]{2,1,0:T(8,128)S(1)}, f32[17,40,128]{2,1,0:T(8,128)S(1)}, u32[]{:S(2)}, u32[]{:S(2)}) collective-permute-start(f32[17,40,128]{2,1,0:T(8,128)S(1)} %get-tuple-element.58), channel_id=1, source_target_pairs={{0,4},{1,5},{2,6},{3,7},{4,0},{5,1},{6,2},{7,3},{8,12},{9,13},{10,... | collective-permute-start | bytes 1044488 | tf_op jit(solution)/shard_map/ppermute | solution.py:636
  6.9 10.3 %collective-permute-start.3 = (f32[25,24,128]{2,1,0:T(8,128)S(1)}, f32[25,24,128]{2,1,0:T(8,128)S(1)}, u32[]{:S(2)}, u32[]{:S(2)}) collective-permute-start(f32[25,24,128]{2,1,0:T(8,128)S(1)} %get-tuple-element.59), channel_id=1, source_target_pairs={{0,2},{1,3},{2,0},{3,1},{4,6},{5,7},{6,4},{7,5},{8,10},{9,11},{10,... | collective-permute-start | bytes 921608 | tf_op jit(solution)/shard_map/ppermute | solution.py:637
  8.4 12.4 %collective-permute-start.7 = (f32[16,40,128]{2,1,0:T(8,128)S(1)}, f32[16,40,128]{2,1,0:T(8,128)S(1)}, u32[]{:S(2)}, u32[]{:S(2)}) collective-permute-start(f32[16,40,128]{2,1,0:T(8,128)S(1)} %get-tuple-element.66), channel_id=1, source_target_pairs={{0,1},{1,0},{2,3},{3,2},{4,8},{5,9},{6,10},{7,11},{8,4},{9,5},{10,... | collective-permute-start | bytes 983048 | tf_op jit(solution)/shard_map/ppermute | solution.py:636
  8.4 8.8 %collective-permute-start.4 = (f32[3,24,128]{2,1,0:T(8,128)S(1)}, f32[3,24,128]{2,1,0:T(8,128)S(1)}, u32[]{:S(2)}, u32[]{:S(2)}) collective-permute-start(f32[3,24,128]{2,1,0:T(8,128)S(1)} %get-tuple-element.60), channel_id=1, source_target_pairs={{0,6},{1,7},{2,4},{3,5},{4,2},{5,3},{6,0},{7,1},{8,14},{9,15},{10,... | collective-permute-start | bytes 110600 | tf_op jit(solution)/shard_map/ppermute | solution.py:639
  11.5 1.2 %collective-permute-start.5 = (f32[2,24,128]{2,1,0:T(8,128)S(1)}, f32[2,24,128]{2,1,0:T(8,128)S(1)}, u32[]{:S(2)}, u32[]{:S(2)}) collective-permute-start(f32[2,24,128]{2,1,0:T(8,128)S(1)} %get-tuple-element.61), channel_id=1, source_target_pairs={{0,1},{1,0},{2,3},{3,2},{4,10},{5,11},{6,8},{7,9},{8,6},{9,7},{10,... | collective-permute-start | bytes 73736 | tf_op jit(solution)/shard_map/ppermute | solution.py:639
  17.2 5.4 %collective-permute-start.6 = (f32[4,16,128]{2,1,0:T(8,128)S(1)}, f32[4,16,128]{2,1,0:T(8,128)S(1)}, u32[]{:S(2)}, u32[]{:S(2)}) collective-permute-start(f32[4,16,128]{2,1,0:T(8,128)S(1)} %shard_map.166), channel_id=1, source_target_pairs={{0,8},{1,9},{2,10},{3,11},{4,12},{5,13},{6,14},{7,15},{8,0},{9,1},... | collective-permute-start | bytes 98312 | tf_op jit(solution)/shard_map/ppermute | solution.py:558
  24.1 8.2 %collective-permute-start.9 = (f32[8,40,128]{2,1,0:T(8,128)S(1)}, f32[8,40,128]{2,1,0:T(8,128)S(1)}, u32[]{:S(2)}, u32[]{:S(2)}) collective-permute-start(f32[8,40,128]{2,1,0:T(8,128)S(1)} %get-tuple-element.74), channel_id=1, source_target_pairs={{0,1},{1,0},{2,3},{3,2},{4,8},{5,9},{6,10},{7,11},{8,4},{9,5},{10,... | collective-permute-start | bytes 491528 | tf_op jit(solution)/shard_map/ppermute | solution.py:636
  24.2 8.2 %collective-permute-start.8 = (f32[8,40,128]{2,1,0:T(8,128)S(1)}, f32[8,40,128]{2,1,0:T(8,128)S(1)}, u32[]{:S(2)}, u32[]{:S(2)}) collective-permute-start(f32[8,40,128]{2,1,0:T(8,128)S(1)} %get-tuple-element.74), channel_id=1, source_target_pairs={{0,4},{1,5},{2,6},{3,7},{4,0},{5,1},{6,2},{7,3},{8,12},{9,13},{10,... | collective-permute-start | bytes 491528 | tf_op jit(solution)/shard_map/ppermute | solution.py:636
  27.7 4.6 %collective-permute-start.10 = (f32[8,24,128]{2,1,0:T(8,128)S(1)}, f32[8,24,128]{2,1,0:T(8,128)S(1)}, u32[]{:S(2)}, u32[]{:S(2)}) collective-permute-start(f32[8,24,128]{2,1,0:T(8,128)S(1)} %get-tuple-element.75), channel_id=1, source_target_pairs={{0,2},{1,3},{2,0},{3,1},{4,6},{5,7},{6,4},{7,5},{8,10},{9,11},{10,... | collective-permute-start | bytes 294920 | tf_op jit(solution)/shard_map/ppermute | solution.py:637
  29.1 4.7 %collective-permute-start.11 = (f32[2,24,128]{2,1,0:T(8,128)S(1)}, f32[2,24,128]{2,1,0:T(8,128)S(1)}, u32[]{:S(2)}, u32[]{:S(2)}) collective-permute-start(f32[2,24,128]{2,1,0:T(8,128)S(1)} %get-tuple-element.76), channel_id=1, source_target_pairs={{0,6},{1,7},{2,4},{3,5},{4,2},{5,3},{6,0},{7,1},{8,14},{9,15},{10,... | collective-permute-start | bytes 73736 | tf_op jit(solution)/shard_map/ppermute | solution.py:639
  29.2 4.7 %collective-permute-start.12 = (f32[2,24,128]{2,1,0:T(8,128)S(1)}, f32[2,24,128]{2,1,0:T(8,128)S(1)}, u32[]{:S(2)}, u32[]{:S(2)}) collective-permute-start(f32[2,24,128]{2,1,0:T(8,128)S(1)} %get-tuple-element.77), channel_id=1, source_target_pairs={{0,1},{1,0},{2,3},{3,2},{4,10},{5,11},{6,8},{7,9},{8,6},{9,7},{10,... | collective-permute-start | bytes 73736 | tf_op jit(solution)/shard_map/ppermute | solution.py:639
  34.8 7.4 %collective-permute-start.14 = (f32[8,40,128]{2,1,0:T(8,128)S(1)}, f32[8,40,128]{2,1,0:T(8,128)S(1)}, u32[]{:S(2)}, u32[]{:S(2)}) collective-permute-start(f32[8,40,128]{2,1,0:T(8,128)S(1)} %get-tuple-element.80), channel_id=1, source_target_pairs={{0,1},{1,0},{2,3},{3,2},{4,8},{5,9},{6,10},{7,11},{8,4},{9,5},{10,... | collective-permute-start | bytes 491528 | tf_op jit(solution)/shard_map/ppermute | solution.py:636
  34.8 7.3 %collective-permute-start.13 = (f32[8,40,128]{2,1,0:T(8,128)S(1)}, f32[8,40,128]{2,1,0:T(8,128)S(1)}, u32[]{:S(2)}, u32[]{:S(2)}) collective-permute-start(f32[8,40,128]{2,1,0:T(8,128)S(1)} %get-tuple-element.80), channel_id=1, source_target_pairs={{0,4},{1,5},{2,6},{3,7},{4,0},{5,1},{6,2},{7,3},{8,12},{9,13},{10,... | collective-permute-start | bytes 491528 | tf_op jit(solution)/shard_map/ppermute | solution.py:636
  37.3 4.9 %collective-permute-start.15 = (f32[8,24,128]{2,1,0:T(8,128)S(1)}, f32[8,24,128]{2,1,0:T(8,128)S(1)}, u32[]{:S(2)}, u32[]{:S(2)}) collective-permute-start(f32[8,24,128]{2,1,0:T(8,128)S(1)} %get-tuple-element.81), channel_id=1, source_target_pairs={{0,2},{1,3},{2,0},{3,1},{4,6},{5,7},{6,4},{7,5},{8,10},{9,11},{10,... | collective-permute-start | bytes 294920 | tf_op jit(solution)/shard_map/ppermute | solution.py:637
  38.6 4.9 %collective-permute-start.16 = (f32[2,24,128]{2,1,0:T(8,128)S(1)}, f32[2,24,128]{2,1,0:T(8,128)S(1)}, u32[]{:S(2)}, u32[]{:S(2)}) collective-permute-start(f32[2,24,128]{2,1,0:T(8,128)S(1)} %get-tuple-element.82), channel_id=1, source_target_pairs={{0,6},{1,7},{2,4},{3,5},{4,2},{5,3},{6,0},{7,1},{8,14},{9,15},{10,... | collective-permute-start | bytes 73736 | tf_op jit(solution)/shard_map/ppermute | solution.py:639
  38.8 4.8 %collective-permute-start.17 = (f32[2,24,128]{2,1,0:T(8,128)S(1)}, f32[2,24,128]{2,1,0:T(8,128)S(1)}, u32[]{:S(2)}, u32[]{:S(2)}) collective-permute-start(f32[2,24,128]{2,1,0:T(8,128)S(1)} %get-tuple-element.83), channel_id=1, source_target_pairs={{0,1},{1,0},{2,3},{3,2},{4,10},{5,11},{6,8},{7,9},{8,6},{9,7},{10,... | collective-permute-start | bytes 73736 | tf_op jit(solution)/shard_map/ppermute | solution.py:639
  44.4 8.7 %collective-permute-start.19 = (f32[8,40,128]{2,1,0:T(8,128)S(1)}, f32[8,40,128]{2,1,0:T(8,128)S(1)}, u32[]{:S(2)}, u32[]{:S(2)}) collective-permute-start(f32[8,40,128]{2,1,0:T(8,128)S(1)} %get-tuple-element.86), channel_id=1, source_target_pairs={{0,1},{1,0},{2,3},{3,2},{4,8},{5,9},{6,10},{7,11},{8,4},{9,5},{10,... | collective-permute-start | bytes 491528 | tf_op jit(solution)/shard_map/ppermute | solution.py:636
  44.5 8.7 %collective-permute-start.18 = (f32[8,40,128]{2,1,0:T(8,128)S(1)}, f32[8,40,128]{2,1,0:T(8,128)S(1)}, u32[]{:S(2)}, u32[]{:S(2)}) collective-permute-start(f32[8,40,128]{2,1,0:T(8,128)S(1)} %get-tuple-element.86), channel_id=1, source_target_pairs={{0,4},{1,5},{2,6},{3,7},{4,0},{5,1},{6,2},{7,3},{8,12},{9,13},{10,... | collective-permute-start | bytes 491528 | tf_op jit(solution)/shard_map/ppermute | solution.py:636
  48.5 4.6 %collective-permute-start.20 = (f32[8,24,128]{2,1,0:T(8,128)S(1)}, f32[8,24,128]{2,1,0:T(8,128)S(1)}, u32[]{:S(2)}, u32[]{:S(2)}) collective-permute-start(f32[8,24,128]{2,1,0:T(8,128)S(1)} %get-tuple-element.87), channel_id=1, source_target_pairs={{0,2},{1,3},{2,0},{3,1},{4,6},{5,7},{6,4},{7,5},{8,10},{9,11},{10,... | collective-permute-start | bytes 294920 | tf_op jit(solution)/shard_map/ppermute | solution.py:637
  49.7 4.8 %collective-permute-start.21 = (f32[2,24,128]{2,1,0:T(8,128)S(1)}, f32[2,24,128]{2,1,0:T(8,128)S(1)}, u32[]{:S(2)}, u32[]{:S(2)}) collective-permute-start(f32[2,24,128]{2,1,0:T(8,128)S(1)} %get-tuple-element.88), channel_id=1, source_target_pairs={{0,6},{1,7},{2,4},{3,5},{4,2},{5,3},{6,0},{7,1},{8,14},{9,15},{10,... | collective-permute-start | bytes 73736 | tf_op jit(solution)/shard_map/ppermute | solution.py:639
  50.0 4.5 %collective-permute-start.22 = (f32[2,24,128]{2,1,0:T(8,128)S(1)}, f32[2,24,128]{2,1,0:T(8,128)S(1)}, u32[]{:S(2)}, u32[]{:S(2)}) collective-permute-start(f32[2,24,128]{2,1,0:T(8,128)S(1)} %get-tuple-element.89), channel_id=1, source_target_pairs={{0,1},{1,0},{2,3},{3,2},{4,10},{5,11},{6,8},{7,9},{8,6},{9,7},{10,... | collective-permute-start | bytes 73736 | tf_op jit(solution)/shard_map/ppermute | solution.py:639
  55.6 7.6 %collective-permute-start.24 = (f32[8,40,128]{2,1,0:T(8,128)S(1)}, f32[8,40,128]{2,1,0:T(8,128)S(1)}, u32[]{:S(2)}, u32[]{:S(2)}) collective-permute-start(f32[8,40,128]{2,1,0:T(8,128)S(1)} %get-tuple-element.92), channel_id=1, source_target_pairs={{0,1},{1,0},{2,3},{3,2},{4,8},{5,9},{6,10},{7,11},{8,4},{9,5},{10,... | collective-permute-start | bytes 491528 | tf_op jit(solution)/shard_map/ppermute | solution.py:636
  55.6 7.6 %collective-permute-start.23 = (f32[8,40,128]{2,1,0:T(8,128)S(1)}, f32[8,40,128]{2,1,0:T(8,128)S(1)}, u32[]{:S(2)}, u32[]{:S(2)}) collective-permute-start(f32[8,40,128]{2,1,0:T(8,128)S(1)} %get-tuple-element.92), channel_id=1, source_target_pairs={{0,4},{1,5},{2,6},{3,7},{4,0},{5,1},{6,2},{7,3},{8,12},{9,13},{10,... | collective-permute-start | bytes 491528 | tf_op jit(solution)/shard_map/ppermute | solution.py:636
  58.3 4.9 %collective-permute-start.25 = (f32[8,24,128]{2,1,0:T(8,128)S(1)}, f32[8,24,128]{2,1,0:T(8,128)S(1)}, u32[]{:S(2)}, u32[]{:S(2)}) collective-permute-start(f32[8,24,128]{2,1,0:T(8,128)S(1)} %get-tuple-element.93), channel_id=1, source_target_pairs={{0,2},{1,3},{2,0},{3,1},{4,6},{5,7},{6,4},{7,5},{8,10},{9,11},{10,... | collective-permute-start | bytes 294920 | tf_op jit(solution)/shard_map/ppermute | solution.py:637
  59.3 5.2 %collective-permute-start.26 = (f32[2,24,128]{2,1,0:T(8,128)S(1)}, f32[2,24,128]{2,1,0:T(8,128)S(1)}, u32[]{:S(2)}, u32[]{:S(2)}) collective-permute-start(f32[2,24,128]{2,1,0:T(8,128)S(1)} %get-tuple-element.94), channel_id=1, source_target_pairs={{0,6},{1,7},{2,4},{3,5},{4,2},{5,3},{6,0},{7,1},{8,14},{9,15},{10,... | collective-permute-start | bytes 73736 | tf_op jit(solution)/shard_map/ppermute | solution.py:639
  59.8 4.7 %collective-permute-start.27 = (f32[2,24,128]{2,1,0:T(8,128)S(1)}, f32[2,24,128]{2,1,0:T(8,128)S(1)}, u32[]{:S(2)}, u32[]{:S(2)}) collective-permute-start(f32[2,24,128]{2,1,0:T(8,128)S(1)} %get-tuple-element.95), channel_id=1, source_target_pairs={{0,1},{1,0},{2,3},{3,2},{4,10},{5,11},{6,8},{7,9},{8,6},{9,7},{10,... | collective-permute-start | bytes 73736 | tf_op jit(solution)/shard_map/ppermute | solution.py:639
  64.5 3.1 %copy-start = (bf16[4,8,8,320]{3,2,1,0:T(8,128)(2,1)S(1)}, bf16[4,8,8,320]{3,2,1,0:T(8,128)(2,1)}, u32[]{:S(2)}) copy-start(bf16[4,8,8,320]{3,2,1,0:T(8,128)(2,1)} %stored.1) | copy-start | bytes 491524
  65.7 1.9 %collective-permute-start.28 = (f32[5,8,3,8,128]{4,3,2,1,0:T(8,128)S(1)}, f32[5,8,3,8,128]{4,3,2,1,0:T(8,128)S(1)}, u32[]{:S(2)}, u32[]{:S(2)}) collective-permute-start(f32[5,8,3,8,128]{4,3,2,1,0:T(8,128)S(1)} %get-tuple-element.97), channel_id=1, source_target_pairs={{0,1},{1,0},{2,3},{3,2},{4,5},{5,4},{6,7},{7,6},{8,9},{9,8},{10,11... | collective-permute-start | bytes 1474568 | tf_op jit(solution)/shard_map/ppermute | solution.py:686
  (1 other events, 3.1 us)

commit v5 on v4

--- a/solution.py
+++ b/solution.py
@@ -30,7 +30,7 @@
         self.trace_rows = pl.cdiv(steps + 2, 2 * ROWS) * 2 * ROWS
         self.z_parities = [p for p in (0, 1) if p + 1 < self.nx]
         self.y_parities = [p for p in (0, 1) if p + 1 < self.columns]
-        assert self.ny % 2 == 0 and block_x >= HALO and block_y % ROWS == 0 and steps % 2 == 0
+        assert self.ny % 2 == 0 and block_x >= HALO and block_x % 2 == 0 and block_y % ROWS == 0 and steps % 2 == 0
 
     def device(self, x, column, core):
         return x * self.ny + 2 * column + core
@@ -58,7 +58,7 @@
         )
 
     def carriers(self, z_messages, y_messages, d_messages):
-        starts = (self.bx + 2 * REACH, 3 * self.bx, REACH // 2)
+        starts = (self.bx + 2 * REACH, 2 * (self.bx // 2), REACH // 2)
         return [(m, start) for ms, start in zip((z_messages, y_messages, d_messages), starts) for m in ms]
 
     def by_kind(self, messages):
@@ -118,13 +118,48 @@
         row += piece.shape[0]
 
 
-def write_y_message(ref, lead, source, lay, high):
-    for x in range(lay.bx):
+def y_rows_of(source, lay, high):
+    def rows(plane, t):
+        return jnp.where(high, source[plane, t, lay.cy - ROWS : lay.cy, :], source[plane, t, 0:ROWS, :])
+
+    return rows
+
+
+def y_halves_of(first, second, lay, high):
+    upper = lax.broadcasted_iota(jnp.int32, (ROWS, LANES), 0) < REACH
+    a, b = y_rows_of(first, lay, high), y_rows_of(second, lay, high)
+
+    def rows(plane, t):
+        one, two = a(plane, t), b(plane, t)
+        one = jnp.where(high, pltpu.roll(one, REACH, 0), one)
+        two = jnp.where(high, two, pltpu.roll(two, REACH, 0))
+        return jnp.where(upper, one, two)
+
+    return rows
+
+
+def write_y_message(ref, lead, rows_of, lay):
+    half = lay.bx // 2
+    for x in range(half):
+        row = 0
         for t in range(lay.zt):
-            rows = jnp.where(
-                high, source[x, t, lay.cy - ROWS : lay.cy, :], source[x, t, 0:ROWS, :]
-            )
-            ref[lead * lay.bx + x, t * ROWS : (t + 1) * ROWS, :] = rows
+            a, b = rows_of(x, t), rows_of(x + half, t)
+            both = [a + pltpu.roll(b, LANES // 2, 1)] if lay.packed and t + 1 == lay.zt else [a, b]
+            for rows in both:
+                ref[lead * half + x, row : row + ROWS, :] = rows
+                row += ROWS
+
+
+def read_y_message(ref, lead, lay, x, t):
+    half = lay.bx // 2
+    plane, second = lead * half + x % half, x >= half
+    row = 2 * t * ROWS
+    if not lay.packed or t + 1 < lay.zt:
+        row += ROWS * second
+        return ref[plane, row : row + ROWS, :]
+    both = ref[plane, row : row + ROWS, :]
+    low = lane_ids(ROWS) < LANES // 2
+    return pltpu.roll(jnp.where(low, 0.0, both), LANES // 2, 1) if second else jnp.where(low, both, 0.0)
 
 
 def write_d_message(ref, source, lay, right, high):
@@ -177,7 +212,7 @@
 
 
 def prepare_kernel(lay, *refs):
-    (own, other), refs = refs[:2], refs[2:]
+    (own, other, groups), refs = refs[:3], refs[3:]
     (p, q, s), refs = refs[:3], refs[3:]
     nz, ny = len(lay.z_parities), len(lay.y_parities)
     z_messages, refs = refs[:nz], refs[nz:]
@@ -209,16 +244,12 @@
                 store_packed(message, lay.bx + lead * REACH + x, tiles, lay, lay.cy)
     highs = [lay.y_side(py)[0] for py in lay.y_parities]
     for message, high in zip(y_messages, highs):
-        for lead, ref in enumerate((p, q, s)):
-            write_y_message(message, lead, ref, lay, high)
+        write_y_message(message, 0, y_rows_of(p, lay, high), lay)
+        write_y_message(message, 1, y_halves_of(q, s, lay, high), lay)
     corners = [(right, high) for right in sides for high in highs]
     for message, (right, high) in zip(d_messages, corners):
         write_d_message(message, p, lay, right, high)
-
-
-def append_kernel(lay, *refs):
-    groups, messages = refs[0], refs[1 + (len(refs) - 1) // 2 :]
-    for message, start in lay.carriers(*lay.by_kind(messages)):
+    for message, start in lay.carriers(z_messages[:1], y_messages[:1], d_messages[:1]):
         for group in range(groups.shape[0]):
             for part in range(lay.trace_rows // ROWS):
                 plane, row = lay.spot(message, start, group, part)
@@ -332,7 +363,7 @@
         start = pl.multiple_of(jnp.where(high, own_y + cy, own_y - ROWS), ROWS)
         for x in range(bx):
             for t in range(zt):
-                rows = message[x, t * ROWS : (t + 1) * ROWS, :]
+                rows = read_y_message(message, 0, lay, x, t)
                 buffer[own_x + x, t, pl.ds(start, ROWS), :] = jnp.where(valid, rows, 0.0)
 
     if first:
@@ -348,15 +379,16 @@
                     block = jnp.where(valid, message[bx + lead * REACH + x], 0.0)
                     for t, tile in enumerate(unpack(block, lay, cy)):
                         ext[start + x, t, REACH : REACH + cy, :] = tile
-            for is_high, start, cut in ((False, 0, ROWS - REACH), (True, REACH + cy, 0)):
+            cut = lead * REACH
+            for is_high, start in ((False, 0), (True, REACH + cy)):
                 wants = [v & (h if is_high else ~h) for h, v in y_sides]
                 for x in range(bx):
                     for t in range(zt):
-                        rows = slice(t * ROWS + cut, t * ROWS + cut + REACH)
-                        ext[REACH + x, t, start : start + REACH, :] = sum(
-                            (jnp.where(w, m[(lead + 1) * bx + x, rows, :], 0.0) for w, m in zip(wants, y_in)),
-                            jnp.zeros((REACH, LANES), jnp.float32),
+                        rows = sum(
+                            (jnp.where(w, read_y_message(m, 1, lay, x, t), 0.0) for w, m in zip(wants, y_in)),
+                            jnp.zeros((ROWS, LANES), jnp.float32),
                         )
+                        ext[REACH + x, t, start : start + REACH, :] = rows[cut : cut + REACH]
         q, s = q_ext, s_out
 
     for x in range(lay.ex):
@@ -491,7 +523,7 @@
         for x in range(bx):
             store_packed(z_out, x, [latest[x, t] for t in range(zt)], lay, cy)
         for message, (high, _) in zip(y_out, y_sides):
-            write_y_message(message, 0, latest, lay, high)
+            write_y_message(message, 0, y_rows_of(latest, lay, high), lay)
         corners = [(right, high) for right, _ in z_sides for high, _ in y_sides]
         for message, (right, high) in zip(d_out, corners):
             write_d_message(message, latest, lay, right, high)
@@ -600,10 +632,11 @@
     block = (lay.bx, lay.zt, lay.cy, LANES)
     ext = (lay.ex, lay.zt, lay.ey, LANES)
     field = (lay.bx + 2 * HALO, lay.zt, lay.cy + 2 * HALO, LANES)
-    y_rows = lay.zt * ROWS
+    d_rows = lay.zt * ROWS
+    y_rows = (2 * lay.zt - lay.packed) * ROWS
     z_shape = (lay.bx, lay.zrows, LANES)
-    y_shape = (lay.bx, y_rows, LANES)
-    d_shape = (REACH // 2, y_rows, LANES)
+    y_shape = (lay.bx // 2, y_rows, LANES)
+    d_shape = (REACH // 2, d_rows, LANES)
 
     def carrying(planes, rows, first):
         more = pl.cdiv(groups.shape[0] * lay.trace_rows, rows) if first else 0
@@ -611,25 +644,15 @@
 
     outs = [(block, f32)] * 3
     outs += [carrying(lay.bx + 2 * REACH, lay.zrows, pz == 0) for pz in lay.z_parities]
-    outs += [carrying(3 * lay.bx, y_rows, py == 0) for py in lay.y_parities]
-    outs += [carrying(REACH // 2, y_rows, pz + py == 0) for pz in lay.z_parities for py in lay.y_parities]
+    outs += [carrying(2 * (lay.bx // 2), y_rows, py == 0) for py in lay.y_parities]
+    outs += [carrying(REACH // 2, d_rows, pz + py == 0) for pz in lay.z_parities for py in lay.y_parities]
     made = call(
         functools.partial(prepare_kernel, lay),
         outs,
-        [mine, swapped],
+        [mine, swapped, groups],
     )
     (p, q, s), made = made[:3], made[3:]
     z_out, y_out, d_out = made[:nz], made[nz : nz + ny], made[nz + ny :]
-    filled = z_out[:1] + y_out[:1] + d_out[:1]
-    if filled:
-        filled = call(
-            functools.partial(append_kernel, lay),
-            [(m.shape, f32) for m in filled],
-            [groups, *filled],
-            aliases={1 + i: i for i in range(len(filled))},
-        )
-        z, y, d = lay.by_kind(filled)
-        z_out, y_out, d_out = z + z_out[1:], y + y_out[1:], d + d_out[1:]
 
     for time in range(0, steps, 2):
         begin, end = time == 0, time + 2 == steps

time: 68.5 us -> 68 us (level)
  waiting for transfers between devices: 21.9 us -> 20.9 us
    ppermute x10, starting transfers between devices: 4.16 us -> 7.28 us  [body(): d_in = [lax.ppermute(m, AXES, pairs) for m, pairs in zip(d_out, diagonals)]]
    ppermute x5, starting transfers between devices: 6.4 us -> 3.28 us  [body(): lax.ppermute(m, AXES, lay.y_permutation(py))]
    ppermute x5, waiting for transfers between devices: 13 us -> 12.3 us  [body(): lax.ppermute(m, AXES, lay.y_permutation(py))]
    pallas_call x16 -> x15, Pallas kernels: 14.4 us -> 14.4 us  [call(): pl.pallas_call(kernel, out_shape=[jax.ShapeDtypeStruct(shape, dtype) for...]
  transfers between devices with their start and end apart: 29 -> 29, of which waited for: 10 -> 9; matrix products, arithmetic and copies ran while one was open for 0% -> 0% of each run, Pallas kernels for 10% -> 10%
where the time goes in v5:
time: 68 us; the launch traced here: 67.7 us
  starting transfers between devices  30.7 us (45%)
  waiting for transfers between devices  20.9 us (31%)
  Pallas kernels  14.4 us (21%)
  between operations  1.53 us (2%)
    ppermute x10, starting transfers between devices, body(): lax.ppermute(m, AXES, lay.z_permutation(pz))  16.2 us
    pallas_call x15, Pallas kernels, call(): pl.pallas_call(kernel, out_shape=[jax.ShapeDtypeStruct(shape, dtype) for...  14.4 us
    ppermute x5, waiting for transfers between devices, body(): lax.ppermute(m, AXES, lay.y_permutation(py))  12.3 us
    ppermute x10, starting transfers between devices, body(): d_in = [lax.ppermute(m, AXES, pairs) for m, pairs in zip(d_out, diagonals)]  7.28 us
    ppermute x10, waiting for transfers between devices, body(): d_in = [lax.ppermute(m, AXES, pairs) for m, pairs in zip(d_out, diagonals)]  5.08 us
    ppermute x5, starting transfers between devices, body(): lax.ppermute(m, AXES, lay.y_permutation(py))  3.28 us
    ppermute x1, starting transfers between devices, spread(): message = jnp.concatenate([message, lax.ppermute(message, AXES, pairs)], 0)  3.26 us
    ppermute x1, waiting for transfers between devices, body(): theirs = lax.ppermute(theirs, AXES, lay.core_permutation())  1.85 us
  transfers between devices with their start and end apart: 29, of which 9 were waited for; matrix products, arithmetic and copies ran while one was open for 0% of the time, Pallas kernels for 10%

profile of v5, /device:TPU:0, one launch (start us, length us, event | category | flops | bytes accessed | tf_op | source)
XLA Modules:
  0.0 67.7 jit_solution(4217628411633318346)
XLA Ops:
  0.7 1.2 %shard_map.163 = (f32[3,8,8,320]{3,2,1,0:T(8,128)S(1)}, f32[3,8,8,320]{3,2,1,0:T(8,128)S(1)}, f32[16,64]{1,0:T(8,128)S(1)}) custom-call(f32[8,8,320]{2,1,0:T(8,128)} %src_now.1, f32[8,8,320]{2,1,0:T(8,128)} %src_prev.1, f32[8,8,320]{2,1,0:T(8,128)} %rec_now.1, f32[8,8,320]{2,1,0:T(8,128)} %rec_prev.1, f32[8,8,320]{2,1,0:T(8,128)} %speed.1, f32[10,64]{1,0:T(8,128)} %traces.1, ...), custom_call_target="tpu_custom_call" | custom-call | tf_op jit(solution)/shard_map/pallas_call | solution.py:559
  2.5 1.1 %collective-permute-done = f32[16,64]{1,0:T(8,128)S(1)} collective-permute-done((f32[16,64]{1,0:T(8,128)S(1)}, f32[16,64]{1,0:T(8,128)S(1)}, u32[]{:S(2)}, u32[]{:S(2)}) %collective-permute-start) | collective-permute-done | bytes 4128 | tf_op jit(solution)/shard_map/ppermute | solution.py:571
  3.9 3.0 %collective-permute-start.2 = (f32[17,40,128]{2,1,0:T(8,128)S(1)}, f32[17,40,128]{2,1,0:T(8,128)S(1)}, u32[]{:S(2)}, u32[]{:S(2)}) collective-permute-start(f32[17,40,128]{2,1,0:T(8,128)S(1)} %get-tuple-element.52), channel_id=1, source_target_pairs={{0,4},{1,5},{2,6},{3,7},{4,0},{5,1},{6,2},{7,3},{8,12},{9,13},{10,... | collective-permute-start | bytes 1044488 | tf_op jit(solution)/shard_map/ppermute | solution.py:659
  6.9 1.5 %collective-permute-start.3 = (f32[9,40,128]{2,1,0:T(8,128)S(1)}, f32[9,40,128]{2,1,0:T(8,128)S(1)}, u32[]{:S(2)}, u32[]{:S(2)}) collective-permute-start(f32[9,40,128]{2,1,0:T(8,128)S(1)} %get-tuple-element.53), channel_id=1, source_target_pairs={{0,2},{1,3},{2,0},{3,1},{4,6},{5,7},{6,4},{7,5},{8,10},{9,11},{10,... | collective-permute-start | bytes 552968 | tf_op jit(solution)/shard_map/ppermute | solution.py:660
  8.4 3.1 %collective-permute-start.4 = (f32[3,24,128]{2,1,0:T(8,128)S(1)}, f32[3,24,128]{2,1,0:T(8,128)S(1)}, u32[]{:S(2)}, u32[]{:S(2)}) collective-permute-start(f32[3,24,128]{2,1,0:T(8,128)S(1)} %get-tuple-element.54), channel_id=1, source_target_pairs={{0,6},{1,7},{2,4},{3,5},{4,2},{5,3},{6,0},{7,1},{8,14},{9,15},{10,... | collective-permute-start | bytes 110600 | tf_op jit(solution)/shard_map/ppermute | solution.py:662
  12.2 0.5 collective-permute-done.5.refs_8_
  12.7 4.5 %collective-permute-done.4.refs_4_.refs_7_ = f32[3,24,128]{2,1,0:T(8,128)S(1)} collective-permute-done((f32[3,24,128]{2,1,0:T(8,128)S(1)}, f32[3,24,128]{2,1,0:T(8,128)S(1)}, u32[]{:S(2)}, u32[]{:S(2)}) %collective-permute-start.4) | collective-permute-done | bytes 36896 | tf_op jit(solution)/shard_map/ppermute | solution.py:662
  17.3 3.3 %collective-permute-start.6 = (f32[4,16,128]{2,1,0:T(8,128)S(1)}, f32[4,16,128]{2,1,0:T(8,128)S(1)}, u32[]{:S(2)}, u32[]{:S(2)}) collective-permute-start(f32[4,16,128]{2,1,0:T(8,128)S(1)} %shard_map.165), channel_id=1, source_target_pairs={{0,8},{1,9},{2,10},{3,11},{4,12},{5,13},{6,14},{7,15},{8,0},{9,1},... | collective-permute-start | bytes 98312 | tf_op jit(solution)/shard_map/ppermute | solution.py:590
  20.5 1.4 %shard_map.166 = (f32[16,3,24,128]{3,2,1,0:T(8,128)S(1)}, f32[16,3,24,128]{3,2,1,0:T(8,128)S(1)}) custom-call(f32[8,3,16,128]{3,2,1,0:T(8,128)S(1)} %get-tuple-element.57.refs_0_.refs_6_, f32[8,3,16,128]{3,2,1,0:T(8,128)S(1)} %get-tuple-element.58.refs_1_, f32[8,3,16,128]{3,2,1,0:T(8,128)S(1)} %get-tuple-element.59.refs_2_, ...), custom_call_target="tpu_custom_call" | custom-call | tf_op jit(solution)/shard_map/pallas_call | solution.py:559
  22.9 0.9 %shard_map.168 = (f32[16,3,24,128]{3,2,1,0:T(8,128)S(1)}, f32[10,8,3,16,128]{4,3,2,1,0:T(8,128)S(1)}, f32[8,40,128]{2,1,0:T(8,128)S(1)}, f32[4,40,128]{2,1,0:T(8...) custom-call(s32[1]{0:T(128)S(6)} %copy.36.refs_0_, ...), custom_call_target="tpu_custom_call", output_to_operand_aliasing={{0}: (3, {})} | custom-call | tf_op jit(solution)/shard_map/pallas_call | solution.py:559
  24.0 3.5 %collective-permute-start.8 = (f32[8,40,128]{2,1,0:T(8,128)S(1)}, f32[8,40,128]{2,1,0:T(8,128)S(1)}, u32[]{:S(2)}, u32[]{:S(2)}) collective-permute-start(f32[8,40,128]{2,1,0:T(8,128)S(1)} %get-tuple-element.68), channel_id=1, source_target_pairs={{0,4},{1,5},{2,6},{3,7},{4,0},{5,1},{6,2},{7,3},{8,12},{9,13},{10,... | collective-permute-start | bytes 491528 | tf_op jit(solution)/shard_map/ppermute | solution.py:659
  28.0 0.9 %collective-permute-start.11 = (f32[2,24,128]{2,1,0:T(8,128)S(1)}, f32[2,24,128]{2,1,0:T(8,128)S(1)}, u32[]{:S(2)}, u32[]{:S(2)}) collective-permute-start(f32[2,24,128]{2,1,0:T(8,128)S(1)} %get-tuple-element.70), channel_id=1, source_target_pairs={{0,6},{1,7},{2,4},{3,5},{4,2},{5,3},{6,0},{7,1},{8,14},{9,15},{10,... | collective-permute-start | bytes 73736 | tf_op jit(solution)/shard_map/ppermute | solution.py:662
  28.9 3.0 %collective-permute-done.10.refs_5_ = f32[4,40,128]{2,1,0:T(8,128)S(1)} collective-permute-done((f32[4,40,128]{2,1,0:T(8,128)S(1)}, f32[4,40,128]{2,1,0:T(8,128)S(1)}, u32[]{:S(2)}, u32[]{:S(2)}) %collective-permute-start.10) | collective-permute-done | bytes 81952 | tf_op jit(solution)/shard_map/ppermute | solution.py:660
  31.9 1.3 %shard_map.169.refs_3_ = f32[16,3,24,128]{3,2,1,0:T(8,128)S(1)} custom-call(f32[10,8,3,16,128]{4,3,2,1,0:T(8,128)S(1)} %get-tuple-element.66.refs_0_.refs_6_, f32[16,3,24,128]{3,2,1,0:T(8,128)S(1)} %get-tuple-element.67.refs_1_, f32[16,3,24,128]{3,2,1,0:T(8,128)S(1)} %get-tuple-element.63.refs_4_.refs_2_, f32[8,40,128]{2,1,0:T(8,128)S(1)} %collective-permute-done.8.refs_3_, ...), custom_call_target="tpu_custom_call" | custom-call | tf_op jit(solution)/shard_map/pallas_call | solution.py:559
  33.2 0.9 %shard_map.170 = (f32[16,3,24,128]{3,2,1,0:T(8,128)S(1)}, f32[10,8,3,16,128]{4,3,2,1,0:T(8,128)S(1)}, f32[8,40,128]{2,1,0:T(8,128)S(1)}, f32[4,40,128]{2,1,0:T(8...) custom-call(s32[1]{0:T(128)S(6)} %copy.36.refs_0_, ...), custom_call_target="tpu_custom_call", output_to_operand_aliasing={{0}: (3, {}), {1}: (6, {})} | custom-call | tf_op jit(solution)/shard_map/pallas_call | solution.py:559
  34.2 2.7 %collective-permute-start.13 = (f32[8,40,128]{2,1,0:T(8,128)S(1)}, f32[8,40,128]{2,1,0:T(8,128)S(1)}, u32[]{:S(2)}, u32[]{:S(2)}) collective-permute-start(f32[8,40,128]{2,1,0:T(8,128)S(1)} %get-tuple-element.74), channel_id=1, source_target_pairs={{0,4},{1,5},{2,6},{3,7},{4,0},{5,1},{6,2},{7,3},{8,12},{9,13},{10,... | collective-permute-start | bytes 491528 | tf_op jit(solution)/shard_map/ppermute | solution.py:659
  37.5 0.9 %collective-permute-start.16 = (f32[2,24,128]{2,1,0:T(8,128)S(1)}, f32[2,24,128]{2,1,0:T(8,128)S(1)}, u32[]{:S(2)}, u32[]{:S(2)}) collective-permute-start(f32[2,24,128]{2,1,0:T(8,128)S(1)} %get-tuple-element.76), channel_id=1, source_target_pairs={{0,6},{1,7},{2,4},{3,5},{4,2},{5,3},{6,0},{7,1},{8,14},{9,15},{10,... | collective-permute-start | bytes 73736 | tf_op jit(solution)/shard_map/ppermute | solution.py:662
  38.4 3.2 %collective-permute-done.15.refs_5_ = f32[4,40,128]{2,1,0:T(8,128)S(1)} collective-permute-done((f32[4,40,128]{2,1,0:T(8,128)S(1)}, f32[4,40,128]{2,1,0:T(8,128)S(1)}, u32[]{:S(2)}, u32[]{:S(2)}) %collective-permute-start.15) | collective-permute-done | bytes 81952 | tf_op jit(solution)/shard_map/ppermute | solution.py:660
  41.6 1.3 %shard_map.171.refs_3_ = f32[16,3,24,128]{3,2,1,0:T(8,128)S(1)} custom-call(f32[10,8,3,16,128]{4,3,2,1,0:T(8,128)S(1)} %get-tuple-element.72.refs_0_.refs_6_, f32[16,3,24,128]{3,2,1,0:T(8,128)S(1)} %get-tuple-element.73.refs_1_, f32[16,3,24,128]{3,2,1,0:T(8,128)S(1)} %get-tuple-element.63.refs_4_.refs_2_, f32[8,40,128]{2,1,0:T(8,128)S(1)} %collective-permute-done.13.refs_3_, ...), custom_call_target="tpu_custom_call" | custom-call | tf_op jit(solution)/shard_map/pallas_call | solution.py:559
  43.0 0.9 %shard_map.172 = (f32[16,3,24,128]{3,2,1,0:T(8,128)S(1)}, f32[10,8,3,16,128]{4,3,2,1,0:T(8,128)S(1)}, f32[8,40,128]{2,1,0:T(8,128)S(1)}, f32[4,40,128]{2,1,0:T(8...) custom-call(s32[1]{0:T(128)S(6)} %copy.36.refs_0_, ...), custom_call_target="tpu_custom_call", output_to_operand_aliasing={{0}: (3, {}), {1}: (6, {})} | custom-call | tf_op jit(solution)/shard_map/pallas_call | solution.py:559
  44.0 4.1 %collective-permute-start.18 = (f32[8,40,128]{2,1,0:T(8,128)S(1)}, f32[8,40,128]{2,1,0:T(8,128)S(1)}, u32[]{:S(2)}, u32[]{:S(2)}) collective-permute-start(f32[8,40,128]{2,1,0:T(8,128)S(1)} %get-tuple-element.80), channel_id=1, source_target_pairs={{0,4},{1,5},{2,6},{3,7},{4,0},{5,1},{6,2},{7,3},{8,12},{9,13},{10,... | collective-permute-start | bytes 491528 | tf_op jit(solution)/shard_map/ppermute | solution.py:659
  48.4 1.1 %collective-permute-start.21 = (f32[2,24,128]{2,1,0:T(8,128)S(1)}, f32[2,24,128]{2,1,0:T(8,128)S(1)}, u32[]{:S(2)}, u32[]{:S(2)}) collective-permute-start(f32[2,24,128]{2,1,0:T(8,128)S(1)} %get-tuple-element.82), channel_id=1, source_target_pairs={{0,6},{1,7},{2,4},{3,5},{4,2},{5,3},{6,0},{7,1},{8,14},{9,15},{10,... | collective-permute-start | bytes 73736 | tf_op jit(solution)/shard_map/ppermute | solution.py:662
  49.5 3.0 %collective-permute-done.20.refs_5_ = f32[4,40,128]{2,1,0:T(8,128)S(1)} collective-permute-done((f32[4,40,128]{2,1,0:T(8,128)S(1)}, f32[4,40,128]{2,1,0:T(8,128)S(1)}, u32[]{:S(2)}, u32[]{:S(2)}) %collective-permute-start.20) | collective-permute-done | bytes 81952 | tf_op jit(solution)/shard_map/ppermute | solution.py:660
  52.5 1.3 %shard_map.173.refs_3_ = f32[16,3,24,128]{3,2,1,0:T(8,128)S(1)} custom-call(f32[10,8,3,16,128]{4,3,2,1,0:T(8,128)S(1)} %get-tuple-element.78.refs_0_.refs_6_, f32[16,3,24,128]{3,2,1,0:T(8,128)S(1)} %get-tuple-element.79.refs_1_, f32[16,3,24,128]{3,2,1,0:T(8,128)S(1)} %get-tuple-element.63.refs_4_.refs_2_, f32[8,40,128]{2,1,0:T(8,128)S(1)} %collective-permute-done.18.refs_3_, ...), custom_call_target="tpu_custom_call" | custom-call | tf_op jit(solution)/shard_map/pallas_call | solution.py:559
  53.8 1.1 %shard_map.174 = (f32[16,3,24,128]{3,2,1,0:T(8,128)S(1)}, f32[10,8,3,16,128]{4,3,2,1,0:T(8,128)S(1)}, f32[8,40,128]{2,1,0:T(8,128)S(1)}, f32[4,40,128]{2,1,0:T(8...) custom-call(s32[1]{0:T(128)S(6)} %copy.36.refs_0_, ...), custom_call_target="tpu_custom_call", output_to_operand_aliasing={{0}: (3, {}), {1}: (6, {})} | custom-call | tf_op jit(solution)/shard_map/pallas_call | solution.py:559
  55.0 2.7 %collective-permute-start.23 = (f32[8,40,128]{2,1,0:T(8,128)S(1)}, f32[8,40,128]{2,1,0:T(8,128)S(1)}, u32[]{:S(2)}, u32[]{:S(2)}) collective-permute-start(f32[8,40,128]{2,1,0:T(8,128)S(1)} %get-tuple-element.86), channel_id=1, source_target_pairs={{0,4},{1,5},{2,6},{3,7},{4,0},{5,1},{6,2},{7,3},{8,12},{9,13},{10,... | collective-permute-start | bytes 491528 | tf_op jit(solution)/shard_map/ppermute | solution.py:659
  58.1 1.2 %collective-permute-start.26 = (f32[2,24,128]{2,1,0:T(8,128)S(1)}, f32[2,24,128]{2,1,0:T(8,128)S(1)}, u32[]{:S(2)}, u32[]{:S(2)}) collective-permute-start(f32[2,24,128]{2,1,0:T(8,128)S(1)} %get-tuple-element.88), channel_id=1, source_target_pairs={{0,6},{1,7},{2,4},{3,5},{4,2},{5,3},{6,0},{7,1},{8,14},{9,15},{10,... | collective-permute-start | bytes 73736 | tf_op jit(solution)/shard_map/ppermute | solution.py:662
  59.3 3.2 %collective-permute-done.25.refs_5_ = f32[4,40,128]{2,1,0:T(8,128)S(1)} collective-permute-done((f32[4,40,128]{2,1,0:T(8,128)S(1)}, f32[4,40,128]{2,1,0:T(8,128)S(1)}, u32[]{:S(2)}, u32[]{:S(2)}) %collective-permute-start.25) | collective-permute-done | bytes 81952 | tf_op jit(solution)/shard_map/ppermute | solution.py:660
  62.4 1.3 %shard_map.175.refs_3_ = f32[16,3,24,128]{3,2,1,0:T(8,128)S(1)} custom-call(f32[10,8,3,16,128]{4,3,2,1,0:T(8,128)S(1)} %get-tuple-element.84.refs_0_.refs_6_, f32[16,3,24,128]{3,2,1,0:T(8,128)S(1)} %get-tuple-element.85.refs_1_, f32[16,3,24,128]{3,2,1,0:T(8,128)S(1)} %get-tuple-element.63.refs_4_.refs_2_, f32[8,40,128]{2,1,0:T(8,128)S(1)} %collective-permute-done.23.refs_3_, ...), custom_call_target="tpu_custom_call" | custom-call | tf_op jit(solution)/shard_map/pallas_call | solution.py:559
  63.8 1.1 %shard_map.176 = (f32[16,3,24,128]{3,2,1,0:T(8,128)S(1)}, f32[10,8,3,16,128]{4,3,2,1,0:T(8,128)S(1)}, f32[5,8,3,8,128]{4,3,2,1,0:T(8,128)S(1)}, f32[5,8,3,8,128]{4,3,2,1,0:T(8,128)S(1)}) custom-call(s32[1]{0:T(128)S(6)} %copy.36.refs_0_, s32[1,4]{1,0:T(1,128)S(1)} %bitcast.8, f32[1,10]{1,0:T(1,128)S(1)} %bitcast.13, ...), custom_call_target="tpu_custom_call", output_to_operand_aliasing={{0}: (3, {}), {1}: (6, {})} | custom-call | tf_op jit(solution)/shard_map/pallas_call | solution.py:559
  65.0 1.9 %collective-permute-done.28.theirs = f32[5,8,3,8,128]{4,3,2,1,0:T(8,128)S(1)} collective-permute-done((f32[5,8,3,8,128]{4,3,2,1,0:T(8,128)S(1)}, f32[5,8,3,8,128]{4,3,2,1,0:T(8,128)S(1)}, u32[]{:S(2)}, u32[]{:S(2)}) %collective-permute-start.28) | collective-permute-done | bytes 491552 | tf_op jit(solution)/shard_map/ppermute | solution.py:709
  66.8 0.9 %shard_map.177 = (f32[8,8,320]{2,1,0:T(8,128)}, f32[8,8,320]{2,1,0:T(8,128)}, f32[8,8,320]{2,1,0:T(8,128)}, f32[8,8,320]{2,1,0:T(8,128)}, bf16[4,8,8,320]{3,2,1,0:T(8,128)(2,1)}, /*index=5*/f32[8,8,320]{2,1,0:T(8,128)}) custom-call(f32[5,8,3,8,128]{4,3,2,1,0:T(8,128)S(1)} %get-tuple-element.90.own, f32[5,8,3,8,128]{4,3,2,1,0:T(8,128)S(1)} %collective-permute-done.28.theirs, ...), custom_call_target="tpu_custom_call" | custom-call | tf_op jit(solution)/shard_map/pallas_call | solution.py:559
  (51 shorter events, 4.1 us)
Async XLA Ops:
  0.6 22.3 %copy-start.2 = (s32[4]{0:T(128)S(1)}, s32[4]{0:T(128)}, u32[]{:S(2)}) copy-start(s32[4]{0:T(128)} %param.21) | copy-start | bytes 52
  0.6 22.3 %copy-start.3 = (f32[10]{0:T(128)S(1)}, f32[10]{0:T(128)}, u32[]{:S(2)}) copy-start(f32[10]{0:T(128)} %param.17) | copy-start | bytes 124
  1.9 1.8 %collective-permute-start.1 = (f32[3,8,8,320]{3,2,1,0:T(8,128)S(1)}, f32[3,8,8,320]{3,2,1,0:T(8,128)S(1)}, u32[]{:S(2)}, u32[]{:S(2)}) collective-permute-start(f32[3,8,8,320]{3,2,1,0:T(8,128)S(1)} %get-tuple-element.51), channel_id=1, source_target_pairs={{0,1},{1,0},{2,3},{3,2},{4,5},{5,4},{6,7},{7,6},{8,9},{9,8},{10,11... | collective-permute-start | bytes 737288 | tf_op jit(solution)/shard_map/ppermute | solution.py:630
  2.4 1.2 %collective-permute-start = (f32[16,64]{1,0:T(8,128)S(1)}, f32[16,64]{1,0:T(8,128)S(1)}, u32[]{:S(2)}, u32[]{:S(2)}) collective-permute-start(f32[16,64]{1,0:T(8,128)S(1)} %get-tuple-element.49), channel_id=1, source_target_pairs={{0,1},{1,0},{2,3},{3,2},{4,5},{5,4},{6,7},{7,6},{8,9},{9,8},{10,11... | collective-permute-start | bytes 12296 | tf_op jit(solution)/shard_map/ppermute | solution.py:571
  3.9 13.3 %collective-permute-start.2 = (f32[17,40,128]{2,1,0:T(8,128)S(1)}, f32[17,40,128]{2,1,0:T(8,128)S(1)}, u32[]{:S(2)}, u32[]{:S(2)}) collective-permute-start(f32[17,40,128]{2,1,0:T(8,128)S(1)} %get-tuple-element.52), channel_id=1, source_target_pairs={{0,4},{1,5},{2,6},{3,7},{4,0},{5,1},{6,2},{7,3},{8,12},{9,13},{10,... | collective-permute-start | bytes 1044488 | tf_op jit(solution)/shard_map/ppermute | solution.py:659
  6.9 13.6 %collective-permute-start.7 = (f32[16,40,128]{2,1,0:T(8,128)S(1)}, f32[16,40,128]{2,1,0:T(8,128)S(1)}, u32[]{:S(2)}, u32[]{:S(2)}) collective-permute-start(f32[16,40,128]{2,1,0:T(8,128)S(1)} %get-tuple-element.60), channel_id=1, source_target_pairs={{0,1},{1,0},{2,3},{3,2},{4,8},{5,9},{6,10},{7,11},{8,4},{9,5},{10,... | collective-permute-start | bytes 983048 | tf_op jit(solution)/shard_map/ppermute | solution.py:659
  6.9 10.3 %collective-permute-start.3 = (f32[9,40,128]{2,1,0:T(8,128)S(1)}, f32[9,40,128]{2,1,0:T(8,128)S(1)}, u32[]{:S(2)}, u32[]{:S(2)}) collective-permute-start(f32[9,40,128]{2,1,0:T(8,128)S(1)} %get-tuple-element.53), channel_id=1, source_target_pairs={{0,2},{1,3},{2,0},{3,1},{4,6},{5,7},{6,4},{7,5},{8,10},{9,11},{10,... | collective-permute-start | bytes 552968 | tf_op jit(solution)/shard_map/ppermute | solution.py:660
  8.4 8.8 %collective-permute-start.4 = (f32[3,24,128]{2,1,0:T(8,128)S(1)}, f32[3,24,128]{2,1,0:T(8,128)S(1)}, u32[]{:S(2)}, u32[]{:S(2)}) collective-permute-start(f32[3,24,128]{2,1,0:T(8,128)S(1)} %get-tuple-element.54), channel_id=1, source_target_pairs={{0,6},{1,7},{2,4},{3,5},{4,2},{5,3},{6,0},{7,1},{8,14},{9,15},{10,... | collective-permute-start | bytes 110600 | tf_op jit(solution)/shard_map/ppermute | solution.py:662
  11.5 1.2 %collective-permute-start.5 = (f32[2,24,128]{2,1,0:T(8,128)S(1)}, f32[2,24,128]{2,1,0:T(8,128)S(1)}, u32[]{:S(2)}, u32[]{:S(2)}) collective-permute-start(f32[2,24,128]{2,1,0:T(8,128)S(1)} %get-tuple-element.55), channel_id=1, source_target_pairs={{0,1},{1,0},{2,3},{3,2},{4,10},{5,11},{6,8},{7,9},{8,6},{9,7},{10,... | collective-permute-start | bytes 73736 | tf_op jit(solution)/shard_map/ppermute | solution.py:662
  17.3 5.2 %collective-permute-start.6 = (f32[4,16,128]{2,1,0:T(8,128)S(1)}, f32[4,16,128]{2,1,0:T(8,128)S(1)}, u32[]{:S(2)}, u32[]{:S(2)}) collective-permute-start(f32[4,16,128]{2,1,0:T(8,128)S(1)} %shard_map.165), channel_id=1, source_target_pairs={{0,8},{1,9},{2,10},{3,11},{4,12},{5,13},{6,14},{7,15},{8,0},{9,1},... | collective-permute-start | bytes 98312 | tf_op jit(solution)/shard_map/ppermute | solution.py:590
  23.9 8.0 %collective-permute-start.9 = (f32[8,40,128]{2,1,0:T(8,128)S(1)}, f32[8,40,128]{2,1,0:T(8,128)S(1)}, u32[]{:S(2)}, u32[]{:S(2)}) collective-permute-start(f32[8,40,128]{2,1,0:T(8,128)S(1)} %get-tuple-element.68), channel_id=1, source_target_pairs={{0,1},{1,0},{2,3},{3,2},{4,8},{5,9},{6,10},{7,11},{8,4},{9,5},{10,... | collective-permute-start | bytes 491528 | tf_op jit(solution)/shard_map/ppermute | solution.py:659
  24.0 7.9 %collective-permute-start.8 = (f32[8,40,128]{2,1,0:T(8,128)S(1)}, f32[8,40,128]{2,1,0:T(8,128)S(1)}, u32[]{:S(2)}, u32[]{:S(2)}) collective-permute-start(f32[8,40,128]{2,1,0:T(8,128)S(1)} %get-tuple-element.68), channel_id=1, source_target_pairs={{0,4},{1,5},{2,6},{3,7},{4,0},{5,1},{6,2},{7,3},{8,12},{9,13},{10,... | collective-permute-start | bytes 491528 | tf_op jit(solution)/shard_map/ppermute | solution.py:659
  27.4 4.4 %collective-permute-start.10 = (f32[4,40,128]{2,1,0:T(8,128)S(1)}, f32[4,40,128]{2,1,0:T(8,128)S(1)}, u32[]{:S(2)}, u32[]{:S(2)}) collective-permute-start(f32[4,40,128]{2,1,0:T(8,128)S(1)} %get-tuple-element.69), channel_id=1, source_target_pairs={{0,2},{1,3},{2,0},{3,1},{4,6},{5,7},{6,4},{7,5},{8,10},{9,11},{10,... | collective-permute-start | bytes 245768 | tf_op jit(solution)/shard_map/ppermute | solution.py:660
  28.0 5.2 %collective-permute-start.11 = (f32[2,24,128]{2,1,0:T(8,128)S(1)}, f32[2,24,128]{2,1,0:T(8,128)S(1)}, u32[]{:S(2)}, u32[]{:S(2)}) collective-permute-start(f32[2,24,128]{2,1,0:T(8,128)S(1)} %get-tuple-element.70), channel_id=1, source_target_pairs={{0,6},{1,7},{2,4},{3,5},{4,2},{5,3},{6,0},{7,1},{8,14},{9,15},{10,... | collective-permute-start | bytes 73736 | tf_op jit(solution)/shard_map/ppermute | solution.py:662
  28.9 4.3 %collective-permute-start.12 = (f32[2,24,128]{2,1,0:T(8,128)S(1)}, f32[2,24,128]{2,1,0:T(8,128)S(1)}, u32[]{:S(2)}, u32[]{:S(2)}) collective-permute-start(f32[2,24,128]{2,1,0:T(8,128)S(1)} %get-tuple-element.71), channel_id=1, source_target_pairs={{0,1},{1,0},{2,3},{3,2},{4,10},{5,11},{6,8},{7,9},{8,6},{9,7},{10,... | collective-permute-start | bytes 73736 | tf_op jit(solution)/shard_map/ppermute | solution.py:662
  34.2 7.5 %collective-permute-start.14 = (f32[8,40,128]{2,1,0:T(8,128)S(1)}, f32[8,40,128]{2,1,0:T(8,128)S(1)}, u32[]{:S(2)}, u32[]{:S(2)}) collective-permute-start(f32[8,40,128]{2,1,0:T(8,128)S(1)} %get-tuple-element.74), channel_id=1, source_target_pairs={{0,1},{1,0},{2,3},{3,2},{4,8},{5,9},{6,10},{7,11},{8,4},{9,5},{10,... | collective-permute-start | bytes 491528 | tf_op jit(solution)/shard_map/ppermute | solution.py:659
  34.2 7.4 %collective-permute-start.13 = (f32[8,40,128]{2,1,0:T(8,128)S(1)}, f32[8,40,128]{2,1,0:T(8,128)S(1)}, u32[]{:S(2)}, u32[]{:S(2)}) collective-permute-start(f32[8,40,128]{2,1,0:T(8,128)S(1)} %get-tuple-element.74), channel_id=1, source_target_pairs={{0,4},{1,5},{2,6},{3,7},{4,0},{5,1},{6,2},{7,3},{8,12},{9,13},{10,... | collective-permute-start | bytes 491528 | tf_op jit(solution)/shard_map/ppermute | solution.py:659
  36.9 4.7 %collective-permute-start.15 = (f32[4,40,128]{2,1,0:T(8,128)S(1)}, f32[4,40,128]{2,1,0:T(8,128)S(1)}, u32[]{:S(2)}, u32[]{:S(2)}) collective-permute-start(f32[4,40,128]{2,1,0:T(8,128)S(1)} %get-tuple-element.75), channel_id=1, source_target_pairs={{0,2},{1,3},{2,0},{3,1},{4,6},{5,7},{6,4},{7,5},{8,10},{9,11},{10,... | collective-permute-start | bytes 245768 | tf_op jit(solution)/shard_map/ppermute | solution.py:660
  37.5 5.5 %collective-permute-start.16 = (f32[2,24,128]{2,1,0:T(8,128)S(1)}, f32[2,24,128]{2,1,0:T(8,128)S(1)}, u32[]{:S(2)}, u32[]{:S(2)}) collective-permute-start(f32[2,24,128]{2,1,0:T(8,128)S(1)} %get-tuple-element.76), channel_id=1, source_target_pairs={{0,6},{1,7},{2,4},{3,5},{4,2},{5,3},{6,0},{7,1},{8,14},{9,15},{10,... | collective-permute-start | bytes 73736 | tf_op jit(solution)/shard_map/ppermute | solution.py:662
  38.4 4.6 %collective-permute-start.17 = (f32[2,24,128]{2,1,0:T(8,128)S(1)}, f32[2,24,128]{2,1,0:T(8,128)S(1)}, u32[]{:S(2)}, u32[]{:S(2)}) collective-permute-start(f32[2,24,128]{2,1,0:T(8,128)S(1)} %get-tuple-element.77), channel_id=1, source_target_pairs={{0,1},{1,0},{2,3},{3,2},{4,10},{5,11},{6,8},{7,9},{8,6},{9,7},{10,... | collective-permute-start | bytes 73736 | tf_op jit(solution)/shard_map/ppermute | solution.py:662
  43.9 8.6 %collective-permute-start.19 = (f32[8,40,128]{2,1,0:T(8,128)S(1)}, f32[8,40,128]{2,1,0:T(8,128)S(1)}, u32[]{:S(2)}, u32[]{:S(2)}) collective-permute-start(f32[8,40,128]{2,1,0:T(8,128)S(1)} %get-tuple-element.80), channel_id=1, source_target_pairs={{0,1},{1,0},{2,3},{3,2},{4,8},{5,9},{6,10},{7,11},{8,4},{9,5},{10,... | collective-permute-start | bytes 491528 | tf_op jit(solution)/shard_map/ppermute | solution.py:659
  44.0 8.5 %collective-permute-start.18 = (f32[8,40,128]{2,1,0:T(8,128)S(1)}, f32[8,40,128]{2,1,0:T(8,128)S(1)}, u32[]{:S(2)}, u32[]{:S(2)}) collective-permute-start(f32[8,40,128]{2,1,0:T(8,128)S(1)} %get-tuple-element.80), channel_id=1, source_target_pairs={{0,4},{1,5},{2,6},{3,7},{4,0},{5,1},{6,2},{7,3},{8,12},{9,13},{10,... | collective-permute-start | bytes 491528 | tf_op jit(solution)/shard_map/ppermute | solution.py:659
  48.0 4.4 %collective-permute-start.20 = (f32[4,40,128]{2,1,0:T(8,128)S(1)}, f32[4,40,128]{2,1,0:T(8,128)S(1)}, u32[]{:S(2)}, u32[]{:S(2)}) collective-permute-start(f32[4,40,128]{2,1,0:T(8,128)S(1)} %get-tuple-element.81), channel_id=1, source_target_pairs={{0,2},{1,3},{2,0},{3,1},{4,6},{5,7},{6,4},{7,5},{8,10},{9,11},{10,... | collective-permute-start | bytes 245768 | tf_op jit(solution)/shard_map/ppermute | solution.py:660
  48.4 5.4 %collective-permute-start.21 = (f32[2,24,128]{2,1,0:T(8,128)S(1)}, f32[2,24,128]{2,1,0:T(8,128)S(1)}, u32[]{:S(2)}, u32[]{:S(2)}) collective-permute-start(f32[2,24,128]{2,1,0:T(8,128)S(1)} %get-tuple-element.82), channel_id=1, source_target_pairs={{0,6},{1,7},{2,4},{3,5},{4,2},{5,3},{6,0},{7,1},{8,14},{9,15},{10,... | collective-permute-start | bytes 73736 | tf_op jit(solution)/shard_map/ppermute | solution.py:662
  49.5 4.3 %collective-permute-start.22 = (f32[2,24,128]{2,1,0:T(8,128)S(1)}, f32[2,24,128]{2,1,0:T(8,128)S(1)}, u32[]{:S(2)}, u32[]{:S(2)}) collective-permute-start(f32[2,24,128]{2,1,0:T(8,128)S(1)} %get-tuple-element.83), channel_id=1, source_target_pairs={{0,1},{1,0},{2,3},{3,2},{4,10},{5,11},{6,8},{7,9},{8,6},{9,7},{10,... | collective-permute-start | bytes 73736 | tf_op jit(solution)/shard_map/ppermute | solution.py:662
  54.9 7.5 %collective-permute-start.24 = (f32[8,40,128]{2,1,0:T(8,128)S(1)}, f32[8,40,128]{2,1,0:T(8,128)S(1)}, u32[]{:S(2)}, u32[]{:S(2)}) collective-permute-start(f32[8,40,128]{2,1,0:T(8,128)S(1)} %get-tuple-element.86), channel_id=1, source_target_pairs={{0,1},{1,0},{2,3},{3,2},{4,8},{5,9},{6,10},{7,11},{8,4},{9,5},{10,... | collective-permute-start | bytes 491528 | tf_op jit(solution)/shard_map/ppermute | solution.py:659
  55.0 7.4 %collective-permute-start.23 = (f32[8,40,128]{2,1,0:T(8,128)S(1)}, f32[8,40,128]{2,1,0:T(8,128)S(1)}, u32[]{:S(2)}, u32[]{:S(2)}) collective-permute-start(f32[8,40,128]{2,1,0:T(8,128)S(1)} %get-tuple-element.86), channel_id=1, source_target_pairs={{0,4},{1,5},{2,6},{3,7},{4,0},{5,1},{6,2},{7,3},{8,12},{9,13},{10,... | collective-permute-start | bytes 491528 | tf_op jit(solution)/shard_map/ppermute | solution.py:659
  57.7 4.7 %collective-permute-start.25 = (f32[4,40,128]{2,1,0:T(8,128)S(1)}, f32[4,40,128]{2,1,0:T(8,128)S(1)}, u32[]{:S(2)}, u32[]{:S(2)}) collective-permute-start(f32[4,40,128]{2,1,0:T(8,128)S(1)} %get-tuple-element.87), channel_id=1, source_target_pairs={{0,2},{1,3},{2,0},{3,1},{4,6},{5,7},{6,4},{7,5},{8,10},{9,11},{10,... | collective-permute-start | bytes 245768 | tf_op jit(solution)/shard_map/ppermute | solution.py:660
  58.1 5.7 %collective-permute-start.26 = (f32[2,24,128]{2,1,0:T(8,128)S(1)}, f32[2,24,128]{2,1,0:T(8,128)S(1)}, u32[]{:S(2)}, u32[]{:S(2)}) collective-permute-start(f32[2,24,128]{2,1,0:T(8,128)S(1)} %get-tuple-element.88), channel_id=1, source_target_pairs={{0,6},{1,7},{2,4},{3,5},{4,2},{5,3},{6,0},{7,1},{8,14},{9,15},{10,... | collective-permute-start | bytes 73736 | tf_op jit(solution)/shard_map/ppermute | solution.py:662
  59.3 4.5 %collective-permute-start.27 = (f32[2,24,128]{2,1,0:T(8,128)S(1)}, f32[2,24,128]{2,1,0:T(8,128)S(1)}, u32[]{:S(2)}, u32[]{:S(2)}) collective-permute-start(f32[2,24,128]{2,1,0:T(8,128)S(1)} %get-tuple-element.89), channel_id=1, source_target_pairs={{0,1},{1,0},{2,3},{3,2},{4,10},{5,11},{6,8},{7,9},{8,6},{9,7},{10,... | collective-permute-start | bytes 73736 | tf_op jit(solution)/shard_map/ppermute | solution.py:662
  63.7 3.1 %copy-start = (bf16[4,8,8,320]{3,2,1,0:T(8,128)(2,1)S(1)}, bf16[4,8,8,320]{3,2,1,0:T(8,128)(2,1)}, u32[]{:S(2)}) copy-start(bf16[4,8,8,320]{3,2,1,0:T(8,128)(2,1)} %stored.1) | copy-start | bytes 491524
  64.9 1.9 %collective-permute-start.28 = (f32[5,8,3,8,128]{4,3,2,1,0:T(8,128)S(1)}, f32[5,8,3,8,128]{4,3,2,1,0:T(8,128)S(1)}, u32[]{:S(2)}, u32[]{:S(2)}) collective-permute-start(f32[5,8,3,8,128]{4,3,2,1,0:T(8,128)S(1)} %get-tuple-element.91), channel_id=1, source_target_pairs={{0,1},{1,0},{2,3},{3,2},{4,5},{5,4},{6,7},{7,6},{8,9},{9,8},{10,11... | collective-permute-start | bytes 1474568 | tf_op jit(solution)/shard_map/ppermute | solution.py:709
  (1 other events, 3.1 us)

commit v6 on v5

--- a/solution.py
+++ b/solution.py
@@ -53,9 +53,18 @@
         return self.permutation(lambda x, c: (x, c + (1 if c % 2 == py else -1)))
 
     def d_permutation(self, pz, py):
-        return self.permutation(
-            lambda x, c: (x + (1 if x % 2 == pz else -1), c + (1 if c % 2 == py else -1))
-        )
+        pairs = []
+        for x in range(self.nx):
+            for column in range(self.columns):
+                beside = x + (1 if x % 2 == pz else -1)
+                there = column + (1 if column % 2 == py else -1)
+                for core in (0, 1):
+                    if not 0 <= there < self.columns:
+                        target = self.device(x, column, 1 - core)
+                    else:
+                        target = self.device(beside if 0 <= beside < self.nx else x, there, core)
+                    pairs.append((self.device(x, column, core), target))
+        return pairs
 
     def carriers(self, z_messages, y_messages, d_messages):
         starts = (self.bx + 2 * REACH, 2 * (self.bx // 2), REACH // 2)
@@ -336,7 +345,10 @@
         p = p.at[time - 1]
     z_in, refs = refs[:nz], refs[nz:]
     y_in, refs = refs[:ny], refs[ny:]
+    refs = refs if first else refs[1:]
     stepped, buffer = refs[0], refs[-1]
+    meet = refs[2] if first else refs[1]
+    meet[...] = jnp.zeros_like(meet)
     z_sides = [lay.z_side(pz) for pz in lay.z_parities]
     y_sides = [lay.y_side(py) for py in lay.y_parities]
     bx, cy, zt = lay.bx, lay.cy, lay.zt
@@ -367,7 +379,7 @@
                 buffer[own_x + x, t, pl.ds(start, ROWS), :] = jnp.where(valid, rows, 0.0)
 
     if first:
-        s_out, q_ext = refs[1:3]
+        s_out, q_ext = refs[1], refs[3]
         for lead, own, ext in ((0, q, q_ext), (1, s, s_out)):
             ext[...] = jnp.zeros_like(ext)
             for x in range(bx):
@@ -416,31 +428,29 @@
             turned = pltpu.roll(rows, REACH, 0)
             corner[x, t, ROWS : 2 * ROWS, :] = jnp.where(high, rows, turned) * keep
             corner[x + REACH // 2, t, ROWS : 2 * ROWS, :] = jnp.where(high, turned, rows) * keep
-    high_share, low_share = jnp.where(high, 1.0, 0.0), jnp.where(high, 0.0, 1.0)
     planes_start = jnp.where(right, REACH + lay.bx, 0)
     rows_start = jnp.where(right, lay.bx, REACH)
-    for x in range(REACH):
+
+    def add(is_high):
+        near = REACH + lay.cy - ROWS if is_high else REACH
+        edge, cut = (lay.ey - ROWS, REACH) if is_high else (0, 2 * ROWS - REACH)
         for t in range(lay.zt):
-            above = sum(STENCIL_COEFFS[k] * corner[x, t, k : k + ROWS, :] for k in range(1, REACH + 1))
-            below = sum(
-                STENCIL_COEFFS[k] * corner[x, t, 2 * ROWS - k : 3 * ROWS - k, :] for k in range(1, REACH + 1)
-            )
-            for share, amount, start in (
-                (high_share, above, REACH + lay.cy - ROWS),
-                (low_share, below, REACH),
-            ):
-                rows = slice(start, start + ROWS)
-                field[planes_start + x, t, rows, :] += s[planes_start + x, t, rows, :] * (amount * share)
-            for share, start, cut in (
-                (high_share, lay.ey - ROWS, REACH),
-                (low_share, 0, 2 * ROWS - REACH),
-            ):
-                source = [corner[j, t, cut : cut + ROWS, :] for j in range(REACH)]
+            source = [corner[j, t, cut : cut + ROWS, :] for j in range(REACH)]
+            for x in range(REACH):
+                amount = sum(
+                    STENCIL_COEFFS[k] * corner[x, t, pl.ds(k if is_high else 2 * ROWS - k, ROWS), :]
+                    for k in range(1, REACH + 1)
+                )
+                rows = slice(near, near + ROWS)
+                field[planes_start + x, t, rows, :] += s[planes_start + x, t, rows, :] * amount
                 from_left = sum(STENCIL_COEFFS[x + REACH - j] * source[j] for j in range(x, REACH))
                 from_right = sum(STENCIL_COEFFS[REACH + j - x] * source[j] for j in range(x + 1))
-                amount = jnp.where(right, from_right, from_left) * share
-                rows = slice(start, start + ROWS)
+                amount = jnp.where(right, from_right, from_left)
+                rows = slice(edge, edge + ROWS)
                 field[rows_start + x, t, rows, :] += s[rows_start + x, t, rows, :] * amount
+
+    pl.when(high)(functools.partial(add, True))
+    pl.when(jnp.logical_not(high))(functools.partial(add, False))
 
 
 def round_kernel(lay, time, *refs):
@@ -654,6 +664,7 @@
     (p, q, s), made = made[:3], made[3:]
     z_out, y_out, d_out = made[:nz], made[nz : nz + ny], made[nz + ny :]
 
+    met = []
     for time in range(0, steps, 2):
         begin, end = time == 0, time + 2 == steps
         z_in = [lax.ppermute(m, AXES, lay.z_permutation(pz)) for m, pz in zip(z_out, lay.z_parities)]
@@ -672,11 +683,12 @@
             gathered = spread(lay, gathered)
         made = call(
             functools.partial(side_kernel, lay, time),
-            [(ext, f32)] * (2 if begin else 1),
-            [p, q, s, *z_in, *y_in],
+            [(ext, f32)] * (2 if begin else 1) + [((ROWS, LANES), f32)],
+            [p, q, s, *z_in, *y_in, *met],
             [pltpu.VMEM(ext, f32)] * begin + [pltpu.VMEM(field, f32)],
         )
         stepped = made[0]
+        met = [lax.ppermute(made[-1], AXES, lay.core_permutation())]
         if begin:
             s = made[1]
             gathered, stepped = lax.optimization_barrier((gathered, stepped))
@@ -703,7 +715,8 @@
         if end:
             own, theirs = made[2:]
         else:
-            z_out = [made[2]] * nz
+            packed, met[0] = lax.optimization_barrier((made[2], met[0]))
+            z_out = [packed] * nz
             y_out, d_out = made[3 : 3 + ny], made[3 + ny :]
 
     theirs = lax.ppermute(theirs, AXES, lay.core_permutation())

time: 68 us -> 67.7 us (level)
  waiting for transfers between devices: 20.9 us -> 17.5 us
  starting transfers between devices: 30.7 us -> 33.7 us
    ppermute x10, starting transfers between devices: 7.28 us -> 10.5 us  [body(): d_in = [lax.ppermute(m, AXES, pairs) for m, pairs in zip(d_out, diagonals)]]
    ppermute x5, waiting for transfers between devices: 12.3 us -> 10.2 us  [body(): lax.ppermute(m, AXES, lay.y_permutation(py))]
    ppermute x10, waiting for transfers between devices: 5.08 us -> 3.59 us  [body(): d_in = [lax.ppermute(m, AXES, pairs) for m, pairs in zip(d_out, diagonals)]]
    ppermute x10, starting transfers between devices: 16.2 us -> 15.3 us  [body(): lax.ppermute(m, AXES, lay.z_permutation(pz))]
  transfers between devices with their start and end apart: 29 -> 33, of which waited for: 9 -> 11; matrix products, arithmetic and copies ran while one was open for 0% -> 0% of each run, Pallas kernels for 10% -> 17%
where the time goes in v6:
time: 67.7 us; the launch traced here: 67.5 us
  starting transfers between devices  33.7 us (50%)
  waiting for transfers between devices  17.5 us (26%)
  Pallas kernels  14.6 us (22%)
  between operations  1.56 us (2%)
    ppermute x10, starting transfers between devices, body(): lax.ppermute(m, AXES, lay.z_permutation(pz))  15.3 us
    pallas_call x15, Pallas kernels, call(): pl.pallas_call(kernel, out_shape=[jax.ShapeDtypeStruct(shape, dtype) for...  14.6 us
    ppermute x10, starting transfers between devices, body(): d_in = [lax.ppermute(m, AXES, pairs) for m, pairs in zip(d_out, diagonals)]  10.5 us
    ppermute x5, waiting for transfers between devices, body(): lax.ppermute(m, AXES, lay.y_permutation(py))  10.2 us
    ppermute x5, starting transfers between devices, body(): lax.ppermute(m, AXES, lay.y_permutation(py))  3.68 us
    ppermute x10, waiting for transfers between devices, body(): d_in = [lax.ppermute(m, AXES, pairs) for m, pairs in zip(d_out, diagonals)]  3.59 us
    ppermute x1, starting transfers between devices, spread(): message = jnp.concatenate([message, lax.ppermute(message, AXES, pairs)], 0)  3.26 us
    ppermute x1, waiting for transfers between devices, body(): theirs = lax.ppermute(theirs, AXES, lay.core_permutation())  1.85 us
  transfers between devices with their start and end apart: 33, of which 11 were waited for; matrix products, arithmetic and copies ran while one was open for 0% of the time, Pallas kernels for 17%

profile of v6, /device:TPU:0, one launch (start us, length us, event | category | flops | bytes accessed | tf_op | source)
XLA Modules:
  0.0 67.5 jit_solution(8142790822208254097)
XLA Ops:
  0.7 1.2 %shard_map.163 = (f32[3,8,8,320]{3,2,1,0:T(8,128)S(1)}, f32[3,8,8,320]{3,2,1,0:T(8,128)S(1)}, f32[16,64]{1,0:T(8,128)S(1)}) custom-call(f32[8,8,320]{2,1,0:T(8,128)} %src_now.1, f32[8,8,320]{2,1,0:T(8,128)} %src_prev.1, f32[8,8,320]{2,1,0:T(8,128)} %rec_now.1, f32[8,8,320]{2,1,0:T(8,128)} %rec_prev.1, f32[8,8,320]{2,1,0:T(8,128)} %speed.1, f32[10,64]{1,0:T(8,128)} %traces.1, ...), custom_call_target="tpu_custom_call" | custom-call | tf_op jit(solution)/shard_map/pallas_call | solution.py:569
  2.5 1.1 %collective-permute-done = f32[16,64]{1,0:T(8,128)S(1)} collective-permute-done((f32[16,64]{1,0:T(8,128)S(1)}, f32[16,64]{1,0:T(8,128)S(1)}, u32[]{:S(2)}, u32[]{:S(2)}) %collective-permute-start) | collective-permute-done | bytes 4128 | tf_op jit(solution)/shard_map/ppermute | solution.py:581
  3.9 3.0 %collective-permute-start.2 = (f32[17,40,128]{2,1,0:T(8,128)S(1)}, f32[17,40,128]{2,1,0:T(8,128)S(1)}, u32[]{:S(2)}, u32[]{:S(2)}) collective-permute-start(f32[17,40,128]{2,1,0:T(8,128)S(1)} %get-tuple-element.68), channel_id=1, source_target_pairs={{0,4},{1,5},{2,6},{3,7},{4,0},{5,1},{6,2},{7,3},{8,12},{9,13},{10,... | collective-permute-start | bytes 1044488 | tf_op jit(solution)/shard_map/ppermute | solution.py:670
  6.9 1.5 %collective-permute-start.3 = (f32[9,40,128]{2,1,0:T(8,128)S(1)}, f32[9,40,128]{2,1,0:T(8,128)S(1)}, u32[]{:S(2)}, u32[]{:S(2)}) collective-permute-start(f32[9,40,128]{2,1,0:T(8,128)S(1)} %get-tuple-element.69), channel_id=1, source_target_pairs={{0,2},{1,3},{2,0},{3,1},{4,6},{5,7},{6,4},{7,5},{8,10},{9,11},{10,... | collective-permute-start | bytes 552968 | tf_op jit(solution)/shard_map/ppermute | solution.py:671
  8.4 3.1 %collective-permute-start.4 = (f32[3,24,128]{2,1,0:T(8,128)S(1)}, f32[3,24,128]{2,1,0:T(8,128)S(1)}, u32[]{:S(2)}, u32[]{:S(2)}) collective-permute-start(f32[3,24,128]{2,1,0:T(8,128)S(1)} %get-tuple-element.70), channel_id=1, source_target_pairs={{0,6},{1,7},{2,4},{3,5},{4,2},{5,3},{6,0},{7,1},{8,14},{9,15},{10,... | collective-permute-start | bytes 110600 | tf_op jit(solution)/shard_map/ppermute | solution.py:673
  11.5 1.5 %collective-permute-start.5 = (f32[2,24,128]{2,1,0:T(8,128)S(1)}, f32[2,24,128]{2,1,0:T(8,128)S(1)}, u32[]{:S(2)}, u32[]{:S(2)}) collective-permute-start(f32[2,24,128]{2,1,0:T(8,128)S(1)} %get-tuple-element.71), channel_id=1, source_target_pairs={{0,2},{1,3},{2,0},{3,1},{4,10},{5,11},{6,8},{7,9},{8,6},{9,7},{10,... | collective-permute-start | bytes 73736 | tf_op jit(solution)/shard_map/ppermute | solution.py:673
  13.7 1.7 %collective-permute-done.5.refs_8_ = f32[2,24,128]{2,1,0:T(8,128)S(1)} collective-permute-done((f32[2,24,128]{2,1,0:T(8,128)S(1)}, f32[2,24,128]{2,1,0:T(8,128)S(1)}, u32[]{:S(2)}, u32[]{:S(2)}) %collective-permute-start.5) | collective-permute-done | bytes 24608 | tf_op jit(solution)/shard_map/ppermute | solution.py:673
  15.4 1.9 %collective-permute-done.4.refs_4_.refs_7_ = f32[3,24,128]{2,1,0:T(8,128)S(1)} collective-permute-done((f32[3,24,128]{2,1,0:T(8,128)S(1)}, f32[3,24,128]{2,1,0:T(8,128)S(1)}, u32[]{:S(2)}, u32[]{:S(2)}) %collective-permute-start.4) | collective-permute-done | bytes 36896 | tf_op jit(solution)/shard_map/ppermute | solution.py:673
  17.3 3.3 %collective-permute-start.6 = (f32[4,16,128]{2,1,0:T(8,128)S(1)}, f32[4,16,128]{2,1,0:T(8,128)S(1)}, u32[]{:S(2)}, u32[]{:S(2)}) collective-permute-start(f32[4,16,128]{2,1,0:T(8,128)S(1)} %shard_map.165), channel_id=1, source_target_pairs={{0,8},{1,9},{2,10},{3,11},{4,12},{5,13},{6,14},{7,15},{8,0},{9,1},... | collective-permute-start | bytes 98312 | tf_op jit(solution)/shard_map/ppermute | solution.py:600
  20.5 1.4 %shard_map.166 = (f32[16,3,24,128]{3,2,1,0:T(8,128)S(1)}, f32[16,3,24,128]{3,2,1,0:T(8,128)S(1)}, f32[8,128]{1,0:T(8,128)S(1)}) custom-call(f32[8,3,16,128]{3,2,1,0:T(8,128)S(1)} %get-tuple-element.73.refs_0_.refs_6_, f32[8,3,16,128]{3,2,1,0:T(8,128)S(1)} %get-tuple-element.74.refs_1_, f32[8,3,16,128]{3,2,1,0:T(8,128)S(1)} %get-tuple-element.75.refs_2_, ...), custom_call_target="tpu_custom_call" | custom-call | tf_op jit(solution)/shard_map/pallas_call | solution.py:569
  22.9 1.0 %shard_map.168 = (f32[16,3,24,128]{3,2,1,0:T(8,128)S(1)}, f32[10,8,3,16,128]{4,3,2,1,0:T(8,128)S(1)}, f32[8,40,128]{2,1,0:T(8,128)S(1)}, f32[4,40,128]{2,1,0:T(8...) custom-call(s32[1]{0:T(128)S(6)} %copy.36.refs_0_, ...), custom_call_target="tpu_custom_call", output_to_operand_aliasing={{0}: (3, {})} | custom-call | tf_op jit(solution)/shard_map/pallas_call | solution.py:569
  24.0 3.4 %collective-permute-start.9 = (f32[8,40,128]{2,1,0:T(8,128)S(1)}, f32[8,40,128]{2,1,0:T(8,128)S(1)}, u32[]{:S(2)}, u32[]{:S(2)}) collective-permute-start(f32[8,40,128]{2,1,0:T(8,128)S(1)} %get-tuple-element.86), channel_id=1, source_target_pairs={{0,4},{1,5},{2,6},{3,7},{4,0},{5,1},{6,2},{7,3},{8,12},{9,13},{10,... | collective-permute-start | bytes 491528 | tf_op jit(solution)/shard_map/ppermute | solution.py:670
  28.0 0.9 %collective-permute-start.12 = (f32[2,24,128]{2,1,0:T(8,128)S(1)}, f32[2,24,128]{2,1,0:T(8,128)S(1)}, u32[]{:S(2)}, u32[]{:S(2)}) collective-permute-start(f32[2,24,128]{2,1,0:T(8,128)S(1)} %get-tuple-element.90), channel_id=1, source_target_pairs={{0,6},{1,7},{2,4},{3,5},{4,2},{5,3},{6,0},{7,1},{8,14},{9,15},{10,... | collective-permute-start | bytes 73736 | tf_op jit(solution)/shard_map/ppermute | solution.py:673
  29.4 2.4 %collective-permute-done.11.refs_5_ = f32[4,40,128]{2,1,0:T(8,128)S(1)} collective-permute-done((f32[4,40,128]{2,1,0:T(8,128)S(1)}, f32[4,40,128]{2,1,0:T(8,128)S(1)}, u32[]{:S(2)}, u32[]{:S(2)}) %collective-permute-start.11) | collective-permute-done | bytes 81952 | tf_op jit(solution)/shard_map/ppermute | solution.py:671
  31.9 1.3 %shard_map.169 = (f32[16,3,24,128]{3,2,1,0:T(8,128)S(1)}, f32[8,128]{1,0:T(8,128)S(1)}) custom-call(f32[10,8,3,16,128]{4,3,2,1,0:T(8,128)S(1)} %get-tuple-element.82.refs_0_.refs_6_, f32[16,3,24,128]{3,2,1,0:T(8,128)S(1)} %get-tuple-element.83.refs_1_, f32[16,3,24,128]{3,2,1,0:T(8,128)S(1)} %get-tuple-element.79.refs_4_.refs_2_, ...), custom_call_target="tpu_custom_call" | custom-call | tf_op jit(solution)/shard_map/pallas_call | solution.py:569
  33.3 1.0 %shard_map.170 = (f32[16,3,24,128]{3,2,1,0:T(8,128)S(1)}, f32[10,8,3,16,128]{4,3,2,1,0:T(8,128)S(1)}, f32[8,40,128]{2,1,0:T(8,128)S(1)}, f32[4,40,128]{2,1,0:T(8...) custom-call(s32[1]{0:T(128)S(6)} %copy.36.refs_0_, ...), custom_call_target="tpu_custom_call", output_to_operand_aliasing={{0}: (3, {}), {1}: (6, {})} | custom-call | tf_op jit(solution)/shard_map/pallas_call | solution.py:569
  34.8 2.1 %collective-permute-start.15 = (f32[8,40,128]{2,1,0:T(8,128)S(1)}, f32[8,40,128]{2,1,0:T(8,128)S(1)}, u32[]{:S(2)}, u32[]{:S(2)}) collective-permute-start(f32[8,40,128]{2,1,0:T(8,128)S(1)} %get-tuple-element.96), channel_id=1, source_target_pairs={{0,4},{1,5},{2,6},{3,7},{4,0},{5,1},{6,2},{7,3},{8,12},{9,13},{10,... | collective-permute-start | bytes 491528 | tf_op jit(solution)/shard_map/ppermute | solution.py:670
  37.4 0.9 %collective-permute-start.18 = (f32[2,24,128]{2,1,0:T(8,128)S(1)}, f32[2,24,128]{2,1,0:T(8,128)S(1)}, u32[]{:S(2)}, u32[]{:S(2)}) collective-permute-start(f32[2,24,128]{2,1,0:T(8,128)S(1)} %get-tuple-element.100), channel_id=1, source_target_pairs={{0,6},{1,7},{2,4},{3,5},{4,2},{5,3},{6,0},{7,1},{8,14},{9,15},{10,... | collective-permute-start | bytes 73736 | tf_op jit(solution)/shard_map/ppermute | solution.py:673
  38.9 2.7 %collective-permute-done.17.refs_5_ = f32[4,40,128]{2,1,0:T(8,128)S(1)} collective-permute-done((f32[4,40,128]{2,1,0:T(8,128)S(1)}, f32[4,40,128]{2,1,0:T(8,128)S(1)}, u32[]{:S(2)}, u32[]{:S(2)}) %collective-permute-start.17) | collective-permute-done | bytes 81952 | tf_op jit(solution)/shard_map/ppermute | solution.py:671
  41.6 1.3 %shard_map.171 = (f32[16,3,24,128]{3,2,1,0:T(8,128)S(1)}, f32[8,128]{1,0:T(8,128)S(1)}) custom-call(f32[10,8,3,16,128]{4,3,2,1,0:T(8,128)S(1)} %get-tuple-element.92.refs_0_.refs_6_, f32[16,3,24,128]{3,2,1,0:T(8,128)S(1)} %get-tuple-element.93.refs_1_, f32[16,3,24,128]{3,2,1,0:T(8,128)S(1)} %get-tuple-element.79.refs_4_.refs_2_, ...), custom_call_target="tpu_custom_call" | custom-call | tf_op jit(solution)/shard_map/pallas_call | solution.py:569
  43.0 1.0 %shard_map.172 = (f32[16,3,24,128]{3,2,1,0:T(8,128)S(1)}, f32[10,8,3,16,128]{4,3,2,1,0:T(8,128)S(1)}, f32[8,40,128]{2,1,0:T(8,128)S(1)}, f32[4,40,128]{2,1,0:T(8...) custom-call(s32[1]{0:T(128)S(6)} %copy.36.refs_0_, ...), custom_call_target="tpu_custom_call", output_to_operand_aliasing={{0}: (3, {}), {1}: (6, {})} | custom-call | tf_op jit(solution)/shard_map/pallas_call | solution.py:569
  44.5 3.3 %collective-permute-start.21 = (f32[8,40,128]{2,1,0:T(8,128)S(1)}, f32[8,40,128]{2,1,0:T(8,128)S(1)}, u32[]{:S(2)}, u32[]{:S(2)}) collective-permute-start(f32[8,40,128]{2,1,0:T(8,128)S(1)} %get-tuple-element.106), channel_id=1, source_target_pairs={{0,4},{1,5},{2,6},{3,7},{4,0},{5,1},{6,2},{7,3},{8,12},{9,13},{10,... | collective-permute-start | bytes 491528 | tf_op jit(solution)/shard_map/ppermute | solution.py:670
  48.4 0.9 %collective-permute-start.24 = (f32[2,24,128]{2,1,0:T(8,128)S(1)}, f32[2,24,128]{2,1,0:T(8,128)S(1)}, u32[]{:S(2)}, u32[]{:S(2)}) collective-permute-start(f32[2,24,128]{2,1,0:T(8,128)S(1)} %get-tuple-element.110), channel_id=1, source_target_pairs={{0,6},{1,7},{2,4},{3,5},{4,2},{5,3},{6,0},{7,1},{8,14},{9,15},{10,... | collective-permute-start | bytes 73736 | tf_op jit(solution)/shard_map/ppermute | solution.py:673
  49.9 2.4 %collective-permute-done.23.refs_5_ = f32[4,40,128]{2,1,0:T(8,128)S(1)} collective-permute-done((f32[4,40,128]{2,1,0:T(8,128)S(1)}, f32[4,40,128]{2,1,0:T(8,128)S(1)}, u32[]{:S(2)}, u32[]{:S(2)}) %collective-permute-start.23) | collective-permute-done | bytes 81952 | tf_op jit(solution)/shard_map/ppermute | solution.py:671
  52.3 1.3 %shard_map.173 = (f32[16,3,24,128]{3,2,1,0:T(8,128)S(1)}, f32[8,128]{1,0:T(8,128)S(1)}) custom-call(f32[10,8,3,16,128]{4,3,2,1,0:T(8,128)S(1)} %get-tuple-element.102.refs_0_.refs_6_, f32[16,3,24,128]{3,2,1,0:T(8,128)S(1)} %get-tuple-element.103.refs_1_, f32[16,3,24,128]{3,2,1,0:T(8,128)S(1)} %get-tuple-element.79.refs_4_.refs_2_, ...), custom_call_target="tpu_custom_call" | custom-call | tf_op jit(solution)/shard_map/pallas_call | solution.py:569
  53.7 1.2 %shard_map.174 = (f32[16,3,24,128]{3,2,1,0:T(8,128)S(1)}, f32[10,8,3,16,128]{4,3,2,1,0:T(8,128)S(1)}, f32[8,40,128]{2,1,0:T(8,128)S(1)}, f32[4,40,128]{2,1,0:T(8...) custom-call(s32[1]{0:T(128)S(6)} %copy.36.refs_0_, ...), custom_call_target="tpu_custom_call", output_to_operand_aliasing={{0}: (3, {}), {1}: (6, {})} | custom-call | tf_op jit(solution)/shard_map/pallas_call | solution.py:569
  55.3 2.2 %collective-permute-start.27 = (f32[8,40,128]{2,1,0:T(8,128)S(1)}, f32[8,40,128]{2,1,0:T(8,128)S(1)}, u32[]{:S(2)}, u32[]{:S(2)}) collective-permute-start(f32[8,40,128]{2,1,0:T(8,128)S(1)} %get-tuple-element.116), channel_id=1, source_target_pairs={{0,4},{1,5},{2,6},{3,7},{4,0},{5,1},{6,2},{7,3},{8,12},{9,13},{10,... | collective-permute-start | bytes 491528 | tf_op jit(solution)/shard_map/ppermute | solution.py:670
  58.0 0.9 %collective-permute-start.30 = (f32[2,24,128]{2,1,0:T(8,128)S(1)}, f32[2,24,128]{2,1,0:T(8,128)S(1)}, u32[]{:S(2)}, u32[]{:S(2)}) collective-permute-start(f32[2,24,128]{2,1,0:T(8,128)S(1)} %get-tuple-element.120), channel_id=1, source_target_pairs={{0,6},{1,7},{2,4},{3,5},{4,2},{5,3},{6,0},{7,1},{8,14},{9,15},{10,... | collective-permute-start | bytes 73736 | tf_op jit(solution)/shard_map/ppermute | solution.py:673
  59.5 2.7 %collective-permute-done.29.refs_5_ = f32[4,40,128]{2,1,0:T(8,128)S(1)} collective-permute-done((f32[4,40,128]{2,1,0:T(8,128)S(1)}, f32[4,40,128]{2,1,0:T(8,128)S(1)}, u32[]{:S(2)}, u32[]{:S(2)}) %collective-permute-start.29) | collective-permute-done | bytes 81952 | tf_op jit(solution)/shard_map/ppermute | solution.py:671
  62.2 1.3 %shard_map.175 = (f32[16,3,24,128]{3,2,1,0:T(8,128)S(1)}, f32[8,128]{1,0:T(8,128)}) custom-call(f32[10,8,3,16,128]{4,3,2,1,0:T(8,128)S(1)} %get-tuple-element.112.refs_0_.refs_6_, f32[16,3,24,128]{3,2,1,0:T(8,128)S(1)} %get-tuple-element.113.refs_1_, f32[16,3,24,128]{3,2,1,0:T(8,128)S(1)} %get-tuple-element.79.refs_4_.refs_2_, ...), custom_call_target="tpu_custom_call" | custom-call | tf_op jit(solution)/shard_map/pallas_call | solution.py:569
  63.6 1.1 %shard_map.176 = (f32[16,3,24,128]{3,2,1,0:T(8,128)S(1)}, f32[10,8,3,16,128]{4,3,2,1,0:T(8,128)S(1)}, f32[5,8,3,8,128]{4,3,2,1,0:T(8,128)S(1)}, f32[5,8,3,8,128]{4,3,2,1,0:T(8,128)S(1)}) custom-call(s32[1]{0:T(128)S(6)} %copy.36.refs_0_, s32[1,4]{1,0:T(1,128)S(1)} %bitcast.8, f32[1,10]{1,0:T(1,128)S(1)} %bitcast.13, ...), custom_call_target="tpu_custom_call", output_to_operand_aliasing={{0}: (3, {}), {1}: (6, {})} | custom-call | tf_op jit(solution)/shard_map/pallas_call | solution.py:569
  64.8 1.9 %collective-permute-done.32.theirs = f32[5,8,3,8,128]{4,3,2,1,0:T(8,128)S(1)} collective-permute-done((f32[5,8,3,8,128]{4,3,2,1,0:T(8,128)S(1)}, f32[5,8,3,8,128]{4,3,2,1,0:T(8,128)S(1)}, u32[]{:S(2)}, u32[]{:S(2)}) %collective-permute-start.32) | collective-permute-done | bytes 491552 | tf_op jit(solution)/shard_map/ppermute | solution.py:722
  (59 shorter events, 9.1 us)
Async XLA Ops:
  1.9 1.8 %collective-permute-start.1 = (f32[3,8,8,320]{3,2,1,0:T(8,128)S(1)}, f32[3,8,8,320]{3,2,1,0:T(8,128)S(1)}, u32[]{:S(2)}, u32[]{:S(2)}) collective-permute-start(f32[3,8,8,320]{3,2,1,0:T(8,128)S(1)} %get-tuple-element.67), channel_id=1, source_target_pairs={{0,1},{1,0},{2,3},{3,2},{4,5},{5,4},{6,7},{7,6},{8,9},{9,8},{10,11... | collective-permute-start | bytes 737288 | tf_op jit(solution)/shard_map/ppermute | solution.py:640
  3.9 13.3 %collective-permute-start.2 = (f32[17,40,128]{2,1,0:T(8,128)S(1)}, f32[17,40,128]{2,1,0:T(8,128)S(1)}, u32[]{:S(2)}, u32[]{:S(2)}) collective-permute-start(f32[17,40,128]{2,1,0:T(8,128)S(1)} %get-tuple-element.68), channel_id=1, source_target_pairs={{0,4},{1,5},{2,6},{3,7},{4,0},{5,1},{6,2},{7,3},{8,12},{9,13},{10,... | collective-permute-start | bytes 1044488 | tf_op jit(solution)/shard_map/ppermute | solution.py:670
  6.9 13.6 %collective-permute-start.7 = (f32[16,40,128]{2,1,0:T(8,128)S(1)}, f32[16,40,128]{2,1,0:T(8,128)S(1)}, u32[]{:S(2)}, u32[]{:S(2)}) collective-permute-start(f32[16,40,128]{2,1,0:T(8,128)S(1)} %get-tuple-element.76), channel_id=1, source_target_pairs={{0,1},{1,0},{2,3},{3,2},{4,8},{5,9},{6,10},{7,11},{8,4},{9,5},{10,... | collective-permute-start | bytes 983048 | tf_op jit(solution)/shard_map/ppermute | solution.py:670
  6.9 10.3 %collective-permute-start.3 = (f32[9,40,128]{2,1,0:T(8,128)S(1)}, f32[9,40,128]{2,1,0:T(8,128)S(1)}, u32[]{:S(2)}, u32[]{:S(2)}) collective-permute-start(f32[9,40,128]{2,1,0:T(8,128)S(1)} %get-tuple-element.69), channel_id=1, source_target_pairs={{0,2},{1,3},{2,0},{3,1},{4,6},{5,7},{6,4},{7,5},{8,10},{9,11},{10,... | collective-permute-start | bytes 552968 | tf_op jit(solution)/shard_map/ppermute | solution.py:671
  8.4 8.8 %collective-permute-start.4 = (f32[3,24,128]{2,1,0:T(8,128)S(1)}, f32[3,24,128]{2,1,0:T(8,128)S(1)}, u32[]{:S(2)}, u32[]{:S(2)}) collective-permute-start(f32[3,24,128]{2,1,0:T(8,128)S(1)} %get-tuple-element.70), channel_id=1, source_target_pairs={{0,6},{1,7},{2,4},{3,5},{4,2},{5,3},{6,0},{7,1},{8,14},{9,15},{10,... | collective-permute-start | bytes 110600 | tf_op jit(solution)/shard_map/ppermute | solution.py:673
  11.5 3.8 %collective-permute-start.5 = (f32[2,24,128]{2,1,0:T(8,128)S(1)}, f32[2,24,128]{2,1,0:T(8,128)S(1)}, u32[]{:S(2)}, u32[]{:S(2)}) collective-permute-start(f32[2,24,128]{2,1,0:T(8,128)S(1)} %get-tuple-element.71), channel_id=1, source_target_pairs={{0,2},{1,3},{2,0},{3,1},{4,10},{5,11},{6,8},{7,9},{8,6},{9,7},{10,... | collective-permute-start | bytes 73736 | tf_op jit(solution)/shard_map/ppermute | solution.py:673
  17.3 5.2 %collective-permute-start.6 = (f32[4,16,128]{2,1,0:T(8,128)S(1)}, f32[4,16,128]{2,1,0:T(8,128)S(1)}, u32[]{:S(2)}, u32[]{:S(2)}) collective-permute-start(f32[4,16,128]{2,1,0:T(8,128)S(1)} %shard_map.165), channel_id=1, source_target_pairs={{0,8},{1,9},{2,10},{3,11},{4,12},{5,13},{6,14},{7,15},{8,0},{9,1},... | collective-permute-start | bytes 98312 | tf_op jit(solution)/shard_map/ppermute | solution.py:600
  21.9 2.0 %collective-permute-start.8 = (f32[8,128]{1,0:T(8,128)S(1)}, f32[8,128]{1,0:T(8,128)S(1)}, u32[]{:S(2)}, u32[]{:S(2)}) collective-permute-start(f32[8,128]{1,0:T(8,128)S(1)} %get-tuple-element.85), channel_id=1, source_target_pairs={{0,1},{1,0},{2,3},{3,2},{4,5},{5,4},{6,7},{7,6},{8,9},{9,8},{10,11... | collective-permute-start | bytes 12296 | tf_op jit(solution)/shard_map/ppermute | solution.py:691
  23.9 7.9 %collective-permute-start.10 = (f32[8,40,128]{2,1,0:T(8,128)S(1)}, f32[8,40,128]{2,1,0:T(8,128)S(1)}, u32[]{:S(2)}, u32[]{:S(2)}) collective-permute-start(f32[8,40,128]{2,1,0:T(8,128)S(1)} %get-tuple-element.86), channel_id=1, source_target_pairs={{0,1},{1,0},{2,3},{3,2},{4,8},{5,9},{6,10},{7,11},{8,4},{9,5},{10,... | collective-permute-start | bytes 491528 | tf_op jit(solution)/shard_map/ppermute | solution.py:670
  24.0 7.9 %collective-permute-start.9 = (f32[8,40,128]{2,1,0:T(8,128)S(1)}, f32[8,40,128]{2,1,0:T(8,128)S(1)}, u32[]{:S(2)}, u32[]{:S(2)}) collective-permute-start(f32[8,40,128]{2,1,0:T(8,128)S(1)} %get-tuple-element.86), channel_id=1, source_target_pairs={{0,4},{1,5},{2,6},{3,7},{4,0},{5,1},{6,2},{7,3},{8,12},{9,13},{10,... | collective-permute-start | bytes 491528 | tf_op jit(solution)/shard_map/ppermute | solution.py:670
  27.4 4.4 %collective-permute-start.11 = (f32[4,40,128]{2,1,0:T(8,128)S(1)}, f32[4,40,128]{2,1,0:T(8,128)S(1)}, u32[]{:S(2)}, u32[]{:S(2)}) collective-permute-start(f32[4,40,128]{2,1,0:T(8,128)S(1)} %get-tuple-element.87), channel_id=1, source_target_pairs={{0,2},{1,3},{2,0},{3,1},{4,6},{5,7},{6,4},{7,5},{8,10},{9,11},{10,... | collective-permute-start | bytes 245768 | tf_op jit(solution)/shard_map/ppermute | solution.py:671
  28.0 5.3 %collective-permute-start.12 = (f32[2,24,128]{2,1,0:T(8,128)S(1)}, f32[2,24,128]{2,1,0:T(8,128)S(1)}, u32[]{:S(2)}, u32[]{:S(2)}) collective-permute-start(f32[2,24,128]{2,1,0:T(8,128)S(1)} %get-tuple-element.90), channel_id=1, source_target_pairs={{0,6},{1,7},{2,4},{3,5},{4,2},{5,3},{6,0},{7,1},{8,14},{9,15},{10,... | collective-permute-start | bytes 73736 | tf_op jit(solution)/shard_map/ppermute | solution.py:673
  28.9 4.4 %collective-permute-start.13 = (f32[2,24,128]{2,1,0:T(8,128)S(1)}, f32[2,24,128]{2,1,0:T(8,128)S(1)}, u32[]{:S(2)}, u32[]{:S(2)}) collective-permute-start(f32[2,24,128]{2,1,0:T(8,128)S(1)} %get-tuple-element.91), channel_id=1, source_target_pairs={{0,2},{1,3},{2,0},{3,1},{4,10},{5,11},{6,8},{7,9},{8,6},{9,7},{10,... | collective-permute-start | bytes 73736 | tf_op jit(solution)/shard_map/ppermute | solution.py:673
  33.2 1.2 %collective-permute-start.14 = (f32[8,128]{1,0:T(8,128)S(1)}, f32[8,128]{1,0:T(8,128)S(1)}, u32[]{:S(2)}, u32[]{:S(2)}) collective-permute-start(f32[8,128]{1,0:T(8,128)S(1)} %get-tuple-element.95), channel_id=1, source_target_pairs={{0,1},{1,0},{2,3},{3,2},{4,5},{5,4},{6,7},{7,6},{8,9},{9,8},{10,11... | collective-permute-start | bytes 12296 | tf_op jit(solution)/shard_map/ppermute | solution.py:691
  34.4 7.2 %collective-permute-start.16 = (f32[8,40,128]{2,1,0:T(8,128)S(1)}, f32[8,40,128]{2,1,0:T(8,128)S(1)}, u32[]{:S(2)}, u32[]{:S(2)}) collective-permute-start(f32[8,40,128]{2,1,0:T(8,128)S(1)} %get-tuple-element.96), channel_id=1, source_target_pairs={{0,1},{1,0},{2,3},{3,2},{4,8},{5,9},{6,10},{7,11},{8,4},{9,5},{10,... | collective-permute-start | bytes 491528 | tf_op jit(solution)/shard_map/ppermute | solution.py:670
  34.8 6.9 %collective-permute-start.15 = (f32[8,40,128]{2,1,0:T(8,128)S(1)}, f32[8,40,128]{2,1,0:T(8,128)S(1)}, u32[]{:S(2)}, u32[]{:S(2)}) collective-permute-start(f32[8,40,128]{2,1,0:T(8,128)S(1)} %get-tuple-element.96), channel_id=1, source_target_pairs={{0,4},{1,5},{2,6},{3,7},{4,0},{5,1},{6,2},{7,3},{8,12},{9,13},{10,... | collective-permute-start | bytes 491528 | tf_op jit(solution)/shard_map/ppermute | solution.py:670
  36.9 4.7 %collective-permute-start.17 = (f32[4,40,128]{2,1,0:T(8,128)S(1)}, f32[4,40,128]{2,1,0:T(8,128)S(1)}, u32[]{:S(2)}, u32[]{:S(2)}) collective-permute-start(f32[4,40,128]{2,1,0:T(8,128)S(1)} %get-tuple-element.97), channel_id=1, source_target_pairs={{0,2},{1,3},{2,0},{3,1},{4,6},{5,7},{6,4},{7,5},{8,10},{9,11},{10,... | collective-permute-start | bytes 245768 | tf_op jit(solution)/shard_map/ppermute | solution.py:671
  37.4 5.6 %collective-permute-start.18 = (f32[2,24,128]{2,1,0:T(8,128)S(1)}, f32[2,24,128]{2,1,0:T(8,128)S(1)}, u32[]{:S(2)}, u32[]{:S(2)}) collective-permute-start(f32[2,24,128]{2,1,0:T(8,128)S(1)} %get-tuple-element.100), channel_id=1, source_target_pairs={{0,6},{1,7},{2,4},{3,5},{4,2},{5,3},{6,0},{7,1},{8,14},{9,15},{10,... | collective-permute-start | bytes 73736 | tf_op jit(solution)/shard_map/ppermute | solution.py:673
  38.4 4.7 %collective-permute-start.19 = (f32[2,24,128]{2,1,0:T(8,128)S(1)}, f32[2,24,128]{2,1,0:T(8,128)S(1)}, u32[]{:S(2)}, u32[]{:S(2)}) collective-permute-start(f32[2,24,128]{2,1,0:T(8,128)S(1)} %get-tuple-element.101), channel_id=1, source_target_pairs={{0,2},{1,3},{2,0},{3,1},{4,10},{5,11},{6,8},{7,9},{8,6},{9,7},{10,... | collective-permute-start | bytes 73736 | tf_op jit(solution)/shard_map/ppermute | solution.py:673
  42.9 1.2 %collective-permute-start.20 = (f32[8,128]{1,0:T(8,128)S(1)}, f32[8,128]{1,0:T(8,128)S(1)}, u32[]{:S(2)}, u32[]{:S(2)}) collective-permute-start(f32[8,128]{1,0:T(8,128)S(1)} %get-tuple-element.105), channel_id=1, source_target_pairs={{0,1},{1,0},{2,3},{3,2},{4,5},{5,4},{6,7},{7,6},{8,9},{9,8},{10,11... | collective-permute-start | bytes 12296 | tf_op jit(solution)/shard_map/ppermute | solution.py:691
  44.2 8.1 %collective-permute-start.22 = (f32[8,40,128]{2,1,0:T(8,128)S(1)}, f32[8,40,128]{2,1,0:T(8,128)S(1)}, u32[]{:S(2)}, u32[]{:S(2)}) collective-permute-start(f32[8,40,128]{2,1,0:T(8,128)S(1)} %get-tuple-element.106), channel_id=1, source_target_pairs={{0,1},{1,0},{2,3},{3,2},{4,8},{5,9},{6,10},{7,11},{8,4},{9,5},{10,... | collective-permute-start | bytes 491528 | tf_op jit(solution)/shard_map/ppermute | solution.py:670
  44.5 7.8 %collective-permute-start.21 = (f32[8,40,128]{2,1,0:T(8,128)S(1)}, f32[8,40,128]{2,1,0:T(8,128)S(1)}, u32[]{:S(2)}, u32[]{:S(2)}) collective-permute-start(f32[8,40,128]{2,1,0:T(8,128)S(1)} %get-tuple-element.106), channel_id=1, source_target_pairs={{0,4},{1,5},{2,6},{3,7},{4,0},{5,1},{6,2},{7,3},{8,12},{9,13},{10,... | collective-permute-start | bytes 491528 | tf_op jit(solution)/shard_map/ppermute | solution.py:670
  47.8 4.4 %collective-permute-start.23 = (f32[4,40,128]{2,1,0:T(8,128)S(1)}, f32[4,40,128]{2,1,0:T(8,128)S(1)}, u32[]{:S(2)}, u32[]{:S(2)}) collective-permute-start(f32[4,40,128]{2,1,0:T(8,128)S(1)} %get-tuple-element.107), channel_id=1, source_target_pairs={{0,2},{1,3},{2,0},{3,1},{4,6},{5,7},{6,4},{7,5},{8,10},{9,11},{10,... | collective-permute-start | bytes 245768 | tf_op jit(solution)/shard_map/ppermute | solution.py:671
  48.4 5.3 %collective-permute-start.24 = (f32[2,24,128]{2,1,0:T(8,128)S(1)}, f32[2,24,128]{2,1,0:T(8,128)S(1)}, u32[]{:S(2)}, u32[]{:S(2)}) collective-permute-start(f32[2,24,128]{2,1,0:T(8,128)S(1)} %get-tuple-element.110), channel_id=1, source_target_pairs={{0,6},{1,7},{2,4},{3,5},{4,2},{5,3},{6,0},{7,1},{8,14},{9,15},{10,... | collective-permute-start | bytes 73736 | tf_op jit(solution)/shard_map/ppermute | solution.py:673
  49.3 4.4 %collective-permute-start.25 = (f32[2,24,128]{2,1,0:T(8,128)S(1)}, f32[2,24,128]{2,1,0:T(8,128)S(1)}, u32[]{:S(2)}, u32[]{:S(2)}) collective-permute-start(f32[2,24,128]{2,1,0:T(8,128)S(1)} %get-tuple-element.111), channel_id=1, source_target_pairs={{0,2},{1,3},{2,0},{3,1},{4,10},{5,11},{6,8},{7,9},{8,6},{9,7},{10,... | collective-permute-start | bytes 73736 | tf_op jit(solution)/shard_map/ppermute | solution.py:673
  53.6 1.3 %collective-permute-start.26 = (f32[8,128]{1,0:T(8,128)S(1)}, f32[8,128]{1,0:T(8,128)S(1)}, u32[]{:S(2)}, u32[]{:S(2)}) collective-permute-start(f32[8,128]{1,0:T(8,128)S(1)} %get-tuple-element.115), channel_id=1, source_target_pairs={{0,1},{1,0},{2,3},{3,2},{4,5},{5,4},{6,7},{7,6},{8,9},{9,8},{10,11... | collective-permute-start | bytes 12296 | tf_op jit(solution)/shard_map/ppermute | solution.py:691
  54.8 7.4 %collective-permute-start.28 = (f32[8,40,128]{2,1,0:T(8,128)S(1)}, f32[8,40,128]{2,1,0:T(8,128)S(1)}, u32[]{:S(2)}, u32[]{:S(2)}) collective-permute-start(f32[8,40,128]{2,1,0:T(8,128)S(1)} %get-tuple-element.116), channel_id=1, source_target_pairs={{0,1},{1,0},{2,3},{3,2},{4,8},{5,9},{6,10},{7,11},{8,4},{9,5},{10,... | collective-permute-start | bytes 491528 | tf_op jit(solution)/shard_map/ppermute | solution.py:670
  55.3 6.9 %collective-permute-start.27 = (f32[8,40,128]{2,1,0:T(8,128)S(1)}, f32[8,40,128]{2,1,0:T(8,128)S(1)}, u32[]{:S(2)}, u32[]{:S(2)}) collective-permute-start(f32[8,40,128]{2,1,0:T(8,128)S(1)} %get-tuple-element.116), channel_id=1, source_target_pairs={{0,4},{1,5},{2,6},{3,7},{4,0},{5,1},{6,2},{7,3},{8,12},{9,13},{10,... | collective-permute-start | bytes 491528 | tf_op jit(solution)/shard_map/ppermute | solution.py:670
  57.5 4.7 %collective-permute-start.29 = (f32[4,40,128]{2,1,0:T(8,128)S(1)}, f32[4,40,128]{2,1,0:T(8,128)S(1)}, u32[]{:S(2)}, u32[]{:S(2)}) collective-permute-start(f32[4,40,128]{2,1,0:T(8,128)S(1)} %get-tuple-element.117), channel_id=1, source_target_pairs={{0,2},{1,3},{2,0},{3,1},{4,6},{5,7},{6,4},{7,5},{8,10},{9,11},{10,... | collective-permute-start | bytes 245768 | tf_op jit(solution)/shard_map/ppermute | solution.py:671
  58.0 5.5 %collective-permute-start.30 = (f32[2,24,128]{2,1,0:T(8,128)S(1)}, f32[2,24,128]{2,1,0:T(8,128)S(1)}, u32[]{:S(2)}, u32[]{:S(2)}) collective-permute-start(f32[2,24,128]{2,1,0:T(8,128)S(1)} %get-tuple-element.120), channel_id=1, source_target_pairs={{0,6},{1,7},{2,4},{3,5},{4,2},{5,3},{6,0},{7,1},{8,14},{9,15},{10,... | collective-permute-start | bytes 73736 | tf_op jit(solution)/shard_map/ppermute | solution.py:673
  58.9 4.6 %collective-permute-start.31 = (f32[2,24,128]{2,1,0:T(8,128)S(1)}, f32[2,24,128]{2,1,0:T(8,128)S(1)}, u32[]{:S(2)}, u32[]{:S(2)}) collective-permute-start(f32[2,24,128]{2,1,0:T(8,128)S(1)} %get-tuple-element.121), channel_id=1, source_target_pairs={{0,2},{1,3},{2,0},{3,1},{4,10},{5,11},{6,8},{7,9},{8,6},{9,7},{10,... | collective-permute-start | bytes 73736 | tf_op jit(solution)/shard_map/ppermute | solution.py:673
  64.7 1.9 %collective-permute-start.32 = (f32[5,8,3,8,128]{4,3,2,1,0:T(8,128)S(1)}, f32[5,8,3,8,128]{4,3,2,1,0:T(8,128)S(1)}, u32[]{:S(2)}, u32[]{:S(2)}) collective-permute-start(f32[5,8,3,8,128]{4,3,2,1,0:T(8,128)S(1)} %get-tuple-element.123), channel_id=1, source_target_pairs={{0,1},{1,0},{2,3},{3,2},{4,5},{5,4},{6,7},{7,6},{8,9},{9,8},{10,11... | collective-permute-start | bytes 1474568 | tf_op jit(solution)/shard_map/ppermute | solution.py:722
  (5 other events, 52.0 us)
